TPU v7x, 32 devices: a whole 2x2x4 slice. The times are simulated.
32 devices in a mesh: ctx: 8 (over z, x), head: 4 (over y, core).
Axes of the slice: x: 2, y: 2, z: 4, core: 2. Of those that a mesh axis runs over, the one named last changes fastest.
Arguments:
- values: bfloat16 [8192, 5120], P(('ctx', 'head')), may hold values from -6 to 6
- state_in: bfloat16 [8192, 128], P('ctx'), may hold values from -0.5 to 0.5
- state_out: bfloat16 [8192, 128], P('ctx'), may hold values from -6 to 6
- log_decay: float32 [8192, 80], P('ctx', 'head'), may hold values from -1 to 0
- level_class: int32 [8192], P('ctx'), may hold values from 0 to 31
- level_table: float32 [32, 8, 80], P(None, None, 'head'), may hold values from 0.2 to 2
- skip_gain: float32 [80], P('head'), may hold values from 0.5 to 2
- norm_gain: float32 [5120], P('head'), may hold values from 0.1 to 1.9
- out_weight: bfloat16 [5120, 2560], P('head', 'ctx'), may hold values from -0.078125 to 0.078125
Outputs:
- projected: bfloat16 [8192, 2560], P(('ctx', 'head'))
All inputs are finite; a program needn't handle non-finite values.
Results may differ from a plain program's by a relative error of at most 0.0049.
Values may be sent and summed in bfloat16 or wider, within the bound.
No kernel may reach another device: no remote copies, remote signals or barrier semaphores. Data moves between devices by JAX's collectives and lax.ppermute only.
A program may use at most 128 MiB of HBM per device.

v0:
```python
import jax
import jax.numpy as jnp
from jax import lax
from jax.experimental import pallas as pl
from jax.experimental.pallas import tpu as pltpu
from jax.sharding import PartitionSpec as P

CH = 64
EPSILON = 1e-05
F32 = jnp.float32
BF16 = jnp.bfloat16
VMEM_LIMIT = 56 * 1024 * 1024


def dot(a, b):
    return lax.dot_general(a, b, (((1,), (0,)), ((), ())), preferred_element_type=F32)


def dot_t(a, b):
    return lax.dot_general(a, b, (((0,), (0,)), ((), ())), preferred_element_type=F32)


def dot_nt(a, b):
    return lax.dot_general(a, b, (((1,), (1,)), ((), ())), preferred_element_type=F32)


def swap(value, axis, distance):
    pairs = [(source, source ^ distance) for source in range(lax.axis_size(axis))]
    return lax.ppermute(value, axis, pairs)


def three_parts(x):
    high = x.astype(BF16)
    rest = x - high.astype(F32)
    middle = rest.astype(BF16)
    low = (rest - middle.astype(F32)).astype(BF16)
    return high, middle, low


def two_parts(x):
    high = x.astype(BF16)
    return high, (x - high.astype(F32)).astype(BF16)


def halves(x, head_count):
    high = x.astype(BF16).astype(F32)
    lane = lax.broadcasted_iota(jnp.int32, x.shape, x.ndim - 1)
    return jnp.where(lane < head_count, high, x - high).astype(BF16)


def merge_rows(stretches):
    rows = [("own", c, 0) for c in range(stretches - 1)]
    for c in range(stretches - 1):
        k = 0
        while (c >> k) & 1:
            rows.append(("merge", c, k))
            k += 1
    return rows


def factors_kernel(
    decay_ref, class_ref, table_ref, fade_ref, lift_ref, read_ref, cross_ref, merge_ref, total_ref
):
    tokens, width = decay_ref.shape
    head_count = width // 2
    stretches = tokens // CH
    levels, classes, _ = table_ref.shape
    local = read_ref.shape[0] - 1
    row = lax.broadcasted_iota(jnp.int32, (CH, CH), 0)
    col = lax.broadcasted_iota(jnp.int32, (CH, CH), 1)
    lower = jnp.where(row >= col, 1.0, 0.0).astype(BF16)
    lower = jnp.concatenate([lower] * 3, axis=1)
    tables = [jnp.concatenate(three_parts(table_ref[level]), axis=0) for level in range(levels)]
    within, starts = [], [jnp.zeros((1, width), F32)]
    for c in range(stretches):
        parts = jnp.concatenate(three_parts(decay_ref[c * CH : (c + 1) * CH, :]), axis=0)
        summed = dot(lower, parts)
        within.append(summed)
        starts.append(starts[-1] + summed[CH - 1 : CH, :])
    total = starts[-1]
    total_ref[...] = total
    class_iota = lax.broadcasted_iota(jnp.int32, (CH, 3 * classes), 1) % classes
    for c in range(stretches):
        rows = slice(c * CH, (c + 1) * CH)
        fade_ref[rows, :] = halves(jnp.exp(total - starts[c] - within[c]), head_count)
        lift_ref[rows, :] = halves(jnp.exp(-within[c]), head_count)
        onehot = jnp.where(class_ref[rows, :] == class_iota, 1.0, 0.0).astype(BF16)
        read_ref[0, rows, :] = halves(jnp.exp(within[c]) * dot(onehot, tables[0]), head_count)
        for level in range(1, local + 1):
            if (c >> (level - 1)) & 1:
                begin = starts[c] - starts[(c >> (level - 1)) << (level - 1)]
                factor = jnp.exp(within[c] + begin) * dot(onehot, tables[level])
                read_ref[level, rows, :] = halves(factor, head_count)
            else:
                read_ref[level, rows, :] = jnp.zeros((CH, width), BF16)
        far = jnp.exp(within[c] + starts[c])
        for level in range(local + 1, levels):
            cross_ref[level - local - 1, rows, :] = far * dot(onehot, tables[level])
    kinds = merge_rows(stretches)
    exps = []
    for kind, c, k in kinds:
        first = c if kind == "own" else c + 1 - 2**k
        exps.append(jnp.exp(starts[c + 1] - starts[first]))
    exps += [jnp.zeros((1, width), F32)] * (merge_ref.shape[0] - len(exps))
    merge_ref[...] = halves(jnp.concatenate(exps, axis=0), head_count)


def partial_state_kernel(
    me_ref, even_ref, odd_ref, even_fade_ref, odd_fade_ref, in_ref, spread_ref, keep_ref, send_ref
):
    features = spread_ref.shape[1]
    tile = feature_tile(features)
    for f in range(0, features, tile):
        cols = slice(f, f + tile)
        spread = spread_ref[:, cols]
        odd = (dot(odd_fade_ref[0], spread) * odd_ref[:, cols].astype(F32)).astype(BF16)
        send_ref[0, :, cols] = dot_t(in_ref[...], odd).astype(BF16)
        even = (dot(even_fade_ref[0], spread) * even_ref[:, cols].astype(F32)).astype(BF16)
        keep_ref[0, :, cols] = dot_t(in_ref[...], even)


def local_kernel(
    me_ref, value_ref, in_ref, out_ref, lift_ref, read_ref, merge_ref, spread_ref, skip_ref,
    pre_ref, sums, operand
):
    tokens = in_ref.shape[0]
    rows_dev = value_ref.shape[1]
    me = me_ref[0]
    stretches = tokens // CH
    spread = spread_ref[...]
    merges = dot(merge_ref[...], spread)
    place = {kind: i for i, kind in enumerate(merge_rows(stretches))}
    row = lax.broadcasted_iota(jnp.int32, (CH, CH), 0)
    col = lax.broadcasted_iota(jnp.int32, (CH, CH), 1)
    causal = row >= col
    skip = skip_ref[...]
    for c in range(stretches):
        rows = slice(c * CH, (c + 1) * CH)
        block, first = divmod(c * CH, rows_dev)
        value = value_ref[me ^ block, first : first + CH, :].astype(F32)
        lifted = dot(lift_ref[rows, :], spread) * value
        high, low = two_parts(lifted)
        own_in, own_out = in_ref[rows, :], out_ref[rows, :]
        scores = jnp.where(causal, dot_nt(own_out, own_in), 0.0)
        s_high, s_low = two_parts(scores)
        direct = dot(
            jnp.concatenate([s_high, s_low, s_high], axis=1),
            jnp.concatenate([high, high, low], axis=0),
        )
        total = dot(read_ref[0, rows, :], spread) * direct + skip * value
        twice = jnp.concatenate([own_out, own_out], axis=1)
        level = 1
        while 2 ** (level - 1) < stretches:
            if (c >> (level - 1)) & 1:
                gained = dot(twice, operand[level - 1])
                total = total + dot(read_ref[level, rows, :], spread) * gained
            level += 1
        pre_ref[rows, :] = total
        if c + 1 < stretches:
            node = dot_t(
                jnp.concatenate([own_in, own_in], axis=0), jnp.concatenate([high, low], axis=0)
            )
            at = place[("own", c, 0)]
            node = node * merges[at : at + 1, :]
            k = 0
            while (c >> k) & 1:
                at = place[("merge", c, k)]
                node = node + merges[at : at + 1, :] * sums[k]
                k += 1
            sums[k] = node
            n_high, n_low = two_parts(node)
            operand[k] = jnp.concatenate([n_high, n_low], axis=0)


def finish_kernel(
    me_ref, pre_ref, out_ref, cross_ref, state_ref, spread_ref, same_ref, gain_ref, keep_ref, send_ref
):
    parts = pre_ref.shape[0]
    me = me_ref[0]
    spread = spread_ref[...]
    same = same_ref[...]
    gain = gain_ref[...]
    for r in range(parts):
        at = me ^ r
        total = pre_ref[at]
        readers = out_ref[at]
        for level in range(cross_ref.shape[0]):
            total = total + dot(cross_ref[level, at], spread) * dot(readers, state_ref[level])
        mean_square = dot((total * total).astype(BF16), same) * (1.0 / CH)
        normed = (total * lax.rsqrt(mean_square + EPSILON) * gain).astype(BF16)
        if r % 2 == 0:
            keep_ref[r // 2] = normed
        else:
            send_ref[r // 2] = normed


def assemble_kernel(me_ref, own_ref, far_ref, out_ref):
    blocks = own_ref.shape[0]
    width = own_ref.shape[2]
    me = me_ref[0]
    for j in range(blocks):
        at = me ^ j
        total = own_ref[at]
        for i in range(far_ref.shape[0]):
            total = total + far_ref[i, at].astype(F32)
        out_ref[:, j * width : (j + 1) * width] = total.astype(BF16)


def feature_tile(features):
    for tile in (256, 128):
        if features % tile == 0:
            return tile
    return features


def whole(shape):
    return pl.BlockSpec(shape, lambda *_: (0,) * len(shape))


def on_device(
    values,
    state_in,
    state_out,
    log_decay,
    level_class,
    level_table,
    skip_gain,
    norm_gain,
    out_weight,
):
    heads_size = lax.axis_size("head")
    ctx_size = lax.axis_size("ctx")
    ctx_bits = ctx_size.bit_length() - 1
    me = lax.axis_index("head")
    me1 = me.reshape(1).astype(jnp.int32)
    position = lax.axis_index("ctx")
    tokens = state_in.shape[0]
    rows_dev = values.shape[0]
    head_count = log_decay.shape[1]
    features = values.shape[1] // heads_size
    head_width = features // head_count
    state_size = state_in.shape[1]
    stretches = tokens // CH
    local = stretches.bit_length() - 1
    levels = level_table.shape[1]
    wide = 2 * head_count
    tile = feature_tile(features)
    tiles = features // tile
    half = heads_size // 2
    params = pltpu.CompilerParams(vmem_limit_bytes=VMEM_LIMIT)

    spread = (
        jnp.arange(wide)[:, None] % head_count == (jnp.arange(features) // head_width)[None, :]
    ).astype(BF16)
    same = (
        jnp.arange(tile)[:, None] // head_width == jnp.arange(tile)[None, :] // head_width
    ).astype(BF16)

    merge_count = -(-len(merge_rows(stretches)) // 16) * 16
    double = jnp.concatenate([log_decay, log_decay], axis=1)
    table = jnp.transpose(level_table, (1, 0, 2))
    table = jnp.concatenate([table, table], axis=2)
    fade, lift, read, cross, merge, total = pl.pallas_call(
        factors_kernel,
        out_shape=(
            jax.ShapeDtypeStruct((tokens, wide), BF16),
            jax.ShapeDtypeStruct((tokens, wide), BF16),
            jax.ShapeDtypeStruct((local + 1, tokens, wide), BF16),
            jax.ShapeDtypeStruct((levels - local - 1, tokens, wide), F32),
            jax.ShapeDtypeStruct((merge_count, wide), BF16),
            jax.ShapeDtypeStruct((1, wide), F32),
        ),
        compiler_params=params,
        name="factors",
    )(double, level_class.reshape(tokens, 1), table)

    def own_rows(array, owner):
        return lax.dynamic_slice_in_dim(array, owner * rows_dev, rows_dev, 0)

    fades = [own_rows(fade, me)]
    for r in range(1, heads_size):
        fades.append(swap(own_rows(fade, me ^ r), "head", r))
    even_fade = jnp.stack(fades[0::2])
    odd_fade = jnp.stack(fades[1::2])

    def head_columns(owner):
        return lax.dynamic_slice_in_dim(values, owner * features, features, 1)

    gathered = [head_columns(me)]
    for r in range(1, heads_size):
        gathered.append(swap(head_columns(me ^ r), "head", r))

    blocks = [out_weight] + [None] * (ctx_size - 1)
    for r in range(1, ctx_size):
        low = r & -r
        blocks[r] = swap(blocks[r ^ low], "ctx", low)
    partner_blocks = [swap(block, "head", 1) for block in blocks]

    keep, send = pl.pallas_call(
        partial_state_kernel,
        grid_spec=pltpu.PrefetchScalarGridSpec(
            num_scalar_prefetch=1,
            grid=(half,),
            in_specs=[
                pl.BlockSpec((rows_dev, features), lambda i, m: (0, m[0] ^ (2 * i))),
                pl.BlockSpec((rows_dev, features), lambda i, m: (0, m[0] ^ (2 * i + 1))),
                pl.BlockSpec((1, rows_dev, wide), lambda i, m: (i, 0, 0)),
                pl.BlockSpec((1, rows_dev, wide), lambda i, m: (i, 0, 0)),
                pl.BlockSpec((rows_dev, state_size), lambda i, m: (m[0], 0)),
                whole((wide, features)),
            ],
            out_specs=[
                pl.BlockSpec((1, state_size, features), lambda i, m: (i, 0, 0)),
                pl.BlockSpec((1, state_size, features), lambda i, m: (i, 0, 0)),
            ],
        ),
        out_shape=(
            jax.ShapeDtypeStruct((half, state_size, features), F32),
            jax.ShapeDtypeStruct((half, state_size, features), BF16),
        ),
        compiler_params=params,
        name="partial_states",
    )(me1, values, values, even_fade, odd_fade, state_in, spread)
    summed = keep + swap(send, "head", 1).astype(F32)
    running = summed[0]
    for i in range(1, half):
        running = running + swap(summed[i].astype(BF16), "head", 2 * i).astype(F32)

    totals = total
    for bit in range(ctx_bits):
        totals = jnp.concatenate([totals, swap(totals, "ctx", 2**bit)], axis=0)

    offset = jnp.zeros((wide,), F32)
    scaled = []
    states = []
    for bit in range(ctx_bits):
        upper = position // 2**bit % 2 == 1
        own_total = jnp.sum(totals[: 2**bit], axis=0)
        partner_total = jnp.sum(totals[2**bit : 2 ** (bit + 1)], axis=0)
        factor = jnp.where(upper, jnp.exp(offset), 0.0)
        scaled.append(halves(cross[bit] * factor[None, :], head_count))
        offset = jnp.where(upper, offset + partner_total, offset)
        sent = running.astype(BF16)
        partner = swap(sent, "ctx", 2**bit)
        states.append(partner)
        if bit + 1 < ctx_bits:
            on_partner = jnp.repeat(
                jnp.where(upper, jnp.exp(own_total), 1.0)[:head_count], head_width
            )
            on_own = jnp.repeat(
                jnp.where(upper, 1.0, jnp.exp(partner_total))[:head_count], head_width
            )
            running = on_own[None, :] * running + on_partner[None, :] * partner.astype(F32)
    crossed = jnp.stack(scaled).reshape(ctx_bits, heads_size, rows_dev, wide)
    all_states = jnp.stack(states)

    skip_row = jnp.repeat(skip_gain, head_width)[None, :]
    pre = pl.pallas_call(
        local_kernel,
        grid_spec=pltpu.PrefetchScalarGridSpec(
            num_scalar_prefetch=1,
            grid=(tiles,),
            in_specs=[
                pl.BlockSpec((heads_size, rows_dev, tile), lambda f, m: (0, 0, f)),
                whole((tokens, state_size)),
                whole((tokens, state_size)),
                whole((tokens, wide)),
                whole((local + 1, tokens, wide)),
                whole((merge_count, wide)),
                pl.BlockSpec((wide, tile), lambda f, m: (0, f)),
                pl.BlockSpec((1, tile), lambda f, m: (0, f)),
            ],
            out_specs=pl.BlockSpec((tokens, tile), lambda f, m: (0, f)),
            scratch_shapes=[
                pltpu.VMEM((max(local, 1), state_size, tile), F32),
                pltpu.VMEM((max(local, 1), 2 * state_size, tile), BF16),
            ],
        ),
        out_shape=jax.ShapeDtypeStruct((tokens, features), F32),
        compiler_params=params,
        name="local_levels",
    )(me1, jnp.stack(gathered), state_in, state_out, lift, read, merge, spread, skip_row)

    kept, sent = pl.pallas_call(
        finish_kernel,
        grid_spec=pltpu.PrefetchScalarGridSpec(
            num_scalar_prefetch=1,
            grid=(tiles,),
            in_specs=[
                pl.BlockSpec((heads_size, rows_dev, tile), lambda f, m: (0, 0, f)),
                whole((heads_size, rows_dev, state_size)),
                whole((ctx_bits, heads_size, rows_dev, wide)),
                pl.BlockSpec((ctx_bits, state_size, tile), lambda f, m: (0, 0, f)),
                pl.BlockSpec((wide, tile), lambda f, m: (0, f)),
                whole((tile, tile)),
                pl.BlockSpec((1, tile), lambda f, m: (0, f)),
            ],
            out_specs=[
                pl.BlockSpec((half, rows_dev, tile), lambda f, m: (0, 0, f)),
                pl.BlockSpec((half, rows_dev, tile), lambda f, m: (0, 0, f)),
            ],
        ),
        out_shape=(
            jax.ShapeDtypeStruct((half, rows_dev, features), BF16),
            jax.ShapeDtypeStruct((half, rows_dev, features), BF16),
        ),
        compiler_params=params,
        name="finish",
    )(
        me1,
        pre.reshape(heads_size, rows_dev, features),
        state_out.reshape(heads_size, rows_dev, state_size),
        crossed,
        all_states,
        spread,
        same,
        norm_gain[None, :],
    )
    other = swap(sent, "head", 1)

    own_sums = []
    far_sums = [[] for _ in range(1, half)]
    for r in range(ctx_size):
        for i in range(1, half):
            product = dot(kept[i], blocks[r]) + dot(other[i], partner_blocks[r])
            far_sums[i - 1].append(swap(product.astype(BF16), "head", 2 * i))
        own_sums.append(dot(kept[0], blocks[r]) + dot(other[0], partner_blocks[r]))
    columns = out_weight.shape[1]
    return pl.pallas_call(
        assemble_kernel,
        in_specs=[
            pl.BlockSpec(memory_space=pltpu.SMEM),
            pl.BlockSpec(memory_space=pltpu.VMEM),
            pl.BlockSpec(memory_space=pltpu.VMEM),
        ],
        out_shape=jax.ShapeDtypeStruct((rows_dev, ctx_size * columns), BF16),
        compiler_params=params,
        name="assemble",
    )(
        position.reshape(1).astype(jnp.int32),
        jnp.stack(own_sums),
        jnp.stack([jnp.stack(far) for far in far_sums]),
    )


def solution(mesh):
    return jax.shard_map(
        on_device,
        mesh=mesh,
        in_specs=(
            P(("ctx", "head"), None),
            P("ctx", None),
            P("ctx", None),
            P("ctx", "head"),
            P("ctx"),
            P(None, None, "head"),
            P("head"),
            P("head"),
            P("head", "ctx"),
        ),
        out_specs=P(("ctx", "head"), None),
        check_vma=False,
    )
```

profile of v0, /device:TPU:0, one launch (start us, length us, event | category | flops | bytes accessed | tf_op | source)
XLA Modules:
  0.0 279.1 jit_solution(17145909670610669530)
XLA Ops:
  4.6 4.1 %factors.1 = (bf16[1024,40]{1,0:T(8,128)(2,1)}, bf16[1024,40]{1,0:T(8,128)(2,1)}, bf16[5,1024,40]{2,1,0:T(8,128)(2,1)}, f32[3,1024,40]{2,1,0:T(8,128)}, bf16[32,40]{1,0:T(8,128)(2,1)}, /*index=5*/f32[1,40]{1,0:T(1,128)}) custom-call(f32[1024,40]{1,0:T(8,128)} %copy.208.decay_ref, s32[1024,1]{1,0:T(8,128)} %copy.209.class_ref, ...), custom_call_target="tpu_custom_call" | custom-call | tf_op jit(solution)/shard_map/factors/pallas_call | solution.py:263
  8.7 2.9 %collective-permute-start.3 = (f32[1,40]{1,0:T(1,128)}, f32[1,40]{1,0:T(1,128)S(1)}, u32[]{:S(2)}, u32[]{:S(2)}) collective-permute-start(f32[1,40]{1,0:T(1,128)} %get-tuple-element.19), channel_id=1, source_target_pairs={{0,4},{4,0},{8,12},{12,8},{16,20},{20,16},{24,28},{28,24},{1,5},{5... | collective-permute-start | bytes 488 | tf_op jit(solution)/shard_map/ppermute | solution.py:29
  19.3 7.2 %partial_states.1 = (f32[2,128,1280]{2,1,0:T(8,128)}, bf16[2,128,1280]{2,1,0:T(8,128)(2,1)}) custom-call(s32[1]{0:T(128)} %bitcast.1.me_ref, bf16[256,5120]{1,0:T(8,128)(2,1)} %odd_ref.1, bf16[256,5120]{1,0:T(8,128)(2,1)} %odd_ref.1, bf16[2,256,40]{2,1,0:T(8,128)(2,1)} %pad_maximum_fusion.5.even_fade_ref, ...), custom_call_target="tpu_custom_call" | custom-call | tf_op jit(solution)/shard_map/partial_states/pallas_call | solution.py:299
  38.8 27.5 %collective-permute-done.9 = bf16[128,1280]{1,0:T(8,128)(2,1)S(1)} collective-permute-done((bf16[128,1280]{1,0:T(8,128)(2,1)S(1)}, bf16[128,1280]{1,0:T(8,128)(2,1)S(1)}, u32[]{:S(2)}, u32[]{:S(2)}) %collective-permute-start.9) | collective-permute-done | bytes 327712 | tf_op jit(solution)/shard_map/ppermute | solution.py:29
  68.3 7.9 %collective-permute-done.10 = bf16[128,1280]{1,0:T(8,128)(2,1)S(1)} collective-permute-done((bf16[128,1280]{1,0:T(8,128)(2,1)}, bf16[128,1280]{1,0:T(8,128)(2,1)S(1)}, u32[]{:S(2)}, u32[]{:S(2)}) %collective-permute-start.10) | collective-permute-done | bytes 327712 | tf_op jit(solution)/shard_map/ppermute | solution.py:29
  79.7 16.1 %collective-permute-done.11 = bf16[128,1280]{1,0:T(8,128)(2,1)S(1)} collective-permute-done((bf16[128,1280]{1,0:T(8,128)(2,1)S(1)}, bf16[128,1280]{1,0:T(8,128)(2,1)S(1)}, u32[]{:S(2)}, u32[]{:S(2)}) %collective-permute-start.11) | collective-permute-done | bytes 327712 | tf_op jit(solution)/shard_map/ppermute | solution.py:29
  99.1 3.2 %pad_maximum_fusion.value_ref = bf16[4,256,1280]{2,1,0:T(8,128)(2,1)} fusion(bf16[1,256,1280]{2,1,0:T(8,128)(2,1)} %bitcast.5, bf16[1,256,1280]{2,1,0:T(8,128)(2,1)} %bitcast.4, bf16[1,256,1280]{2,1,0:T(8,128)(2,1)S(1)} %bitcast.178, bf16[1,256,1280]{2,1,0:T(8,128)(2,1)S(1)} %get-tuple-element.25), kind=kLoop, calls=%fused_computation | loop fusion | flops 3932160 | bytes 5242880 | tf_op jit(solution)/shard_map/stack | solution.py:382
  102.3 24.4 %local_levels.1 = f32[1024,1280]{1,0:T(8,128)} custom-call(s32[1]{0:T(128)} %bitcast.1.me_ref, bf16[4,256,1280]{2,1,0:T(8,128)(2,1)} %pad_maximum_fusion.value_ref, bf16[1024,128]{1,0:T(8,128)(2,1)} %in_ref.3, bf16[1024,128]{1,0:T(8,128)(2,1)} %out_ref.1, bf16[1024,40]{1,0:T(8,128)(2,1)} %get-tuple-element.15.lift_ref, ...), custom_call_target="tpu_custom_call" | custom-call | tf_op jit(solution)/shard_map/local_levels/pallas_call | solution.py:358
  126.7 10.8 %collective-permute-done.21 = bf16[1280,320]{0,1:T(8,128)(2,1)} collective-permute-done((bf16[1280,320]{0,1:T(8,128)(2,1)}, bf16[1280,320]{0,1:T(8,128)(2,1)}, u32[]{:S(2)}, u32[]{:S(2)}) %collective-permute-start.21) | collective-permute-done | bytes 819232 | tf_op jit(solution)/shard_map/ppermute | solution.py:29
  138.2 2.8 collective-permute-done.12
  142.1 10.3 %finish.1 = (bf16[2,256,1280]{2,1,0:T(8,128)(2,1)}, bf16[2,256,1280]{2,1,0:T(8,128)(2,1)}) custom-call(s32[1]{0:T(128)} %bitcast.1.me_ref, f32[4,256,1280]{2,1,0:T(8,128)} %bitcast.170, bf16[4,256,128]{2,1,0:T(8,128)(2,1)} %bitcast.174, bf16[3,4,256,40]{3,2,1,0:T(8,128)(2,1)} %pad_maximum_fusion.2.cross_ref, ...), custom_call_target="tpu_custom_call" | custom-call | tf_op jit(solution)/shard_map/finish/pallas_call | solution.py:384
  152.4 2.6 fusion.15
  155.0 2.3 fusion.31
  158.9 2.3 fusion.11
  161.2 2.3 fusion.7
  169.4 2.3 fusion.21
  171.7 2.4 fusion.23
  174.1 10.7 %collective-permute-done.19 = bf16[1280,320]{0,1:T(8,128)(2,1)} collective-permute-done((bf16[1280,320]{0,1:T(8,128)(2,1)}, bf16[1280,320]{0,1:T(8,128)(2,1)}, u32[]{:S(2)}, u32[]{:S(2)}) %collective-permute-start.19) | collective-permute-done | bytes 819232 | tf_op jit(solution)/shard_map/ppermute | solution.py:29
  194.0 7.9 %collective-permute-done.27 = bf16[1280,320]{0,1:T(8,128)(2,1)S(1)} collective-permute-done((bf16[1280,320]{0,1:T(8,128)(2,1)S(1)}, bf16[1280,320]{0,1:T(8,128)(2,1)S(1)}, u32[]{:S(2)}, u32[]{:S(2)}) %collective-permute-start.27) | collective-permute-done | bytes 819232 | tf_op jit(solution)/shard_map/ppermute | solution.py:29
  239.7 2.4 convolution_add_fusion.14
  244.0 2.4 convolution_add_fusion.15
  250.0 2.3 convolution_add_fusion.8
  267.9 4.1 %collective-permute-done.35 = bf16[256,320]{1,0:T(8,128)(2,1)S(1)} collective-permute-done((bf16[256,320]{1,0:T(8,128)(2,1)S(1)}, bf16[256,320]{1,0:T(8,128)(2,1)S(1)}, u32[]{:S(2)}, u32[]{:S(2)}) %collective-permute-start.35) | collective-permute-done | bytes 163872 | tf_op jit(solution)/shard_map/ppermute | solution.py:29
  275.3 3.8 %assemble.1 = bf16[256,2560]{1,0:T(8,128)(2,1)} custom-call(s32[1]{0:T(128)} %bitcast.me_ref, f32[8,256,320]{2,1,0:T(8,128)} %bitcast_dynamic-update-slice_fusion.own_ref, bf16[1,8,256,320]{3,2,1,0:T(8,128)(2,1)} %bitcast.172), custom_call_target="tpu_custom_call" | custom-call | tf_op jit(solution)/shard_map/assemble/pallas_call | solution.py:429
  (210 shorter events, 113.5 us)
Async XLA Ops:
  8.7 22.0 %collective-permute-start.3 = (f32[1,40]{1,0:T(1,128)}, f32[1,40]{1,0:T(1,128)S(1)}, u32[]{:S(2)}, u32[]{:S(2)}) collective-permute-start(f32[1,40]{1,0:T(1,128)} %get-tuple-element.19), channel_id=1, source_target_pairs={{0,4},{4,0},{8,12},{12,8},{16,20},{20,16},{24,28},{28,24},{1,5},{5... | collective-permute-start | bytes 488 | tf_op jit(solution)/shard_map/ppermute | solution.py:29
  27.9 51.3 %collective-permute-start = (bf16[256,1280]{1,0:T(8,128)(2,1)}, bf16[256,1280]{1,0:T(8,128)(2,1)S(1)}, u32[]{:S(2)}, u32[]{:S(2)}) collective-permute-start(bf16[256,1280]{1,0:T(8,128)(2,1)} %get-tuple-element.27), channel_id=1, source_target_pairs={{0,1},{1,0},{2,3},{3,2},{4,5},{5,4},{6,7},{7,6},{8,9},{9,8},{10,11... | collective-permute-start | bytes 1966088 | tf_op jit(solution)/shard_map/ppermute | solution.py:29
  28.4 69.3 %collective-permute-start.1 = (bf16[256,1280]{1,0:T(8,128)(2,1)}, bf16[256,1280]{1,0:T(8,128)(2,1)}, u32[]{:S(2)}, u32[]{:S(2)}) collective-permute-start(bf16[256,1280]{1,0:T(8,128)(2,1)} %get-tuple-element.26), channel_id=1, source_target_pairs={{0,2},{1,3},{2,0},{3,1},{4,6},{5,7},{6,4},{7,5},{8,10},{9,11},{10,... | collective-permute-start | bytes 1966088 | tf_op jit(solution)/shard_map/ppermute | solution.py:29
  29.9 67.9 %collective-permute-start.2 = (bf16[256,1280]{1,0:T(8,128)(2,1)}, bf16[256,1280]{1,0:T(8,128)(2,1)}, u32[]{:S(2)}, u32[]{:S(2)}) collective-permute-start(bf16[256,1280]{1,0:T(8,128)(2,1)} %get-tuple-element.28), channel_id=1, source_target_pairs={{0,3},{1,2},{2,1},{3,0},{4,7},{5,6},{6,5},{7,4},{8,11},{9,10},{10,... | collective-permute-start | bytes 1966088 | tf_op jit(solution)/shard_map/ppermute | solution.py:29
  34.3 103.8 %collective-permute-start.15 = (bf16[1280,320]{0,1:T(8,128)(2,1)}, bf16[1280,320]{0,1:T(8,128)(2,1)}, u32[]{:S(2)}, u32[]{:S(2)}) collective-permute-start(bf16[1280,320]{0,1:T(8,128)(2,1)} %param.17), channel_id=1, source_target_pairs={{0,4},{4,0},{8,12},{12,8},{16,20},{20,16},{24,28},{28,24},{1,5},{5... | collective-permute-start | bytes 2457608 | tf_op jit(solution)/shard_map/ppermute | solution.py:29
  37.4 29.0 %collective-permute-start.9 = (bf16[128,1280]{1,0:T(8,128)(2,1)S(1)}, bf16[128,1280]{1,0:T(8,128)(2,1)S(1)}, u32[]{:S(2)}, u32[]{:S(2)}) collective-permute-start(bf16[128,1280]{1,0:T(8,128)(2,1)S(1)} %fusion.40), channel_id=1, source_target_pairs={{0,2},{1,3},{2,0},{3,1},{4,6},{5,7},{6,4},{7,5},{8,10},{9,11},{10,... | collective-permute-start | bytes 983048 | tf_op jit(solution)/shard_map/ppermute | solution.py:29
  76.3 19.5 %collective-permute-start.11 = (bf16[128,1280]{1,0:T(8,128)(2,1)S(1)}, bf16[128,1280]{1,0:T(8,128)(2,1)S(1)}, u32[]{:S(2)}, u32[]{:S(2)}) collective-permute-start(bf16[128,1280]{1,0:T(8,128)(2,1)S(1)} %fusion.41), channel_id=1, source_target_pairs={{0,8},{4,12},{8,0},{12,4},{16,24},{20,28},{24,16},{28,20},{1,9},{5... | collective-permute-start | bytes 983048 | tf_op jit(solution)/shard_map/ppermute | solution.py:29
  79.3 58.8 %collective-permute-start.17 = (bf16[1280,320]{0,1:T(8,128)(2,1)}, bf16[1280,320]{0,1:T(8,128)(2,1)}, u32[]{:S(2)}, u32[]{:S(2)}) collective-permute-start(bf16[1280,320]{0,1:T(8,128)(2,1)} %param.17), channel_id=1, source_target_pairs={{0,8},{4,12},{8,0},{12,4},{16,24},{20,28},{24,16},{28,20},{1,9},{5... | collective-permute-start | bytes 2457608 | tf_op jit(solution)/shard_map/ppermute | solution.py:29
  95.8 41.7 %collective-permute-start.21 = (bf16[1280,320]{0,1:T(8,128)(2,1)}, bf16[1280,320]{0,1:T(8,128)(2,1)}, u32[]{:S(2)}, u32[]{:S(2)}) collective-permute-start(bf16[1280,320]{0,1:T(8,128)(2,1)} %param.17), channel_id=1, source_target_pairs={{0,16},{4,20},{8,24},{12,28},{16,0},{20,4},{24,8},{28,12},{1,17},{... | collective-permute-start | bytes 2457608 | tf_op jit(solution)/shard_map/ppermute | solution.py:29
  97.7 108.6 %collective-permute-start.14 = (bf16[1280,320]{0,1:T(8,128)(2,1)}, bf16[1280,320]{0,1:T(8,128)(2,1)S(1)}, u32[]{:S(2)}, u32[]{:S(2)}) collective-permute-start(bf16[1280,320]{0,1:T(8,128)(2,1)} %param.17), channel_id=1, source_target_pairs={{0,1},{1,0},{2,3},{3,2},{4,5},{5,4},{6,7},{7,6},{8,9},{9,8},{10,11... | collective-permute-start | bytes 2457608 | tf_op jit(solution)/shard_map/ppermute | solution.py:29
  97.8 43.1 %collective-permute-start.12 = (bf16[128,1280]{1,0:T(8,128)(2,1)S(1)}, bf16[128,1280]{1,0:T(8,128)(2,1)S(1)}, u32[]{:S(2)}, u32[]{:S(2)}) collective-permute-start(bf16[128,1280]{1,0:T(8,128)(2,1)S(1)} %add_convert_fusion), channel_id=1, source_target_pairs={{0,16},{4,20},{8,24},{12,28},{16,0},{20,4},{24,8},{28,12},{1,17},{... | collective-permute-start | bytes 983048 | tf_op jit(solution)/shard_map/ppermute | solution.py:29
  137.5 28.0 %collective-permute-start.23 = (bf16[1280,320]{0,1:T(8,128)(2,1)}, bf16[1280,320]{0,1:T(8,128)(2,1)}, u32[]{:S(2)}, u32[]{:S(2)}) collective-permute-start(bf16[1280,320]{0,1:T(8,128)(2,1)} %collective-permute-done.21), channel_id=1, source_target_pairs={{0,4},{4,0},{8,12},{12,8},{16,20},{20,16},{24,28},{28,24},{1,5},{5... | collective-permute-start | bytes 2457608 | tf_op jit(solution)/shard_map/ppermute | solution.py:29
  138.1 25.4 %collective-permute-start.25 = (bf16[1280,320]{0,1:T(8,128)(2,1)}, bf16[1280,320]{0,1:T(8,128)(2,1)S(1)}, u32[]{:S(2)}, u32[]{:S(2)}) collective-permute-start(bf16[1280,320]{0,1:T(8,128)(2,1)} %collective-permute-done.21), channel_id=1, source_target_pairs={{0,8},{4,12},{8,0},{12,4},{16,24},{20,28},{24,16},{28,20},{1,9},{5... | collective-permute-start | bytes 2457608 | tf_op jit(solution)/shard_map/ppermute | solution.py:29
  138.1 66.2 %collective-permute-start.16 = (bf16[1280,320]{0,1:T(8,128)(2,1)}, bf16[1280,320]{0,1:T(8,128)(2,1)S(1)}, u32[]{:S(2)}, u32[]{:S(2)}) collective-permute-start(bf16[1280,320]{0,1:T(8,128)(2,1)} %collective-permute-done.15), channel_id=1, source_target_pairs={{0,1},{1,0},{2,3},{3,2},{4,5},{5,4},{6,7},{7,6},{8,9},{9,8},{10,11... | collective-permute-start | bytes 2457608 | tf_op jit(solution)/shard_map/ppermute | solution.py:29
  141.0 68.1 %collective-permute-start.18 = (bf16[1280,320]{0,1:T(8,128)(2,1)}, bf16[1280,320]{0,1:T(8,128)(2,1)S(1)}, u32[]{:S(2)}, u32[]{:S(2)}) collective-permute-start(bf16[1280,320]{0,1:T(8,128)(2,1)} %collective-permute-done.17), channel_id=1, source_target_pairs={{0,1},{1,0},{2,3},{3,2},{4,5},{5,4},{6,7},{7,6},{8,9},{9,8},{10,11... | collective-permute-start | bytes 2457608 | tf_op jit(solution)/shard_map/ppermute | solution.py:29
  163.5 21.4 %collective-permute-start.19 = (bf16[1280,320]{0,1:T(8,128)(2,1)}, bf16[1280,320]{0,1:T(8,128)(2,1)}, u32[]{:S(2)}, u32[]{:S(2)}) collective-permute-start(bf16[1280,320]{0,1:T(8,128)(2,1)} %collective-permute-done.17), channel_id=1, source_target_pairs={{0,4},{4,0},{8,12},{12,8},{16,20},{20,16},{24,28},{28,24},{1,5},{5... | collective-permute-start | bytes 2457608 | tf_op jit(solution)/shard_map/ppermute | solution.py:29
  165.6 36.3 %collective-permute-start.27 = (bf16[1280,320]{0,1:T(8,128)(2,1)S(1)}, bf16[1280,320]{0,1:T(8,128)(2,1)S(1)}, u32[]{:S(2)}, u32[]{:S(2)}) collective-permute-start(bf16[1280,320]{0,1:T(8,128)(2,1)S(1)} %collective-permute-done.25), channel_id=1, source_target_pairs={{0,4},{4,0},{8,12},{12,8},{16,20},{20,16},{24,28},{28,24},{1,5},{5... | collective-permute-start | bytes 2457608 | tf_op jit(solution)/shard_map/ppermute | solution.py:29
  184.8 20.0 %collective-permute-start.13 = (bf16[2,256,1280]{2,1,0:T(8,128)(2,1)S(1)}, bf16[2,256,1280]{2,1,0:T(8,128)(2,1)S(1)}, u32[]{:S(2)}, u32[]{:S(2)}) collective-permute-start(bf16[2,256,1280]{2,1,0:T(8,128)(2,1)S(1)} %copy-done.17), channel_id=1, source_target_pairs={{0,1},{1,0},{2,3},{3,2},{4,5},{5,4},{6,7},{7,6},{8,9},{9,8},{10,11... | collective-permute-start | bytes 3932168 | tf_op jit(solution)/shard_map/ppermute | solution.py:29
  209.1 16.2 %collective-permute-start.28 = (bf16[1280,320]{0,1:T(8,128)(2,1)}, bf16[1280,320]{0,1:T(8,128)(2,1)}, u32[]{:S(2)}, u32[]{:S(2)}) collective-permute-start(bf16[1280,320]{0,1:T(8,128)(2,1)} %copy-done.20), channel_id=1, source_target_pairs={{0,1},{1,0},{2,3},{3,2},{4,5},{5,4},{6,7},{7,6},{8,9},{9,8},{10,11... | collective-permute-start | bytes 2457608 | tf_op jit(solution)/shard_map/ppermute | solution.py:29
  211.6 49.9 %collective-permute-start.30 = (bf16[256,320]{1,0:T(8,128)(2,1)}, bf16[256,320]{1,0:T(8,128)(2,1)}, u32[]{:S(2)}, u32[]{:S(2)}) collective-permute-start(bf16[256,320]{1,0:T(8,128)(2,1)} %copy.221), channel_id=1, source_target_pairs={{0,2},{1,3},{2,0},{3,1},{4,6},{5,7},{6,4},{7,5},{8,10},{9,11},{10,... | collective-permute-start | bytes 491528 | tf_op jit(solution)/shard_map/ppermute | solution.py:29
  215.5 44.5 %collective-permute-start.29 = (bf16[256,320]{1,0:T(8,128)(2,1)}, bf16[256,320]{1,0:T(8,128)(2,1)}, u32[]{:S(2)}, u32[]{:S(2)}) collective-permute-start(bf16[256,320]{1,0:T(8,128)(2,1)} %copy.220), channel_id=1, source_target_pairs={{0,2},{1,3},{2,0},{3,1},{4,6},{5,7},{6,4},{7,5},{8,10},{9,11},{10,... | collective-permute-start | bytes 491528 | tf_op jit(solution)/shard_map/ppermute | solution.py:29
  218.5 45.5 %collective-permute-start.31 = (bf16[256,320]{1,0:T(8,128)(2,1)}, bf16[256,320]{1,0:T(8,128)(2,1)}, u32[]{:S(2)}, u32[]{:S(2)}) collective-permute-start(bf16[256,320]{1,0:T(8,128)(2,1)} %copy.222), channel_id=1, source_target_pairs={{0,2},{1,3},{2,0},{3,1},{4,6},{5,7},{6,4},{7,5},{8,10},{9,11},{10,... | collective-permute-start | bytes 491528 | tf_op jit(solution)/shard_map/ppermute | solution.py:29
  222.4 43.3 %collective-permute-start.32 = (bf16[256,320]{1,0:T(8,128)(2,1)}, bf16[256,320]{1,0:T(8,128)(2,1)}, u32[]{:S(2)}, u32[]{:S(2)}) collective-permute-start(bf16[256,320]{1,0:T(8,128)(2,1)} %copy.223), channel_id=1, source_target_pairs={{0,2},{1,3},{2,0},{3,1},{4,6},{5,7},{6,4},{7,5},{8,10},{9,11},{10,... | collective-permute-start | bytes 491528 | tf_op jit(solution)/shard_map/ppermute | solution.py:29
  225.3 41.3 %collective-permute-start.33 = (bf16[256,320]{1,0:T(8,128)(2,1)}, bf16[256,320]{1,0:T(8,128)(2,1)}, u32[]{:S(2)}, u32[]{:S(2)}) collective-permute-start(bf16[256,320]{1,0:T(8,128)(2,1)} %copy.224), channel_id=1, source_target_pairs={{0,2},{1,3},{2,0},{3,1},{4,6},{5,7},{6,4},{7,5},{8,10},{9,11},{10,... | collective-permute-start | bytes 491528 | tf_op jit(solution)/shard_map/ppermute | solution.py:29
  (38 other events, 219.3 us)
where the time goes:
time: 281 us; the launch traced here: 279 us
  waiting for transfers between devices  93.2 us (33%)
  matrix products  57.9 us (21%)
  Pallas kernels  49.9 us (18%)
  local copies, waits for them, and re-layouts  35.8 us (13%)
  starting transfers between devices  28.8 us (10%)
  other arithmetic  13 us (5%)
    ppermute x37, waiting for transfers between devices, swap(): return lax.ppermute(value, axis, pairs)  93.2 us
    dot_general x32, matrix products, dot(): lax.dot_general(a, b, (((1,), (0,)), ((), ())), preferred_element_type=F32)  57.9 us
    ppermute x37, starting transfers between devices, swap(): return lax.ppermute(value, axis, pairs)  28.8 us
    pallas_call x1, Pallas kernels, on_device(): pl.pallas_call(local_kernel, grid_spec=pltpu.PrefetchScalarGridSpec(num_s...  24.4 us
    unnamed x65, local copies, waits for them, and re-layouts  14.8 us
    pallas_call x1, Pallas kernels, on_device(): pl.pallas_call(finish_kernel, grid_spec=pltpu.PrefetchScalarGridSpec(num_...  10.3 us
    pallas_call x1, Pallas kernels, on_device(): pl.pallas_call(partial_state_kernel, grid_spec=pltpu.PrefetchScalarGridSp...  7.21 us
    add x8, local copies, waits for them, and re-layouts, on_device(): own_sums.append(dot(kept[0], blocks[r]) + dot(other[0], partner_blocks[r]))  6.69 us
  transfers between devices with their start and end apart: 37, of which 13 were waited for; matrix products, arithmetic and copies ran while one was open for 36% of the time, Pallas kernels for 15%

commit v1 on v0

v1 whole, which is shorter than its diff:
```python
import jax
import jax.numpy as jnp
from jax import lax
from jax.experimental import pallas as pl
from jax.experimental.pallas import tpu as pltpu
from jax.sharding import PartitionSpec as P

CH = 64
EPSILON = 1e-05
F32 = jnp.float32
BF16 = jnp.bfloat16
VMEM_LIMIT = 32 * 1024 * 1024


def dot(a, b):
    return lax.dot_general(a, b, (((1,), (0,)), ((), ())), preferred_element_type=F32)


def dot_t(a, b):
    return lax.dot_general(a, b, (((0,), (0,)), ((), ())), preferred_element_type=F32)


def dot_nt(a, b):
    return lax.dot_general(a, b, (((1,), (1,)), ((), ())), preferred_element_type=F32)


def swap(value, axis, distance):
    pairs = [(source, source ^ distance) for source in range(lax.axis_size(axis))]
    return lax.ppermute(value, axis, pairs)


def tie(value, *after):
    return lax.optimization_barrier((value,) + after)[0]


def three_parts(x):
    high = x.astype(BF16)
    rest = x - high.astype(F32)
    middle = rest.astype(BF16)
    low = (rest - middle.astype(F32)).astype(BF16)
    return high, middle, low


def two_parts(x):
    high = x.astype(BF16)
    return high, (x - high.astype(F32)).astype(BF16)


def halves(x, head_count):
    high = x.astype(BF16).astype(F32)
    lane = lax.broadcasted_iota(jnp.int32, x.shape, x.ndim - 1)
    return jnp.where(lane < head_count, high, x - high).astype(BF16)


def merge_rows(stretches):
    rows = [("own", c, 0) for c in range(stretches - 1)]
    for c in range(stretches - 1):
        k = 0
        while (c >> k) & 1:
            rows.append(("merge", c, k))
            k += 1
    return rows


def stretch_sums(decay_ref):
    tokens, width = decay_ref.shape
    row = lax.broadcasted_iota(jnp.int32, (CH, CH), 0)
    col = lax.broadcasted_iota(jnp.int32, (CH, CH), 1)
    lower = jnp.where(row >= col, 1.0, 0.0).astype(BF16)
    lower = jnp.concatenate([lower] * 3, axis=1)
    within, starts = [], [jnp.zeros((1, width), F32)]
    for c in range(tokens // CH):
        parts = jnp.concatenate(three_parts(decay_ref[c * CH : (c + 1) * CH, :]), axis=0)
        summed = dot(lower, parts)
        within.append(summed)
        starts.append(starts[-1] + summed[CH - 1 : CH, :])
    return within, starts


def fade_kernel(decay_ref, fade_ref, total_ref):
    head_count = decay_ref.shape[1] // 2
    within, starts = stretch_sums(decay_ref)
    total_ref[...] = starts[-1]
    for c, summed in enumerate(within):
        left = starts[-1] - starts[c] - summed
        fade_ref[c * CH : (c + 1) * CH, :] = halves(jnp.exp(left), head_count)


def factors_kernel(
    decay_ref, class_ref, table_ref, in_ref, out_ref,
    lift_ref, read_ref, cross_ref, merge_ref, score_ref, masked_ref,
):
    tokens, width = decay_ref.shape
    head_count = width // 2
    stretches = tokens // CH
    levels, classes, _ = table_ref.shape
    local = read_ref.shape[0] - 1
    tables = [jnp.concatenate(three_parts(table_ref[level]), axis=0) for level in range(levels)]
    within, starts = stretch_sums(decay_ref)
    class_iota = lax.broadcasted_iota(jnp.int32, (CH, 3 * classes), 1) % classes
    for c in range(stretches):
        rows = slice(c * CH, (c + 1) * CH)
        lift_ref[rows, :] = halves(jnp.exp(-within[c]), head_count)
        onehot = jnp.where(class_ref[rows, :] == class_iota, 1.0, 0.0).astype(BF16)
        read_ref[0, rows, :] = halves(jnp.exp(within[c]) * dot(onehot, tables[0]), head_count)
        for level in range(1, local + 1):
            if (c >> (level - 1)) & 1:
                begin = starts[c] - starts[(c >> (level - 1)) << (level - 1)]
                factor = jnp.exp(within[c] + begin) * dot(onehot, tables[level])
                read_ref[level, rows, :] = halves(factor, head_count)
            else:
                read_ref[level, rows, :] = jnp.zeros((CH, width), BF16)
        far = jnp.exp(within[c] + starts[c])
        for level in range(local + 1, levels):
            cross_ref[level - local - 1, rows, :] = far * dot(onehot, tables[level])
    exps = []
    for kind, c, k in merge_rows(stretches):
        first = c if kind == "own" else c + 1 - 2**k
        exps.append(jnp.exp(starts[c + 1] - starts[first]))
    exps += [jnp.zeros((1, width), F32)] * (merge_ref.shape[0] - len(exps))
    merge_ref[...] = halves(jnp.concatenate(exps, axis=0), head_count)
    groups, _, group_rows, _ = score_ref.shape
    row = lax.broadcasted_iota(jnp.int32, (group_rows, group_rows), 0)
    col = lax.broadcasted_iota(jnp.int32, (group_rows, group_rows), 1)
    inside = (row // CH == col // CH) & (row >= col)
    state_size = in_ref.shape[1]
    lane = lax.broadcasted_iota(jnp.int32, (state_size, group_rows), 1) // CH
    for g in range(groups):
        rows = slice(g * group_rows, (g + 1) * group_rows)
        scores = jnp.where(inside, dot_nt(out_ref[rows, :], in_ref[rows, :]), 0.0)
        score_ref[g, 0], score_ref[g, 1] = two_parts(scores)
        turned = jnp.transpose(in_ref[rows, :].astype(F32))
        for s in range(group_rows // CH):
            at = slice(s * state_size, (s + 1) * state_size)
            masked_ref[g, at, :] = jnp.where(lane == s, turned, 0.0).astype(BF16)


def partial_state_kernel(
    me_ref, even_ref, odd_ref, even_fade_ref, odd_fade_ref, in_ref, spread_ref, keep_ref, send_ref
):
    spread = spread_ref[...]
    turned = in_ref[...]
    odd = (dot(odd_fade_ref[0], spread) * odd_ref[...].astype(F32)).astype(BF16)
    send_ref[0] = dot(turned, odd).astype(BF16)
    even = (dot(even_fade_ref[0], spread) * even_ref[...].astype(F32)).astype(BF16)
    keep_ref[0] = dot(turned, even)


def local_kernel(
    me_ref, value_ref, out_ref, lift_ref, read_ref, merge_ref, score_ref, masked_ref, spread_ref,
    skip_ref, cross_ref, state_ref, pre_ref, sums, operand
):
    groups, group_rows, _ = value_ref.shape
    me = me_ref[0]
    per_group = group_rows // CH
    stretches = groups * per_group
    state_size = out_ref.shape[1]
    spread = spread_ref[...]
    merges = dot(merge_ref[...], spread)
    place = {kind: i for i, kind in enumerate(merge_rows(stretches))}
    skip = skip_ref[...]
    for g in range(groups):
        rows = slice(g * group_rows, (g + 1) * group_rows)
        value = value_ref[me ^ g].astype(F32)
        high, low = two_parts(dot(lift_ref[rows, :], spread) * value)
        direct = dot(score_ref[g, 0], high) + dot(score_ref[g, 0], low) + dot(score_ref[g, 1], high)
        total = dot(read_ref[0, rows, :], spread) * direct + skip * value
        for level in range(state_ref.shape[0]):
            gained = dot(out_ref[rows, :], state_ref[level])
            total = total + dot(cross_ref[level, rows, :], spread) * gained
        pre_ref[rows, :] = total
        nodes = dot(masked_ref[g], high) + dot(masked_ref[g], low)
        level = 1
        while 2 ** (level - 1) < stretches:
            span = 2 ** (level - 1)
            for first in range(g * per_group, (g + 1) * per_group, max(span, 1)):
                count = min(span, per_group)
                if (first >> (level - 1)) & 1 and span >= per_group:
                    at = slice(first * CH, (first + count) * CH)
                    readers = out_ref[at, :]
                    twice = jnp.concatenate([readers, readers], axis=1)
                    gained = dot(twice, operand[level - 1])
                    pre_ref[at, :] += dot(read_ref[level, at, :], spread) * gained
            level += 1
        for s in range(per_group):
            c = g * per_group + s
            at = slice(c * CH, (c + 1) * CH)
            level = 1
            while 2 ** (level - 1) < per_group:
                span = 2 ** (level - 1)
                if c % (2 * span) == span:
                    where = slice(c * CH, (c + span) * CH)
                    readers = out_ref[where, :]
                    twice = jnp.concatenate([readers, readers], axis=1)
                    gained = dot(twice, operand[level - 1])
                    pre_ref[where, :] += dot(read_ref[level, where, :], spread) * gained
                level += 1
            if c + 1 < stretches:
                row = place[("own", c, 0)]
                node = nodes[s * state_size : (s + 1) * state_size, :] * merges[row : row + 1, :]
                k = 0
                while (c >> k) & 1:
                    row = place[("merge", c, k)]
                    node = node + merges[row : row + 1, :] * sums[k]
                    k += 1
                sums[k] = node
                n_high, n_low = two_parts(node)
                operand[k, :state_size, :] = n_high
                operand[k, state_size:, :] = n_low


def finish_kernel(
    me_ref, pre_ref, out_ref, cross_ref, state_ref, spread_ref, same_ref, gain_ref, keep_ref, send_ref
):
    parts = pre_ref.shape[0]
    me = me_ref[0]
    spread = spread_ref[...]
    same = same_ref[...]
    gain = gain_ref[...]
    state = state_ref[...]
    for r in range(parts):
        at = me ^ r
        total = pre_ref[at] + dot(cross_ref[at], spread) * dot(out_ref[at], state)
        mean_square = dot((total * total).astype(BF16), same)
        normed = (total * lax.rsqrt(mean_square + EPSILON) * gain).astype(BF16)
        if r % 2 == 0:
            keep_ref[r // 2] = normed
        else:
            send_ref[r // 2] = normed


def project_kernel(place_ref, kept_ref, other_ref, *refs):
    far_ref, own_ref = refs[-2:]
    count = (len(refs) - 2) // 2
    weights, partners = refs[:count], refs[count:-2]
    half = kept_ref.shape[0]
    width = weights[0].shape[0]
    for i in list(range(1, half)) + [0]:
        kept, other = kept_ref[i], other_ref[i]
        found = [
            dot_nt(kept, weight[...]) + dot_nt(other, partner[...])
            for weight, partner in zip(weights, partners)
        ]
        for bit in range(count.bit_length() - 1):
            turn = place_ref[0] // 2**bit % 2 == 1
            found = [jnp.where(turn, found[j ^ 2**bit], found[j]) for j in range(count)]
        for j, result in enumerate(found):
            if i > 0:
                far_ref[i - 1, :, j * width : (j + 1) * width] = result.astype(BF16)
            else:
                own_ref[:, j * width : (j + 1) * width] = result


def assemble_kernel(place_ref, *refs):
    out_ref = refs[-1]
    width = refs[0].shape[1]
    groups = out_ref.shape[1] // width
    each = (len(refs) - 1) // groups
    for p in range(groups):
        own_ref, *far_refs = refs[p * each : (p + 1) * each]
        total = own_ref[...]
        for far_ref in far_refs:
            total = total + far_ref[...].astype(F32)
        start = pl.multiple_of((place_ref[0] ^ p) * width, width)
        out_ref[:, pl.ds(start, width)] = total.astype(BF16)


def feature_tile(features):
    for tile in (256, 128):
        if features % tile == 0:
            return tile
    return features


def whole(shape):
    return pl.BlockSpec(shape, lambda *_: (0,) * len(shape))


def on_device(
    values,
    state_in,
    state_out,
    log_decay,
    level_class,
    level_table,
    skip_gain,
    norm_gain,
    out_weight,
):
    heads_size = lax.axis_size("head")
    ctx_size = lax.axis_size("ctx")
    ctx_bits = ctx_size.bit_length() - 1
    me = lax.axis_index("head")
    me1 = me.reshape(1).astype(jnp.int32)
    position = lax.axis_index("ctx")
    tokens = state_in.shape[0]
    rows_dev = values.shape[0]
    head_count = log_decay.shape[1]
    features = values.shape[1] // heads_size
    head_width = features // head_count
    state_size = state_in.shape[1]
    stretches = tokens // CH
    local = stretches.bit_length() - 1
    levels = level_table.shape[1]
    wide = 2 * head_count
    tile = feature_tile(features)
    tiles = features // tile
    half = heads_size // 2
    params = pltpu.CompilerParams(vmem_limit_bytes=VMEM_LIMIT)
    cheap = pl.CostEstimate(flops=0, bytes_accessed=0, transcendentals=0)

    spread = (
        jnp.arange(wide)[:, None] % head_count == (jnp.arange(features) // head_width)[None, :]
    ).astype(BF16)
    same = (
        (jnp.arange(tile)[:, None] // head_width == jnp.arange(tile)[None, :] // head_width)
        / head_width
    ).astype(BF16)

    blocks = [out_weight.T] + [None] * (ctx_size - 1)
    for bit in range(ctx_bits):
        blocks[2**bit] = swap(blocks[0], "ctx", 2**bit)

    def head_columns(owner):
        return lax.dynamic_slice_in_dim(values, owner * features, features, 1)

    def value_swap(r, after=None):
        sent = head_columns(me ^ r)
        return swap(sent if after is None else tie(sent, after), "head", r)

    gathered = [head_columns(me)] + [None] * (heads_size - 1)
    early = [r for r in range(1, heads_size) if r <= half]
    for r in early:
        gathered[r] = value_swap(r)

    merge_count = -(-len(merge_rows(stretches)) // 16) * 16
    double = jnp.concatenate([log_decay, log_decay], axis=1)
    fade, total = pl.pallas_call(
        fade_kernel,
        out_shape=(
            jax.ShapeDtypeStruct((tokens, wide), BF16),
            jax.ShapeDtypeStruct((1, wide), F32),
        ),
        compiler_params=params,
        cost_estimate=cheap,
        name="fade",
    )(double)

    def own_rows(array, owner):
        return lax.dynamic_slice_in_dim(array, owner * rows_dev, rows_dev, 0)

    fades = [own_rows(fade, me)]
    for r in range(1, heads_size):
        fades.append(swap(own_rows(fade, me ^ r), "head", r))
    even_fade = jnp.stack(fades[0::2])
    odd_fade = jnp.stack(fades[1::2])
    in_turned = own_rows(state_in, me).T

    keep, send = pl.pallas_call(
        partial_state_kernel,
        grid_spec=pltpu.PrefetchScalarGridSpec(
            num_scalar_prefetch=1,
            grid=(half,),
            in_specs=[
                pl.BlockSpec((rows_dev, features), lambda i, m: (0, m[0] ^ (2 * i))),
                pl.BlockSpec((rows_dev, features), lambda i, m: (0, m[0] ^ (2 * i + 1))),
                pl.BlockSpec((1, rows_dev, wide), lambda i, m: (i, 0, 0)),
                pl.BlockSpec((1, rows_dev, wide), lambda i, m: (i, 0, 0)),
                whole((state_size, rows_dev)),
                whole((wide, features)),
            ],
            out_specs=[
                pl.BlockSpec((1, state_size, features), lambda i, m: (i, 0, 0)),
                pl.BlockSpec((1, state_size, features), lambda i, m: (i, 0, 0)),
            ],
        ),
        out_shape=(
            jax.ShapeDtypeStruct((half, state_size, features), F32),
            jax.ShapeDtypeStruct((half, state_size, features), BF16),
        ),
        compiler_params=params,
        cost_estimate=cheap,
        name="partial_states",
    )(me1, values, values, even_fade, odd_fade, in_turned, spread)
    summed = keep + swap(send, "head", 1).astype(F32)
    running = summed[0]
    for i in range(1, half):
        running = running + swap(summed[i].astype(BF16), "head", 2 * i).astype(F32)

    table = jnp.transpose(level_table, (1, 0, 2))
    table = jnp.concatenate([table, table], axis=2)
    lift, read, cross, merge, scores, masked = pl.pallas_call(
        factors_kernel,
        out_shape=(
            jax.ShapeDtypeStruct((tokens, wide), BF16),
            jax.ShapeDtypeStruct((local + 1, tokens, wide), BF16),
            jax.ShapeDtypeStruct((levels - local - 1, tokens, wide), F32),
            jax.ShapeDtypeStruct((merge_count, wide), BF16),
            jax.ShapeDtypeStruct((heads_size, 2, rows_dev, rows_dev), BF16),
            jax.ShapeDtypeStruct((heads_size, rows_dev // CH * state_size, rows_dev), BF16),
        ),
        compiler_params=params,
        cost_estimate=cheap,
        name="factors",
    )(double, level_class.reshape(tokens, 1), table, state_in, state_out)

    totals = total
    for bit in range(ctx_bits):
        totals = jnp.concatenate([totals, swap(totals, "ctx", 2**bit)], axis=0)

    for r in range(1, heads_size):
        if r not in early:
            gathered[r] = value_swap(r, running)

    offset = jnp.zeros((wide,), F32)
    scaled = []
    states = []
    for bit in range(ctx_bits):
        upper = position // 2**bit % 2 == 1
        own_total = jnp.sum(totals[: 2**bit], axis=0)
        partner_total = jnp.sum(totals[2**bit : 2 ** (bit + 1)], axis=0)
        factor = jnp.where(upper, jnp.exp(offset), 0.0)
        scaled.append(halves(cross[bit] * factor[None, :], head_count))
        offset = jnp.where(upper, offset + partner_total, offset)
        sent = running.astype(BF16)
        if bit + 1 < ctx_bits:
            sent = tie(sent, blocks[2**bit])
        partner = swap(sent, "ctx", 2**bit)
        states.append(partner)
        if bit + 1 < ctx_bits:
            on_partner = jnp.repeat(
                jnp.where(upper, jnp.exp(own_total), 1.0)[:head_count], head_width
            )
            on_own = jnp.repeat(
                jnp.where(upper, 1.0, jnp.exp(partner_total))[:head_count], head_width
            )
            running = on_own[None, :] * running + on_partner[None, :] * partner.astype(F32)

    for r in range(1, ctx_size):
        if blocks[r] is None:
            low = r & -r
            held = blocks[r ^ low]
            step = low.bit_length() - 1
            held = tie(held, states[step]) if step + 1 < ctx_bits else held
            blocks[r] = swap(held, "ctx", low)
    partner_blocks = [swap(block, "head", 1) for block in blocks]

    skip_row = jnp.repeat(skip_gain, head_width)[None, :]
    near = ctx_bits - 1
    pre = pl.pallas_call(
        local_kernel,
        grid_spec=pltpu.PrefetchScalarGridSpec(
            num_scalar_prefetch=1,
            grid=(tiles,),
            in_specs=[
                pl.BlockSpec((heads_size, rows_dev, tile), lambda f, m: (0, 0, f)),
                whole((tokens, state_size)),
                whole((tokens, wide)),
                whole((local + 1, tokens, wide)),
                whole((merge_count, wide)),
                whole(scores.shape),
                whole(masked.shape),
                pl.BlockSpec((wide, tile), lambda f, m: (0, f)),
                pl.BlockSpec((1, tile), lambda f, m: (0, f)),
                whole((near, tokens, wide)),
                pl.BlockSpec((near, state_size, tile), lambda f, m: (0, 0, f)),
            ],
            out_specs=pl.BlockSpec((tokens, tile), lambda f, m: (0, f)),
            scratch_shapes=[
                pltpu.VMEM((max(local, 1), state_size, tile), F32),
                pltpu.VMEM((max(local, 1), 2 * state_size, tile), BF16),
            ],
        ),
        out_shape=jax.ShapeDtypeStruct((tokens, features), F32),
        compiler_params=params,
        cost_estimate=cheap,
        name="local_levels",
    )(
        me1, jnp.stack(gathered), state_out, lift, read, merge, scores, masked, spread, skip_row,
        jnp.stack(scaled[:near]), jnp.stack(states[:near]),
    )

    kept, sent = pl.pallas_call(
        finish_kernel,
        grid_spec=pltpu.PrefetchScalarGridSpec(
            num_scalar_prefetch=1,
            grid=(tiles,),
            in_specs=[
                pl.BlockSpec((heads_size, rows_dev, tile), lambda f, m: (0, 0, f)),
                whole((heads_size, rows_dev, state_size)),
                whole((heads_size, rows_dev, wide)),
                pl.BlockSpec((state_size, tile), lambda f, m: (0, f)),
                pl.BlockSpec((wide, tile), lambda f, m: (0, f)),
                whole((tile, tile)),
                pl.BlockSpec((1, tile), lambda f, m: (0, f)),
            ],
            out_specs=[
                pl.BlockSpec((half, rows_dev, tile), lambda f, m: (0, 0, f)),
                pl.BlockSpec((half, rows_dev, tile), lambda f, m: (0, 0, f)),
            ],
        ),
        out_shape=(
            jax.ShapeDtypeStruct((half, rows_dev, features), BF16),
            jax.ShapeDtypeStruct((half, rows_dev, features), BF16),
        ),
        compiler_params=params,
        cost_estimate=cheap,
        name="finish",
    )(
        me1,
        pre.reshape(heads_size, rows_dev, features),
        state_out.reshape(heads_size, rows_dev, state_size),
        scaled[-1].reshape(heads_size, rows_dev, wide),
        states[-1],
        spread,
        same,
        norm_gain[None, :],
    )
    other = swap(sent, "head", 1)

    columns = out_weight.shape[1]
    count = 1
    while count * columns % 128 and 2 * count <= ctx_size:
        count *= 2
    place1 = position.reshape(1).astype(jnp.int32)
    smem = pl.BlockSpec(memory_space=pltpu.SMEM)
    vmem = pl.BlockSpec(memory_space=pltpu.VMEM)
    pieces = []
    for r in range(0, ctx_size, count):
        far, own = pl.pallas_call(
            project_kernel,
            in_specs=[smem] + [vmem] * (2 + 2 * count),
            out_shape=(
                jax.ShapeDtypeStruct((half - 1, rows_dev, count * columns), BF16),
                jax.ShapeDtypeStruct((rows_dev, count * columns), F32),
            ),
            compiler_params=params,
            cost_estimate=cheap,
            name="project",
        )(place1, kept, other, *blocks[r : r + count], *partner_blocks[r : r + count])
        pieces.append(own)
        pieces += [swap(far[i - 1], "head", 2 * i) for i in range(1, half)]
    return pl.pallas_call(
        assemble_kernel,
        in_specs=[smem] + [vmem] * len(pieces),
        out_shape=jax.ShapeDtypeStruct((rows_dev, ctx_size * columns), BF16),
        compiler_params=params,
        cost_estimate=cheap,
        name="assemble",
    )(place1 // count, *pieces)


def solution(mesh):
    return jax.shard_map(
        on_device,
        mesh=mesh,
        in_specs=(
            P(("ctx", "head"), None),
            P("ctx", None),
            P("ctx", None),
            P("ctx", "head"),
            P("ctx"),
            P(None, None, "head"),
            P("head"),
            P("head"),
            P("head", "ctx"),
        ),
        out_specs=P(("ctx", "head"), None),
        check_vma=False,
    )
```

time: 281 us -> 213 us (0.76)
  matrix products: 57.9 us -> 0 us
  local copies, waits for them, and re-layouts: 35.8 us -> 12.7 us
  waiting for transfers between devices: 93.2 us -> 114 us
  other arithmetic: 13 us -> 7.48 us
  Pallas kernels: 49.9 us -> 46.7 us
    dot_general x32 -> x0, matrix products: 57.9 us -> none  [dot(): lax.dot_general(a, b, (((1,), (0,)), ((), ())), preferred_element_type=F32)]
    ppermute x37 -> x33, waiting for transfers between devices: 93.2 us -> 114 us  [swap(): return lax.ppermute(value, axis, pairs)]
    pallas_call x1 -> x6, Pallas kernels: 3.82 us -> 17.4 us  [the longest x4 15.5 us: on_device(): pl.pallas_call(project_kernel, in_specs=[smem] + [vmem] * (2 + 2 * count)...]
    add x16 -> x0, local copies, waits for them, and re-layouts: 13.2 us -> none  [the longest x8 6.69 us: on_device(): own_sums.append(dot(kept[0], blocks[r]) + dot(other[0], partner_blocks[r]))]
    unnamed x65 -> x50, local copies, waits for them, and re-layouts: 14.8 us -> 7.58 us
    pallas_call x1, Pallas kernels: 24.4 us -> 19.4 us  [on_device(): pl.pallas_call(local_kernel, grid_spec=pltpu.PrefetchScalarGridSpec(num_s...]
    pallas_call x1, Pallas kernels: 7.21 us -> 2.45 us  [on_device(): pl.pallas_call(partial_state_kernel, grid_spec=pltpu.PrefetchScalarGridSp...]
    pallas_call x1, Pallas kernels: 10.3 us -> 5.71 us  [on_device(): pl.pallas_call(finish_kernel, grid_spec=pltpu.PrefetchScalarGridSpec(num_...]
  transfers between devices with their start and end apart: 37 -> 33, of which waited for: 13 -> 12; matrix products, arithmetic and copies ran while one was open for 36% -> 6% of each run, Pallas kernels for 15% -> 21%
where the time goes in v1:
time: 213 us; the launch traced here: 212 us
  waiting for transfers between devices  114 us (54%)
  Pallas kernels  46.7 us (22%)
  starting transfers between devices  30.6 us (14%)
  local copies, waits for them, and re-layouts  12.7 us (6%)
  other arithmetic  7.48 us (4%)
    ppermute x33, waiting for transfers between devices, swap(): return lax.ppermute(value, axis, pairs)  114 us
    ppermute x33, starting transfers between devices, swap(): return lax.ppermute(value, axis, pairs)  30.6 us
    pallas_call x1, Pallas kernels, on_device(): pl.pallas_call(local_kernel, grid_spec=pltpu.PrefetchScalarGridSpec(num_s...  19.4 us
    pallas_call x4, Pallas kernels, on_device(): pl.pallas_call(project_kernel, in_specs=[smem] + [vmem] * (2 + 2 * count)...  15.5 us
    unnamed x50, local copies, waits for them, and re-layouts  7.58 us
    pallas_call x1, Pallas kernels, on_device(): pl.pallas_call(finish_kernel, grid_spec=pltpu.PrefetchScalarGridSpec(num_...  5.71 us
  transfers between devices with their start and end apart: 33, of which 12 were waited for; matrix products, arithmetic and copies ran while one was open for 6% of the time, Pallas kernels for 21%

profile of v1, /device:TPU:0, one launch (start us, length us, event | category | flops | bytes accessed | tf_op | source)
XLA Modules:
  0.0 212.3 jit_solution(2692034676323450032)
XLA Ops:
  0.0 2.9 %collective-permute-start.9 = (bf16[320,1280]{1,0:T(8,128)(2,1)}, bf16[320,1280]{1,0:T(8,128)(2,1)}, u32[]{:S(2)}, u32[]{:S(2)}) collective-permute-start(bf16[320,1280]{1,0:T(8,128)(2,1)} %bitcast.49), channel_id=1, source_target_pairs={{0,4},{4,0},{8,12},{12,8},{16,20},{20,16},{24,28},{28,24},{1,5},{5... | collective-permute-start | bytes 2457608 | tf_op jit(solution)/shard_map/ppermute | solution.py:29
  14.7 2.4 %partial_states.1 = (f32[2,128,1280]{2,1,0:T(8,128)S(1)}, bf16[2,128,1280]{2,1,0:T(8,128)(2,1)}) custom-call(s32[1]{0:T(128)} %bitcast.1.me_ref, bf16[256,5120]{1,0:T(8,128)(2,1)S(1)} %copy-done, bf16[256,5120]{1,0:T(8,128)(2,1)S(1)} %copy-done, bf16[2,256,40]{2,1,0:T(8,128)(2,1)S(1)} %pad_maximum_fusion.4.even_fade_ref, ...), custom_call_target="tpu_custom_call" | custom-call | tf_op jit(solution)/shard_map/partial_states/pallas_call | solution.py:359
  19.9 1.6 collective-permute-done.8
  21.5 1.9 collective-permute-start.13
  26.3 1.6 factors.1
  30.7 2.6 %collective-permute-start.23 = (bf16[320,1280]{1,0:T(8,128)(2,1)}, bf16[320,1280]{1,0:T(8,128)(2,1)}, u32[]{:S(2)}, u32[]{:S(2)}) collective-permute-start(bf16[320,1280]{1,0:T(8,128)(2,1)} %bitcast.52), channel_id=1, source_target_pairs={{0,16},{4,20},{8,24},{12,28},{16,0},{20,4},{24,8},{28,12},{1,17},{... | collective-permute-start | bytes 2457608 | tf_op jit(solution)/shard_map/ppermute | solution.py:29
  36.6 6.5 %collective-permute-done.6 = bf16[128,1280]{1,0:T(8,128)(2,1)S(1)} collective-permute-done((bf16[128,1280]{1,0:T(8,128)(2,1)S(1)}, bf16[128,1280]{1,0:T(8,128)(2,1)S(1)}, u32[]{:S(2)}, u32[]{:S(2)}) %collective-permute-start.6) | collective-permute-done | bytes 327712 | tf_op jit(solution)/shard_map/ppermute | solution.py:29
  47.0 4.8 %collective-permute-done.10 = bf16[128,1280]{1,0:T(8,128)(2,1)S(1)} collective-permute-done((bf16[128,1280]{1,0:T(8,128)(2,1)S(1)}, bf16[128,1280]{1,0:T(8,128)(2,1)S(1)}, u32[]{:S(2)}, u32[]{:S(2)}) %collective-permute-start.10) | collective-permute-done | bytes 327712 | tf_op jit(solution)/shard_map/ppermute | solution.py:29
  52.7 15.7 %collective-permute-done.23.refs_0_ = bf16[320,1280]{1,0:T(8,128)(2,1)} collective-permute-done((bf16[320,1280]{1,0:T(8,128)(2,1)}, bf16[320,1280]{1,0:T(8,128)(2,1)}, u32[]{:S(2)}, u32[]{:S(2)}) %collective-permute-start.23) | collective-permute-done | bytes 819232 | tf_op jit(solution)/shard_map/ppermute | solution.py:29
  68.4 6.8 %collective-permute-done.12 = bf16[128,1280]{1,0:T(8,128)(2,1)S(1)} collective-permute-done((bf16[128,1280]{1,0:T(8,128)(2,1)S(1)}, bf16[128,1280]{1,0:T(8,128)(2,1)S(1)}, u32[]{:S(2)}, u32[]{:S(2)}) %collective-permute-start.12) | collective-permute-done | bytes 327712 | tf_op jit(solution)/shard_map/ppermute | solution.py:29
  77.3 2.5 %collective-permute-start.28 = (bf16[320,1280]{1,0:T(8,128)(2,1)}, bf16[320,1280]{1,0:T(8,128)(2,1)S(1)}, u32[]{:S(2)}, u32[]{:S(2)}) collective-permute-start(bf16[320,1280]{1,0:T(8,128)(2,1)} %collective-permute-done.23.refs_0_), channel_id=1, source_target_pairs={{0,8},{4,12},{8,0},{12,4},{16,24},{20,28},{24,16},{28,20},{1,9},{5... | collective-permute-start | bytes 2457608 | tf_op jit(solution)/shard_map/ppermute | solution.py:29
  79.8 12.2 %collective-permute-done.7 = bf16[256,1280]{1,0:T(8,128)(2,1)S(1)} collective-permute-done((bf16[256,1280]{1,0:T(8,128)(2,1)S(1)}, bf16[256,1280]{1,0:T(8,128)(2,1)S(1)}, u32[]{:S(2)}, u32[]{:S(2)}) %collective-permute-start.7) | collective-permute-done | bytes 655392 | tf_op jit(solution)/shard_map/ppermute | solution.py:29
  94.1 19.4 %local_levels.1 = f32[1024,1280]{1,0:T(8,128)S(1)} custom-call(s32[1]{0:T(128)} %bitcast.1.me_ref, bf16[4,256,1280]{2,1,0:T(8,128)(2,1)S(1)} %pad_maximum_fusion.value_ref, bf16[1024,128]{1,0:T(8,128)(2,1)S(1)} %copy-done.1, bf16[1024,40]{1,0:T(8,128)(2,1)S(1)} %copy-done.15, bf16[5,1024,40]{2,1,0:T(8,128)(2,1)S(1)} %copy-done.5, ...), custom_call_target="tpu_custom_call" | custom-call | tf_op jit(solution)/shard_map/local_levels/pallas_call | solution.py:450
  113.6 5.7 %finish.1 = (bf16[2,256,1280]{2,1,0:T(8,128)(2,1)S(1)}, bf16[2,256,1280]{2,1,0:T(8,128)(2,1)S(1)}) custom-call(s32[1]{0:T(128)} %bitcast.1.me_ref, f32[4,256,1280]{2,1,0:T(8,128)S(1)} %bitcast.47, bf16[4,256,128]{2,1,0:T(8,128)(2,1)S(1)} %bitcast.48, bf16[4,256,40]{2,1,0:T(8,128)(2,1)S(1)} %fusion.3.cross_ref, ...), custom_call_target="tpu_custom_call" | custom-call | tf_op jit(solution)/shard_map/finish/pallas_call | solution.py:483
  123.3 17.8 %collective-permute-done.19.refs_1_ = bf16[320,1280]{1,0:T(8,128)(2,1)S(1)} collective-permute-done((bf16[320,1280]{1,0:T(8,128)(2,1)}, bf16[320,1280]{1,0:T(8,128)(2,1)S(1)}, u32[]{:S(2)}, u32[]{:S(2)}) %collective-permute-start.19) | collective-permute-done | bytes 819232 | tf_op jit(solution)/shard_map/ppermute | solution.py:29
  141.6 17.0 %collective-permute-done.24.refs_1_ = bf16[320,1280]{1,0:T(8,128)(2,1)S(1)} collective-permute-done((bf16[320,1280]{1,0:T(8,128)(2,1)}, bf16[320,1280]{1,0:T(8,128)(2,1)S(1)}, u32[]{:S(2)}, u32[]{:S(2)}) %collective-permute-start.24) | collective-permute-done | bytes 819232 | tf_op jit(solution)/shard_map/ppermute | solution.py:29
  159.1 16.2 %collective-permute-done.29.refs_1_ = bf16[320,1280]{1,0:T(8,128)(2,1)S(1)} collective-permute-done((bf16[320,1280]{1,0:T(8,128)(2,1)S(1)}, bf16[320,1280]{1,0:T(8,128)(2,1)S(1)}, u32[]{:S(2)}, u32[]{:S(2)}) %collective-permute-start.29) | collective-permute-done | bytes 819232 | tf_op jit(solution)/shard_map/ppermute | solution.py:29
  175.4 4.4 %project.4 = (bf16[1,256,640]{2,1,0:T(8,128)(2,1)S(1)}, f32[256,640]{1,0:T(8,128)S(1)}) custom-call(s32[1]{0:T(128)} %bitcast.place_ref, bf16[2,256,1280]{2,1,0:T(8,128)(2,1)S(1)} %get-tuple-element.45.kept_ref, bf16[2,256,1280]{2,1,0:T(8,128)(2,1)S(1)} %collective-permute-done.15.other_ref, bf16[320,1280]{1,0:T(8,128)(2,1)S(1)} %bitcast.53, ...), custom_call_target="tpu_custom_call" | custom-call | tf_op jit(solution)/shard_map/project/pallas_call | solution.py:530
  181.3 4.1 %project.5 = (bf16[1,256,640]{2,1,0:T(8,128)(2,1)S(1)}, f32[256,640]{1,0:T(8,128)S(1)}) custom-call(s32[1]{0:T(128)} %bitcast.place_ref, bf16[2,256,1280]{2,1,0:T(8,128)(2,1)S(1)} %get-tuple-element.45.kept_ref, bf16[2,256,1280]{2,1,0:T(8,128)(2,1)S(1)} %collective-permute-done.15.other_ref, bf16[320,1280]{1,0:T(8,128)(2,1)} %collective-permute-done.11.refs_0_, ...), custom_call_target="tpu_custom_call" | custom-call | tf_op jit(solution)/shard_map/project/pallas_call | solution.py:530
  186.0 4.1 %project.6 = (bf16[1,256,640]{2,1,0:T(8,128)(2,1)S(1)}, f32[256,640]{1,0:T(8,128)S(1)}) custom-call(s32[1]{0:T(128)} %bitcast.place_ref, bf16[2,256,1280]{2,1,0:T(8,128)(2,1)S(1)} %get-tuple-element.45.kept_ref, bf16[2,256,1280]{2,1,0:T(8,128)(2,1)S(1)} %collective-permute-done.15.other_ref, bf16[320,1280]{1,0:T(8,128)(2,1)} %collective-permute-done.23.refs_0_, ...), custom_call_target="tpu_custom_call" | custom-call | tf_op jit(solution)/shard_map/project/pallas_call | solution.py:530
  191.7 3.0 %project.7 = (bf16[1,256,640]{2,1,0:T(8,128)(2,1)S(1)}, f32[256,640]{1,0:T(8,128)S(1)}) custom-call(s32[1]{0:T(128)} %bitcast.place_ref, bf16[2,256,1280]{2,1,0:T(8,128)(2,1)S(1)} %get-tuple-element.45.kept_ref, bf16[2,256,1280]{2,1,0:T(8,128)(2,1)S(1)} %collective-permute-done.15.other_ref, bf16[320,1280]{1,0:T(8,128)(2,1)S(1)} %collective-permute-done.28.refs_0_, ...), custom_call_target="tpu_custom_call" | custom-call | tf_op jit(solution)/shard_map/project/pallas_call | solution.py:530
  195.3 2.0 collective-permute-done.22.refs_3_
  197.3 7.0 %collective-permute-done.27.refs_5_ = bf16[256,640]{1,0:T(8,128)(2,1)S(1)} collective-permute-done((bf16[256,640]{1,0:T(8,128)(2,1)S(1)}, bf16[256,640]{1,0:T(8,128)(2,1)S(1)}, u32[]{:S(2)}, u32[]{:S(2)}) %collective-permute-start.27) | collective-permute-done | bytes 327712 | tf_op jit(solution)/shard_map/ppermute | solution.py:29
  204.4 6.6 %collective-permute-done.32.refs_7_ = bf16[256,640]{1,0:T(8,128)(2,1)S(1)} collective-permute-done((bf16[256,640]{1,0:T(8,128)(2,1)S(1)}, bf16[256,640]{1,0:T(8,128)(2,1)S(1)}, u32[]{:S(2)}, u32[]{:S(2)}) %collective-permute-start.32) | collective-permute-done | bytes 327712 | tf_op jit(solution)/shard_map/ppermute | solution.py:29
  (144 shorter events, 42.9 us)
Async XLA Ops:
  0.0 44.7 %collective-permute-start.9 = (bf16[320,1280]{1,0:T(8,128)(2,1)}, bf16[320,1280]{1,0:T(8,128)(2,1)}, u32[]{:S(2)}, u32[]{:S(2)}) collective-permute-start(bf16[320,1280]{1,0:T(8,128)(2,1)} %bitcast.49), channel_id=1, source_target_pairs={{0,4},{4,0},{8,12},{12,8},{16,20},{20,16},{24,28},{28,24},{1,5},{5... | collective-permute-start | bytes 2457608 | tf_op jit(solution)/shard_map/ppermute | solution.py:29
  2.9 49.0 %collective-permute-start.11 = (bf16[320,1280]{1,0:T(8,128)(2,1)}, bf16[320,1280]{1,0:T(8,128)(2,1)}, u32[]{:S(2)}, u32[]{:S(2)}) collective-permute-start(bf16[320,1280]{1,0:T(8,128)(2,1)} %bitcast.50), channel_id=1, source_target_pairs={{0,8},{4,12},{8,0},{12,4},{16,24},{20,28},{24,16},{28,20},{1,9},{5... | collective-permute-start | bytes 2457608 | tf_op jit(solution)/shard_map/ppermute | solution.py:29
  4.5 116.7 %collective-permute-start.16 = (bf16[320,1280]{1,0:T(8,128)(2,1)}, bf16[320,1280]{1,0:T(8,128)(2,1)}, u32[]{:S(2)}, u32[]{:S(2)}) collective-permute-start(bf16[320,1280]{1,0:T(8,128)(2,1)} %bitcast.51), channel_id=1, source_target_pairs={{0,1},{1,0},{2,3},{3,2},{4,5},{5,4},{6,7},{7,6},{8,9},{9,8},{10,11... | collective-permute-start | bytes 2457608 | tf_op jit(solution)/shard_map/ppermute | solution.py:29
  18.3 15.1 %collective-permute-start.5 = (bf16[2,128,1280]{2,1,0:T(8,128)(2,1)}, bf16[2,128,1280]{2,1,0:T(8,128)(2,1)}, u32[]{:S(2)}, u32[]{:S(2)}) collective-permute-start(bf16[2,128,1280]{2,1,0:T(8,128)(2,1)} %get-tuple-element.34), channel_id=1, source_target_pairs={{0,1},{1,0},{2,3},{3,2},{4,5},{5,4},{6,7},{7,6},{8,9},{9,8},{10,11... | collective-permute-start | bytes 1966088 | tf_op jit(solution)/shard_map/ppermute | solution.py:29
  30.7 37.7 %collective-permute-start.23 = (bf16[320,1280]{1,0:T(8,128)(2,1)}, bf16[320,1280]{1,0:T(8,128)(2,1)}, u32[]{:S(2)}, u32[]{:S(2)}) collective-permute-start(bf16[320,1280]{1,0:T(8,128)(2,1)} %bitcast.52), channel_id=1, source_target_pairs={{0,16},{4,20},{8,24},{12,28},{16,0},{20,4},{24,8},{28,12},{1,17},{... | collective-permute-start | bytes 2457608 | tf_op jit(solution)/shard_map/ppermute | solution.py:29
  43.1 33.5 %collective-permute-start.1 = (bf16[256,1280]{1,0:T(8,128)(2,1)}, bf16[256,1280]{1,0:T(8,128)(2,1)}, u32[]{:S(2)}, u32[]{:S(2)}) collective-permute-start(bf16[256,1280]{1,0:T(8,128)(2,1)} %get-tuple-element.62), channel_id=1, source_target_pairs={{0,2},{1,3},{2,0},{3,1},{4,6},{5,7},{6,4},{7,5},{8,10},{9,11},{10,... | collective-permute-start | bytes 1966088 | tf_op jit(solution)/shard_map/ppermute | solution.py:29
  51.8 25.5 %collective-permute-start = (bf16[256,1280]{1,0:T(8,128)(2,1)S(1)}, bf16[256,1280]{1,0:T(8,128)(2,1)S(1)}, u32[]{:S(2)}, u32[]{:S(2)}) collective-permute-start(bf16[256,1280]{1,0:T(8,128)(2,1)S(1)} %copy-done.18), channel_id=1, source_target_pairs={{0,1},{1,0},{2,3},{3,2},{4,5},{5,4},{6,7},{7,6},{8,9},{9,8},{10,11... | collective-permute-start | bytes 1966088 | tf_op jit(solution)/shard_map/ppermute | solution.py:29
  52.0 23.2 %collective-permute-start.12 = (bf16[128,1280]{1,0:T(8,128)(2,1)S(1)}, bf16[128,1280]{1,0:T(8,128)(2,1)S(1)}, u32[]{:S(2)}, u32[]{:S(2)}) collective-permute-start(bf16[128,1280]{1,0:T(8,128)(2,1)S(1)} %fusion.6), channel_id=1, source_target_pairs={{0,8},{4,12},{8,0},{12,4},{16,24},{20,28},{24,16},{28,20},{1,9},{5... | collective-permute-start | bytes 983048 | tf_op jit(solution)/shard_map/ppermute | solution.py:29
  68.4 53.5 %collective-permute-start.17 = (bf16[320,1280]{1,0:T(8,128)(2,1)}, bf16[320,1280]{1,0:T(8,128)(2,1)S(1)}, u32[]{:S(2)}, u32[]{:S(2)}) collective-permute-start(bf16[320,1280]{1,0:T(8,128)(2,1)} %collective-permute-done.9.refs_1_), channel_id=1, source_target_pairs={{0,1},{1,0},{2,3},{3,2},{4,5},{5,4},{6,7},{7,6},{8,9},{9,8},{10,11... | collective-permute-start | bytes 2457608 | tf_op jit(solution)/shard_map/ppermute | solution.py:29
  75.2 16.8 %collective-permute-start.7 = (bf16[256,1280]{1,0:T(8,128)(2,1)S(1)}, bf16[256,1280]{1,0:T(8,128)(2,1)S(1)}, u32[]{:S(2)}, u32[]{:S(2)}) collective-permute-start(bf16[256,1280]{1,0:T(8,128)(2,1)S(1)} %copy-done.17), channel_id=1, source_target_pairs={{0,3},{1,2},{2,1},{3,0},{4,7},{5,6},{6,5},{7,4},{8,11},{9,10},{10,... | collective-permute-start | bytes 1966088 | tf_op jit(solution)/shard_map/ppermute | solution.py:29
  76.6 37.0 %collective-permute-start.14 = (bf16[128,1280]{1,0:T(8,128)(2,1)S(1)}, bf16[128,1280]{1,0:T(8,128)(2,1)S(1)}, u32[]{:S(2)}, u32[]{:S(2)}) collective-permute-start(bf16[128,1280]{1,0:T(8,128)(2,1)S(1)} %add_convert_fusion), channel_id=1, source_target_pairs={{0,16},{4,20},{8,24},{12,28},{16,0},{20,4},{24,8},{28,12},{1,17},{... | collective-permute-start | bytes 983048 | tf_op jit(solution)/shard_map/ppermute | solution.py:29
  77.3 43.9 %collective-permute-start.28 = (bf16[320,1280]{1,0:T(8,128)(2,1)}, bf16[320,1280]{1,0:T(8,128)(2,1)S(1)}, u32[]{:S(2)}, u32[]{:S(2)}) collective-permute-start(bf16[320,1280]{1,0:T(8,128)(2,1)} %collective-permute-done.23.refs_0_), channel_id=1, source_target_pairs={{0,8},{4,12},{8,0},{12,4},{16,24},{20,28},{24,16},{28,20},{1,9},{5... | collective-permute-start | bytes 2457608 | tf_op jit(solution)/shard_map/ppermute | solution.py:29
  119.3 39.3 %collective-permute-start.15 = (bf16[2,256,1280]{2,1,0:T(8,128)(2,1)S(1)}, bf16[2,256,1280]{2,1,0:T(8,128)(2,1)S(1)}, u32[]{:S(2)}, u32[]{:S(2)}) collective-permute-start(bf16[2,256,1280]{2,1,0:T(8,128)(2,1)S(1)} %get-tuple-element.46), channel_id=1, source_target_pairs={{0,1},{1,0},{2,3},{3,2},{4,5},{5,4},{6,7},{7,6},{8,9},{9,8},{10,11... | collective-permute-start | bytes 3932168 | tf_op jit(solution)/shard_map/ppermute | solution.py:29
  119.8 21.3 %collective-permute-start.19 = (bf16[320,1280]{1,0:T(8,128)(2,1)}, bf16[320,1280]{1,0:T(8,128)(2,1)S(1)}, u32[]{:S(2)}, u32[]{:S(2)}) collective-permute-start(bf16[320,1280]{1,0:T(8,128)(2,1)} %collective-permute-done.11.refs_0_), channel_id=1, source_target_pairs={{0,4},{4,0},{8,12},{12,8},{16,20},{20,16},{24,28},{28,24},{1,5},{5... | collective-permute-start | bytes 2457608 | tf_op jit(solution)/shard_map/ppermute | solution.py:29
  121.2 19.9 %collective-permute-start.20 = (bf16[320,1280]{1,0:T(8,128)(2,1)}, bf16[320,1280]{1,0:T(8,128)(2,1)S(1)}, u32[]{:S(2)}, u32[]{:S(2)}) collective-permute-start(bf16[320,1280]{1,0:T(8,128)(2,1)} %collective-permute-done.11.refs_0_), channel_id=1, source_target_pairs={{0,1},{1,0},{2,3},{3,2},{4,5},{5,4},{6,7},{7,6},{8,9},{9,8},{10,11... | collective-permute-start | bytes 2457608 | tf_op jit(solution)/shard_map/ppermute | solution.py:29
  121.2 37.4 %collective-permute-start.24 = (bf16[320,1280]{1,0:T(8,128)(2,1)}, bf16[320,1280]{1,0:T(8,128)(2,1)S(1)}, u32[]{:S(2)}, u32[]{:S(2)}) collective-permute-start(bf16[320,1280]{1,0:T(8,128)(2,1)} %collective-permute-done.23.refs_0_), channel_id=1, source_target_pairs={{0,4},{4,0},{8,12},{12,8},{16,20},{20,16},{24,28},{28,24},{1,5},{5... | collective-permute-start | bytes 2457608 | tf_op jit(solution)/shard_map/ppermute | solution.py:29
  121.9 53.5 %collective-permute-start.29 = (bf16[320,1280]{1,0:T(8,128)(2,1)S(1)}, bf16[320,1280]{1,0:T(8,128)(2,1)S(1)}, u32[]{:S(2)}, u32[]{:S(2)}) collective-permute-start(bf16[320,1280]{1,0:T(8,128)(2,1)S(1)} %collective-permute-done.28.refs_0_), channel_id=1, source_target_pairs={{0,4},{4,0},{8,12},{12,8},{16,20},{20,16},{24,28},{28,24},{1,5},{5... | collective-permute-start | bytes 2457608 | tf_op jit(solution)/shard_map/ppermute | solution.py:29
  141.1 38.7 %collective-permute-start.21 = (bf16[320,1280]{1,0:T(8,128)(2,1)S(1)}, bf16[320,1280]{1,0:T(8,128)(2,1)S(1)}, u32[]{:S(2)}, u32[]{:S(2)}) collective-permute-start(bf16[320,1280]{1,0:T(8,128)(2,1)S(1)} %collective-permute-done.19.refs_1_), channel_id=1, source_target_pairs={{0,1},{1,0},{2,3},{3,2},{4,5},{5,4},{6,7},{7,6},{8,9},{9,8},{10,11... | collective-permute-start | bytes 2457608 | tf_op jit(solution)/shard_map/ppermute | solution.py:29
  141.1 44.3 %collective-permute-start.25 = (bf16[320,1280]{1,0:T(8,128)(2,1)}, bf16[320,1280]{1,0:T(8,128)(2,1)S(1)}, u32[]{:S(2)}, u32[]{:S(2)}) collective-permute-start(bf16[320,1280]{1,0:T(8,128)(2,1)} %collective-permute-done.23.refs_0_), channel_id=1, source_target_pairs={{0,1},{1,0},{2,3},{3,2},{4,5},{5,4},{6,7},{7,6},{8,9},{9,8},{10,11... | collective-permute-start | bytes 2457608 | tf_op jit(solution)/shard_map/ppermute | solution.py:29
  158.6 27.4 %collective-permute-start.26 = (bf16[320,1280]{1,0:T(8,128)(2,1)S(1)}, bf16[320,1280]{1,0:T(8,128)(2,1)S(1)}, u32[]{:S(2)}, u32[]{:S(2)}) collective-permute-start(bf16[320,1280]{1,0:T(8,128)(2,1)S(1)} %collective-permute-done.24.refs_1_), channel_id=1, source_target_pairs={{0,1},{1,0},{2,3},{3,2},{4,5},{5,4},{6,7},{7,6},{8,9},{9,8},{10,11... | collective-permute-start | bytes 2457608 | tf_op jit(solution)/shard_map/ppermute | solution.py:29
  158.6 33.0 %collective-permute-start.30 = (bf16[320,1280]{1,0:T(8,128)(2,1)S(1)}, bf16[320,1280]{1,0:T(8,128)(2,1)S(1)}, u32[]{:S(2)}, u32[]{:S(2)}) collective-permute-start(bf16[320,1280]{1,0:T(8,128)(2,1)S(1)} %collective-permute-done.28.refs_0_), channel_id=1, source_target_pairs={{0,1},{1,0},{2,3},{3,2},{4,5},{5,4},{6,7},{7,6},{8,9},{9,8},{10,11... | collective-permute-start | bytes 2457608 | tf_op jit(solution)/shard_map/ppermute | solution.py:29
  175.4 16.3 %collective-permute-start.31 = (bf16[320,1280]{1,0:T(8,128)(2,1)S(1)}, bf16[320,1280]{1,0:T(8,128)(2,1)S(1)}, u32[]{:S(2)}, u32[]{:S(2)}) collective-permute-start(bf16[320,1280]{1,0:T(8,128)(2,1)S(1)} %collective-permute-done.29.refs_1_), channel_id=1, source_target_pairs={{0,1},{1,0},{2,3},{3,2},{4,5},{5,4},{6,7},{7,6},{8,9},{9,8},{10,11... | collective-permute-start | bytes 2457608 | tf_op jit(solution)/shard_map/ppermute | solution.py:29
  179.7 15.5 %collective-permute-start.18 = (bf16[256,640]{1,0:T(8,128)(2,1)S(1)}, bf16[256,640]{1,0:T(8,128)(2,1)S(1)}, u32[]{:S(2)}, u32[]{:S(2)}) collective-permute-start(bf16[256,640]{1,0:T(8,128)(2,1)S(1)} %bitcast.55), channel_id=1, source_target_pairs={{0,2},{1,3},{2,0},{3,1},{4,6},{5,7},{6,4},{7,5},{8,10},{9,11},{10,... | collective-permute-start | bytes 983048 | tf_op jit(solution)/shard_map/ppermute | solution.py:29
  194.6 16.3 %collective-permute-start.32 = (bf16[256,640]{1,0:T(8,128)(2,1)S(1)}, bf16[256,640]{1,0:T(8,128)(2,1)S(1)}, u32[]{:S(2)}, u32[]{:S(2)}) collective-permute-start(bf16[256,640]{1,0:T(8,128)(2,1)S(1)} %bitcast.58), channel_id=1, source_target_pairs={{0,2},{1,3},{2,0},{3,1},{4,6},{5,7},{6,4},{7,5},{8,10},{9,11},{10,... | collective-permute-start | bytes 983048 | tf_op jit(solution)/shard_map/ppermute | solution.py:29
  (33 other events, 287.3 us)

commit v2 on v1

v2 whole, which is shorter than its diff:
```python
import functools

import jax
import jax.numpy as jnp
from jax import lax
from jax.experimental import pallas as pl
from jax.experimental.pallas import tpu as pltpu
from jax.sharding import PartitionSpec as P

CH = 64
EPSILON = 1e-05
EXTRA = 16
F32 = jnp.float32
BF16 = jnp.bfloat16
VMEM_LIMIT = 32 * 1024 * 1024


def dot(a, b):
    return lax.dot_general(a, b, (((1,), (0,)), ((), ())), preferred_element_type=F32)


def dot_t(a, b):
    return lax.dot_general(a, b, (((0,), (0,)), ((), ())), preferred_element_type=F32)


def dot_nt(a, b):
    return lax.dot_general(a, b, (((1,), (1,)), ((), ())), preferred_element_type=F32)


def swap(value, axis, distance):
    pairs = [(source, source ^ distance) for source in range(lax.axis_size(axis))]
    return lax.ppermute(value, axis, pairs)


def tie(value, *after):
    return lax.optimization_barrier((value,) + after)[0]


def three_parts(x):
    high = x.astype(BF16)
    rest = x - high.astype(F32)
    middle = rest.astype(BF16)
    low = (rest - middle.astype(F32)).astype(BF16)
    return high, middle, low


def two_parts(x):
    high = x.astype(BF16)
    return high, (x - high.astype(F32)).astype(BF16)


def halves(x, head_count):
    high = x.astype(BF16).astype(F32)
    lane = lax.broadcasted_iota(jnp.int32, x.shape, x.ndim - 1)
    return jnp.where(lane < head_count, high, x - high).astype(BF16)


def merge_rows(stretches):
    rows = [("own", c, 0) for c in range(stretches - 1)]
    for c in range(stretches - 1):
        k = 0
        while (c >> k) & 1:
            rows.append(("merge", c, k))
            k += 1
    return rows


def stretch_sums(decay_ref):
    tokens, width = decay_ref.shape
    row = lax.broadcasted_iota(jnp.int32, (CH, CH), 0)
    col = lax.broadcasted_iota(jnp.int32, (CH, CH), 1)
    lower = jnp.where(row >= col, 1.0, 0.0).astype(BF16)
    lower = jnp.concatenate([lower] * 3, axis=1)
    within, starts = [], [jnp.zeros((1, width), F32)]
    for c in range(tokens // CH):
        parts = jnp.concatenate(three_parts(decay_ref[c * CH : (c + 1) * CH, :]), axis=0)
        summed = dot(lower, parts)
        within.append(summed)
        starts.append(starts[-1] + summed[CH - 1 : CH, :])
    return within, starts


def fade_kernel(me_ref, decay_ref, *refs):
    fade_refs, total_ref = refs[:-1], refs[-1]
    head_count = decay_ref.shape[1]
    rows_dev = fade_refs[0].shape[0]
    within, starts = stretch_sums(decay_ref)
    total = starts[-1]
    total_ref[...] = jnp.concatenate([total, total], axis=1)
    blocks = len(fade_refs)
    per_block = rows_dev // CH
    me = me_ref[0]
    for block in range(blocks):
        parts = []
        for c in range(block * per_block, (block + 1) * per_block):
            factor = jnp.exp(total - starts[c] - within[c])
            parts.append(halves(jnp.concatenate([factor, factor], axis=1), head_count))
        fade = jnp.concatenate(parts, axis=0)
        for r, fade_ref in enumerate(fade_refs):

            @pl.when((me ^ r) == block)
            def _():
                fade_ref[...] = fade


def factors_kernel(
    decay_ref, class_ref, table_ref, in_ref, out_ref,
    lift_ref, read_ref, cross_ref, merge_ref, score_ref, masked_ref,
):
    tokens, head_count = decay_ref.shape
    width = 2 * head_count
    stretches = tokens // CH
    levels, classes, _ = table_ref.shape
    local = read_ref.shape[0] - 1
    tables = [jnp.concatenate(three_parts(table_ref[level]), axis=0) for level in range(levels)]
    within, starts = stretch_sums(decay_ref)
    within = [jnp.concatenate([x, x], axis=1) for x in within]
    starts = [jnp.concatenate([x, x], axis=1) for x in starts]
    class_iota = lax.broadcasted_iota(jnp.int32, (CH, 3 * classes), 1) % classes
    for c in range(stretches):
        rows = slice(c * CH, (c + 1) * CH)
        lift_ref[rows, :] = halves(jnp.exp(-within[c]), head_count)
        onehot = jnp.where(class_ref[rows, :] == class_iota, 1.0, 0.0).astype(BF16)
        read_ref[0, rows, :] = halves(jnp.exp(within[c]) * dot(onehot, tables[0]), head_count)
        for level in range(1, local + 1):
            if (c >> (level - 1)) & 1:
                begin = starts[c] - starts[(c >> (level - 1)) << (level - 1)]
                factor = jnp.exp(within[c] + begin) * dot(onehot, tables[level])
                read_ref[level, rows, :] = halves(factor, head_count)
            else:
                read_ref[level, rows, :] = jnp.zeros((CH, width), BF16)
        far = jnp.exp(within[c] + starts[c])
        for level in range(local + 1, levels):
            far_factor = far * dot(onehot, tables[level])
            cross_ref[level - local - 1, rows, :] = halves(far_factor, head_count)
    exps = []
    for kind, c, k in merge_rows(stretches):
        first = c if kind == "own" else c + 1 - 2**k
        exps.append(jnp.exp(starts[c + 1] - starts[first]))
    exps += [jnp.zeros((1, width), F32)] * (merge_ref.shape[0] - len(exps))
    merge_ref[...] = halves(jnp.concatenate(exps, axis=0), head_count)
    groups, _, group_rows, _ = score_ref.shape
    row = lax.broadcasted_iota(jnp.int32, (group_rows, group_rows), 0)
    col = lax.broadcasted_iota(jnp.int32, (group_rows, group_rows), 1)
    inside = (row // CH == col // CH) & (row >= col)
    state_size = in_ref.shape[1]
    lane = lax.broadcasted_iota(jnp.int32, (state_size, group_rows), 1) // CH
    for g in range(groups):
        rows = slice(g * group_rows, (g + 1) * group_rows)
        scores = jnp.where(inside, dot_nt(out_ref[rows, :], in_ref[rows, :]), 0.0)
        score_ref[g, 0], score_ref[g, 1] = two_parts(scores)
        turned = jnp.transpose(in_ref[rows, :].astype(F32))
        for s in range(group_rows // CH):
            at = slice(s * state_size, (s + 1) * state_size)
            masked_ref[g, at, :] = jnp.where(lane == s, turned, 0.0).astype(BF16)


def partial_state_kernel(me_ref, *refs):
    even_ref, odd_ref, *fade_refs = refs[:-4]
    in_ref, spread_ref, keep_ref, send_ref = refs[-4:]
    spread = spread_ref[...]
    turned = in_ref[...]
    for i in range(len(fade_refs) // 2):

        @pl.when(pl.program_id(0) == i)
        def _():
            odd = (dot(fade_refs[2 * i + 1][...], spread) * odd_ref[...].astype(F32)).astype(BF16)
            send_ref[0] = dot(turned, odd).astype(BF16)
            even = (dot(fade_refs[2 * i][...], spread) * even_ref[...].astype(F32)).astype(BF16)
            keep_ref[0] = dot(turned, even)


def fold_kernel(keep_ref, got_ref, own_ref, *far_refs):
    own_ref[...] = keep_ref[0] + got_ref[0].astype(F32)
    for i, far_ref in enumerate(far_refs):
        far_ref[...] = (keep_ref[i + 1] + got_ref[i + 1].astype(F32)).astype(BF16)


def pack_state(sent_ref, state, total):
    rows, width = state.shape[0], total.shape[1]
    sent_ref[:rows, :] = state.astype(BF16)
    sent_ref[rows:, :] = jnp.zeros((EXTRA, state.shape[1]), BF16)
    parts = list(three_parts(total))
    parts.append(jnp.zeros((EXTRA - len(parts), width), BF16))
    sent_ref[rows:, :width] = jnp.concatenate(parts, axis=0)


def first_kernel(own_ref, total_ref, *refs):
    *far_refs, running_ref, sent_ref = refs
    running = own_ref[...]
    for far_ref in far_refs:
        running = running + far_ref[...].astype(F32)
    running_ref[...] = running
    pack_state(sent_ref, running, total_ref[...])


def merge_kernel(
    bit, place_ref, running_ref, total_ref, offset_ref, got_ref, spread_ref,
    next_running_ref, next_total_ref, next_offset_ref, factor_ref, sent_ref,
):
    rows, width = running_ref.shape[0], total_ref.shape[1]
    head_count = width // 2
    place = place_ref[0]
    upper = place // 2**bit % 2 == 1
    total = total_ref[...]
    parts = got_ref[rows:, :width].astype(F32)
    partner = parts[0:1] + parts[1:2] + parts[2:3]
    fading = jnp.exp(jnp.where(upper, total, partner))
    fading = halves(jnp.broadcast_to(fading, (EXTRA, width)), head_count)
    fading = dot(fading, spread_ref[...])[0:1, :]
    got, running = got_ref[:rows, :].astype(F32), running_ref[...]
    merged = fading * jnp.where(upper, got, running) + jnp.where(upper, running, got)
    next_running_ref[...] = merged
    joined = total + partner
    next_total_ref[...] = joined
    offset = jnp.where(upper, offset_ref[...] + partner, offset_ref[...])
    next_offset_ref[...] = offset
    next_upper = place // 2 ** (bit + 1) % 2 == 1
    factor = jnp.where(next_upper, jnp.exp(offset), 0.0)
    factor_ref[...] = halves(jnp.broadcast_to(factor, (EXTRA, width)), head_count)
    pack_state(sent_ref, merged, joined)


def local_kernel(me_ref, near, parts, *refs):
    value_refs, refs = refs[:parts], refs[parts:]
    out_ref, lift_ref, read_ref, merge_ref, score_ref, masked_ref, spread_ref = refs[:7]
    skip_ref, cross_ref, *refs = refs[7:]
    factor_refs, state_refs, refs = refs[:near], refs[near : 2 * near], refs[2 * near :]
    pre_ref, nodes, sums, operand = refs
    group_rows = value_refs[0].shape[0]
    groups = len(value_refs)
    me = me_ref[0]
    per_group = group_rows // CH
    stretches = groups * per_group
    state_size = out_ref.shape[2]
    spread = spread_ref[...]
    merges = dot(merge_ref[...], spread)
    place = {kind: i for i, kind in enumerate(merge_rows(stretches))}
    skip = skip_ref[...]
    states = [
        (state_ref[:state_size, :], dot(factor_ref[...], spread)[0:1, :])
        for state_ref, factor_ref in zip(state_refs, factor_refs)
    ]
    for r, value_ref in enumerate(value_refs):
        g = me ^ r
        value = value_ref[...].astype(F32)
        high, low = two_parts(dot(lift_ref[g], spread) * value)
        direct = dot(score_ref[g, 0], high) + dot(score_ref[g, 0], low) + dot(score_ref[g, 1], high)
        total = dot(read_ref[0, g], spread) * direct + skip * value
        for level, (state, row) in enumerate(states):
            total = total + dot(cross_ref[level, g], spread) * (dot(out_ref[g], state) * row)
        pre_ref[g] = total
        nodes[g] = dot(masked_ref[g], high) + dot(masked_ref[g], low)

    def gain(level, g, first, count):
        at = slice(first * CH, (first + count) * CH)
        readers = out_ref[g, at, :]
        twice = jnp.concatenate([readers, readers], axis=1)
        gained = dot(twice, operand[level - 1])
        pre_ref[g, at, :] += dot(read_ref[level, g, at, :], spread) * gained

    for c in range(stretches):
        g, s = divmod(c, per_group)
        level = 1
        while 2 ** (level - 1) < stretches:
            span = 2 ** (level - 1)
            if c % (2 * span) == span:
                for other in range(c, c + span, per_group):
                    gain(level, other // per_group, other % per_group, min(span, per_group))
            level += 1
        if c + 1 < stretches:
            row = place[("own", c, 0)]
            node = nodes[g, s * state_size : (s + 1) * state_size, :] * merges[row : row + 1, :]
            k = 0
            while (c >> k) & 1:
                row = place[("merge", c, k)]
                node = node + merges[row : row + 1, :] * sums[k]
                k += 1
            sums[k] = node
            n_high, n_low = two_parts(node)
            operand[k, :state_size, :] = n_high
            operand[k, state_size:, :] = n_low


def finish_kernel(
    me_ref, pre_ref, out_ref, cross_ref, factor_ref, state_ref, spread_ref, same_ref, gain_ref, *refs
):
    keep_ref, send_refs = refs[0], refs[1:]
    parts = pre_ref.shape[0]
    me = me_ref[0]
    spread = spread_ref[...]
    same = same_ref[...]
    gain = gain_ref[...]
    state = state_ref[: out_ref.shape[2], :]
    row = dot(factor_ref[...], spread)[0:1, :]
    for r in range(parts):
        at = me ^ r
        total = pre_ref[at] + dot(cross_ref[at], spread) * (dot(out_ref[at], state) * row)
        mean_square = dot((total * total).astype(BF16), same)
        normed = (total * lax.rsqrt(mean_square + EPSILON) * gain).astype(BF16)
        if r % 2 == 0:
            keep_ref[r // 2] = normed
        else:
            send_refs[r // 2][...] = normed


def project_kernel(place_ref, kept_ref, *refs):
    far_ref, own_ref = refs[-2:]
    half = kept_ref.shape[0]
    other_refs, refs = refs[:half], refs[half:-2]
    count = len(refs) // 2
    weights, partners = refs[:count], refs[count:]
    width = weights[0].shape[0]
    for i in list(range(1, half)) + [0]:
        kept, other = kept_ref[i], other_refs[i][...]
        found = [
            dot_nt(kept, weight[...]) + dot_nt(other, partner[...])
            for weight, partner in zip(weights, partners)
        ]
        for bit in range(count.bit_length() - 1):
            turn = place_ref[0] // 2**bit % 2 == 1
            found = [jnp.where(turn, found[j ^ 2**bit], found[j]) for j in range(count)]
        for j, result in enumerate(found):
            if i > 0:
                far_ref[i - 1, :, j * width : (j + 1) * width] = result.astype(BF16)
            else:
                own_ref[:, j * width : (j + 1) * width] = result


def assemble_kernel(place_ref, *refs):
    out_ref = refs[-1]
    width = refs[0].shape[1]
    groups = out_ref.shape[1] // width
    each = (len(refs) - 1) // groups
    for p in range(groups):
        own_ref, *far_refs = refs[p * each : (p + 1) * each]
        total = own_ref[...]
        for far_ref in far_refs:
            total = total + far_ref[...].astype(F32)
        start = pl.multiple_of((place_ref[0] ^ p) * width, width)
        out_ref[:, pl.ds(start, width)] = total.astype(BF16)


def feature_tile(features):
    for tile in (256, 128):
        if features % tile == 0:
            return tile
    return features


def whole(shape):
    return pl.BlockSpec(shape, lambda *_: (0,) * len(shape))


def on_device(
    values,
    state_in,
    state_out,
    log_decay,
    level_class,
    level_table,
    skip_gain,
    norm_gain,
    out_weight,
):
    heads_size = lax.axis_size("head")
    ctx_size = lax.axis_size("ctx")
    ctx_bits = ctx_size.bit_length() - 1
    me = lax.axis_index("head")
    me1 = me.reshape(1).astype(jnp.int32)
    position = lax.axis_index("ctx")
    tokens = state_in.shape[0]
    rows_dev = values.shape[0]
    head_count = log_decay.shape[1]
    features = values.shape[1] // heads_size
    head_width = features // head_count
    state_size = state_in.shape[1]
    stretches = tokens // CH
    local = stretches.bit_length() - 1
    levels = level_table.shape[1]
    wide = 2 * head_count
    tile = feature_tile(features)
    tiles = features // tile
    half = heads_size // 2
    params = pltpu.CompilerParams(vmem_limit_bytes=VMEM_LIMIT)
    cheap = pl.CostEstimate(flops=0, bytes_accessed=0, transcendentals=0)

    spread = (
        jnp.arange(wide)[:, None] % head_count == (jnp.arange(features) // head_width)[None, :]
    ).astype(BF16)
    same = (
        (jnp.arange(tile)[:, None] // head_width == jnp.arange(tile)[None, :] // head_width)
        / head_width
    ).astype(BF16)

    def kernel_call(body, name, out_shape, **kwargs):
        return pl.pallas_call(
            body, out_shape=out_shape, compiler_params=params, cost_estimate=cheap, name=name, **kwargs
        )

    def shape(dims, kind=BF16):
        return jax.ShapeDtypeStruct(dims, kind)

    smem = pl.BlockSpec(memory_space=pltpu.SMEM)
    vmem = pl.BlockSpec(memory_space=pltpu.VMEM)
    place1 = position.reshape(1).astype(jnp.int32)

    *fades, total = kernel_call(
        fade_kernel,
        "fade",
        tuple([shape((rows_dev, wide))] * heads_size + [shape((1, wide), F32)]),
        in_specs=[smem, vmem],
    )(me1, log_decay)
    fades = [fades[0]] + [swap(fades[r], "head", r) for r in range(1, heads_size)]

    held = {0: out_weight.T}
    for bit in range(ctx_bits):
        held[2**bit] = swap(held[0], "ctx", 2**bit)

    def value_swap(r, after=None):
        sent = lax.dynamic_slice_in_dim(values, (me ^ r) * features, features, 1)
        return swap(sent if after is None else tie(sent, after), "head", r)

    early = {r: value_swap(r) for r in range(1, heads_size) if r <= half}

    in_turned = lax.dynamic_slice_in_dim(state_in, me * rows_dev, rows_dev, 0).T
    keep, send = kernel_call(
        partial_state_kernel,
        "partial_states",
        (shape((half, state_size, features), F32), shape((half, state_size, features))),
        grid_spec=pltpu.PrefetchScalarGridSpec(
            num_scalar_prefetch=1,
            grid=(half,),
            in_specs=[
                pl.BlockSpec((rows_dev, features), lambda i, m: (0, m[0] ^ (2 * i))),
                pl.BlockSpec((rows_dev, features), lambda i, m: (0, m[0] ^ (2 * i + 1))),
            ]
            + [whole((rows_dev, wide))] * heads_size
            + [whole((state_size, rows_dev)), whole((wide, features))],
            out_specs=[
                pl.BlockSpec((1, state_size, features), lambda i, m: (i, 0, 0)),
                pl.BlockSpec((1, state_size, features), lambda i, m: (i, 0, 0)),
            ],
        ),
    )(me1, values, values, *fades, in_turned, spread)
    own_state, *far_states = kernel_call(
        fold_kernel,
        "fold",
        tuple(
            [shape((state_size, features), F32)] + [shape((state_size, features))] * (half - 1)
        ),
    )(keep, swap(send, "head", 1))
    got_states = [
        swap(tie(far, *early.values()), "head", 2 * (i + 1)) for i, far in enumerate(far_states)
    ]

    merge_count = -(-len(merge_rows(stretches)) // 16) * 16
    table = jnp.transpose(level_table, (1, 0, 2))
    table = jnp.concatenate([table, table], axis=2)
    lift, read, cross, merge, scores, masked = kernel_call(
        factors_kernel,
        "factors",
        (
            shape((tokens, wide)),
            shape((local + 1, tokens, wide)),
            shape((levels - local - 1, tokens, wide)),
            shape((merge_count, wide)),
            shape((heads_size, 2, rows_dev, rows_dev)),
            shape((heads_size, rows_dev // CH * state_size, rows_dev)),
        ),
    )(
        tie(log_decay, own_state), level_class.reshape(tokens, 1), table, state_in, state_out
    )

    running, sent = kernel_call(
        first_kernel,
        "first_state",
        (shape((state_size, features), F32), shape((state_size + EXTRA, features))),
    )(own_state, total, *got_states)
    late = {r: value_swap(r, got_states[-1]) for r in range(1, heads_size) if r not in early}
    offset = jnp.zeros((1, wide), F32)
    factors = [jnp.broadcast_to((position % 2).astype(BF16), (EXTRA, wide))]
    factors[0] = jnp.where(jnp.arange(wide)[None, :] < head_count, factors[0], 0)
    states = []
    for bit in range(ctx_bits):
        if bit == 0:
            sent = tie(sent, held[1], held[2])
        if bit == ctx_bits - 1:
            sent = tie(sent, *late.values())
        states.append(swap(sent, "ctx", 2**bit))
        if bit + 1 < ctx_bits:
            running, total, offset, factor, sent = kernel_call(
                functools.partial(merge_kernel, bit),
                "merge",
                (
                    shape((state_size, features), F32),
                    shape((1, wide), F32),
                    shape((1, wide), F32),
                    shape((EXTRA, wide)),
                    shape((state_size + EXTRA, features)),
                ),
                in_specs=[smem] + [vmem] * 5,
            )(place1, running, total, offset, states[-1], spread)
            factors.append(factor)

    columns = out_weight.shape[1]
    near = ctx_bits - 1
    for r in range(2, ctx_size):
        low = r & -r
        if r not in held and low > 1:
            held[r] = swap(tie(held[r ^ low], states[min(low.bit_length() - 1, near - 1)]), "ctx", low)
    for bit in range(1, ctx_bits):
        r = 2**bit
        held[r + 1] = swap(tie(held[r], states[min(bit - 1, near - 1)]), "ctx", 1)

    skip_row = jnp.repeat(skip_gain, head_width)[None, :]
    grouped = (heads_size, rows_dev)
    pre = kernel_call(
        lambda me_ref, *refs: local_kernel(me_ref, near, heads_size, *refs),
        "local_levels",
        shape((heads_size, rows_dev, features), F32),
        grid_spec=pltpu.PrefetchScalarGridSpec(
            num_scalar_prefetch=1,
            grid=(tiles,),
            in_specs=[pl.BlockSpec((rows_dev, tile), lambda f, m: (0, m[0] * tiles + f))]
            + [pl.BlockSpec((rows_dev, tile), lambda f, m: (0, f))] * (heads_size - 1)
            + [
                whole(grouped + (state_size,)),
                whole(grouped + (wide,)),
                whole((local + 1,) + grouped + (wide,)),
                whole((merge_count, wide)),
                whole(scores.shape),
                whole(masked.shape),
                pl.BlockSpec((wide, tile), lambda f, m: (0, f)),
                pl.BlockSpec((1, tile), lambda f, m: (0, f)),
                whole((ctx_bits,) + grouped + (wide,)),
            ]
            + [whole((EXTRA, wide))] * near
            + [pl.BlockSpec((state_size + EXTRA, tile), lambda f, m: (0, f))] * near,
            out_specs=pl.BlockSpec(grouped + (tile,), lambda f, m: (0, 0, f)),
            scratch_shapes=[
                pltpu.VMEM((heads_size, rows_dev // CH * state_size, tile), F32),
                pltpu.VMEM((max(local, 1), state_size, tile), F32),
                pltpu.VMEM((max(local, 1), 2 * state_size, tile), BF16),
            ],
        ),
    )(
        me1,
        values,
        *[early[r] if r in early else late[r] for r in range(1, heads_size)],
        state_out.reshape(grouped + (state_size,)),
        lift.reshape(grouped + (wide,)),
        read.reshape((local + 1,) + grouped + (wide,)),
        merge,
        scores,
        masked,
        spread,
        skip_row,
        cross.reshape((ctx_bits,) + grouped + (wide,)),
        *factors[:near],
        *states[:near],
    )

    kept, *sends = kernel_call(
        finish_kernel,
        "finish",
        tuple([shape((half, rows_dev, features))] + [shape((rows_dev, features))] * half),
        grid_spec=pltpu.PrefetchScalarGridSpec(
            num_scalar_prefetch=1,
            grid=(tiles,),
            in_specs=[
                pl.BlockSpec(grouped + (tile,), lambda f, m: (0, 0, f)),
                whole(grouped + (state_size,)),
                whole(grouped + (wide,)),
                whole((EXTRA, wide)),
                pl.BlockSpec((state_size + EXTRA, tile), lambda f, m: (0, f)),
                pl.BlockSpec((wide, tile), lambda f, m: (0, f)),
                whole((tile, tile)),
                pl.BlockSpec((1, tile), lambda f, m: (0, f)),
            ],
            out_specs=[pl.BlockSpec((half, rows_dev, tile), lambda f, m: (0, 0, f))]
            + [pl.BlockSpec((rows_dev, tile), lambda f, m: (0, f))] * half,
        ),
    )(
        me1,
        pre,
        state_out.reshape(grouped + (state_size,)),
        cross[-1].reshape(grouped + (wide,)),
        tie(factors[-1], *[held[r] for r in range(2, ctx_size // 2 + 1) if r in held]),
        states[-1],
        spread,
        same,
        norm_gain[None, :],
    )
    others = [swap(array, "head", 1) for array in sends]

    count = 1
    while count * columns % 128 and 2 * count <= ctx_size:
        count *= 2
    partners = {r: swap(held[r], "head", 1) for r in range(count)}
    pieces = []
    for first in range(0, ctx_size, count):
        group = range(first, first + count)
        for r in group:
            if r not in held:
                side = (r ^ 1) & -(r ^ 1)
                top = lax.slice_in_dim(tie(held[r ^ 1], pieces[0]), 0, columns // 2, axis=0)
                rest = lax.slice_in_dim(tie(held[r ^ side], pieces[0]), columns // 2, columns, axis=0)
                held[r] = jnp.concatenate([swap(top, "ctx", 1), swap(rest, "ctx", side)], axis=0)
            if r not in partners:
                partners[r] = swap(tie(held[r], pieces[0]), "head", 1)
        far, own = kernel_call(
            project_kernel,
            "project",
            (
                shape((half - 1, rows_dev, count * columns)),
                shape((rows_dev, count * columns), F32),
            ),
            in_specs=[smem] + [vmem] * (1 + half + 2 * count),
        )(place1, kept, *others, *[held[r] for r in group], *[partners[r] for r in group])
        pieces.append(own)
        pieces += [swap(far[i - 1], "head", 2 * i) for i in range(1, half)]
    return kernel_call(
        assemble_kernel,
        "assemble",
        shape((rows_dev, ctx_size * columns)),
        in_specs=[smem] + [vmem] * len(pieces),
    )(place1 // count, *pieces)


def solution(mesh):
    return jax.shard_map(
        on_device,
        mesh=mesh,
        in_specs=(
            P(("ctx", "head"), None),
            P("ctx", None),
            P("ctx", None),
            P("ctx", "head"),
            P("ctx"),
            P(None, None, "head"),
            P("head"),
            P("head"),
            P("head", "ctx"),
        ),
        out_specs=P(("ctx", "head"), None),
        check_vma=False,
    )
```

time: 213 us -> 194 us (0.911)
  waiting for transfers between devices: 114 us -> 88.6 us
  local copies, waits for them, and re-layouts: 12.7 us -> 19.9 us
  other arithmetic: 7.48 us -> 3.12 us
  Pallas kernels: 46.7 us -> 50.4 us
    ppermute x33, waiting for transfers between devices: 114 us -> 88.6 us  [swap(): return lax.ppermute(value, axis, pairs)]
    unnamed x50 -> x58, local copies, waits for them, and re-layouts: 7.58 us -> 12 us
    pallas_call x10 -> x14, Pallas kernels: 46.7 us -> 50.4 us  [the longest x1 18.5 us: on_device(): kernel_call(lambda me_ref, *refs: local_kernel(me_ref, near, heads_size,...]
    another operation x5 -> x0, other arithmetic: 2.64 us -> none  [the longest x1 1.56 us: on_device(): jnp.stack(gathered)]
    dynamic_slice x2, local copies, waits for them, and re-layouts: 1.58 us -> 3.85 us  [the longest x1 3 us: value_swap(): sent = lax.dynamic_slice_in_dim(values, (me ^ r) * features, features, 1)]
  transfers between devices with their start and end apart: 33 -> 33, of which waited for: 12 -> 13; matrix products, arithmetic and copies ran while one was open for 6% -> 7% of each run, Pallas kernels for 21% -> 24%
where the time goes in v2:
time: 194 us; the launch traced here: 193 us
  waiting for transfers between devices  88.6 us (46%)
  Pallas kernels  50.4 us (26%)
  starting transfers between devices  30.4 us (16%)
  local copies, waits for them, and re-layouts  19.9 us (10%)
  other arithmetic  3.12 us (2%)
    ppermute x33, waiting for transfers between devices, swap(): return lax.ppermute(value, axis, pairs)  88.6 us
    ppermute x33, starting transfers between devices, swap(): return lax.ppermute(value, axis, pairs)  30.4 us
    pallas_call x1, Pallas kernels, on_device(): kernel_call(lambda me_ref, *refs: local_kernel(me_ref, near, heads_size,...  18.5 us
    pallas_call x4, Pallas kernels, on_device(): kernel_call(project_kernel, 'project', (shape((half - 1, rows_dev, count...  17 us
    unnamed x58, local copies, waits for them, and re-layouts  12 us
    pallas_call x1, Pallas kernels, on_device(): kernel_call(finish_kernel, 'finish', tuple([shape((half, rows_dev, featur...  6.53 us
  transfers between devices with their start and end apart: 33, of which 13 were waited for; matrix products, arithmetic and copies ran while one was open for 7% of the time, Pallas kernels for 24%

profile of v2, /device:TPU:0, one launch (start us, length us, event | category | flops | bytes accessed | tf_op | source)
XLA Modules:
  0.0 192.9 jit_solution(11838391155584919917)
XLA Ops:
  2.6 2.6 %collective-permute-start.3 = (bf16[256,40]{1,0:T(8,128)(2,1)S(1)}, bf16[256,40]{1,0:T(8,128)(2,1)S(1)}, u32[]{:S(2)}, u32[]{:S(2)}) collective-permute-start(bf16[256,40]{1,0:T(8,128)(2,1)S(1)} %get-tuple-element.56), channel_id=1, source_target_pairs={{0,2},{1,3},{2,0},{3,1},{4,6},{5,7},{6,4},{7,5},{8,10},{9,11},{10,... | collective-permute-start | bytes 61448 | tf_op jit(solution)/shard_map/ppermute | solution.py:32
  5.4 3.0 %constant_dynamic-slice_fusion.1 = (bf16[256,1280]{1,0:T(8,128)(2,1)}, bf16[256,1280]{1,0:T(8,128)(2,1)}, bf16[256,1280]{1,0:T(8,128)(2,1)}) fusion(bf16[256,5120]{1,0:T(8,128)(2,1)} %refs_0_.3, s32[]{:T(128)S(6)} %select_n.85, s32[]{:T(128)S(6)} %select_n.84, s32[]{:T(128)S(6)} %select_n.83), kind=kLoop, calls=%fused_computation.19 | loop fusion | bytes 3932172 | tf_op jit(solution)/shard_map/dynamic_slice | solution.py:421
  9.4 1.9 partial_states.1
  16.9 12.0 %collective-permute-done.1.refs_2_ = bf16[256,1280]{1,0:T(8,128)(2,1)S(1)} collective-permute-done((bf16[256,1280]{1,0:T(8,128)(2,1)S(1)}, bf16[256,1280]{1,0:T(8,128)(2,1)S(1)}, u32[]{:S(2)}, u32[]{:S(2)}) %collective-permute-start.1) | collective-permute-done | bytes 655392 | tf_op jit(solution)/shard_map/ppermute | solution.py:32
  31.5 7.4 %collective-permute-done.6.refs_0_ = bf16[128,1280]{1,0:T(8,128)(2,1)S(1)} collective-permute-done((bf16[128,1280]{1,0:T(8,128)(2,1)S(1)}, bf16[128,1280]{1,0:T(8,128)(2,1)S(1)}, u32[]{:S(2)}, u32[]{:S(2)}) %collective-permute-start.6) | collective-permute-done | bytes 327712 | tf_op jit(solution)/shard_map/ppermute | solution.py:32
  42.8 2.6 %collective-permute-start.13 = (bf16[320,1280]{1,0:T(8,128)(2,1)}, bf16[320,1280]{1,0:T(8,128)(2,1)}, u32[]{:S(2)}, u32[]{:S(2)}) collective-permute-start(bf16[320,1280]{1,0:T(8,128)(2,1)} %bitcast.9.refs_2_), channel_id=1, source_target_pairs={{0,16},{4,20},{8,24},{12,28},{16,0},{20,4},{24,8},{28,12},{1,17},{... | collective-permute-start | bytes 2457608 | tf_op jit(solution)/shard_map/ppermute | solution.py:32
  45.4 4.8 %collective-permute-done.10.got_ref.refs_15_ = bf16[144,1280]{1,0:T(8,128)(2,1)S(1)} collective-permute-done((bf16[144,1280]{1,0:T(8,128)(2,1)S(1)}, bf16[144,1280]{1,0:T(8,128)(2,1)S(1)}, u32[]{:S(2)}, u32[]{:S(2)}) %collective-permute-start.10) | collective-permute-done | bytes 368672 | tf_op jit(solution)/shard_map/ppermute | solution.py:32
  53.3 1.8 collective-permute-start.11
  56.6 15.1 %collective-permute-done.11.refs_16_.got_ref = bf16[144,1280]{1,0:T(8,128)(2,1)S(1)} collective-permute-done((bf16[144,1280]{1,0:T(8,128)(2,1)}, bf16[144,1280]{1,0:T(8,128)(2,1)S(1)}, u32[]{:S(2)}, u32[]{:S(2)}) %collective-permute-start.11) | collective-permute-done | bytes 368672 | tf_op jit(solution)/shard_map/ppermute | solution.py:32
  74.1 2.3 %collective-permute-start.14 = (bf16[144,1280]{1,0:T(8,128)(2,1)}, bf16[144,1280]{1,0:T(8,128)(2,1)}, u32[]{:S(2)}, u32[]{:S(2)}) collective-permute-start(bf16[144,1280]{1,0:T(8,128)(2,1)} %get-tuple-element.84), channel_id=1, source_target_pairs={{0,16},{4,20},{8,24},{12,28},{16,0},{20,4},{24,8},{28,12},{1,17},{... | collective-permute-start | bytes 1105928 | tf_op jit(solution)/shard_map/ppermute | solution.py:32
  77.7 12.2 %collective-permute-done.13.refs_2_ = bf16[320,1280]{1,0:T(8,128)(2,1)} collective-permute-done((bf16[320,1280]{1,0:T(8,128)(2,1)}, bf16[320,1280]{1,0:T(8,128)(2,1)}, u32[]{:S(2)}, u32[]{:S(2)}) %collective-permute-start.13) | collective-permute-done | bytes 819232 | tf_op jit(solution)/shard_map/ppermute | solution.py:32
  94.4 1.7 pad_maximum_fusion.table_ref
  96.2 2.0 %copy.17.decay_ref = f32[1024,20]{1,0:T(8,128)} copy(f32[1024,20]{0,1:T(8,128)} %param.12) | data formatting | bytes 163840 | tf_op jit(solution)/shard_map/optimization_barrier | solution.py:36
  102.9 18.5 %local_levels.1.pre_ref = f32[4,256,1280]{2,1,0:T(8,128)S(1)} custom-call(s32[1]{0:T(128)} %bitcast.1.me_ref, bf16[256,5120]{1,0:T(8,128)(2,1)S(1)} %copy-done, bf16[256,1280]{1,0:T(8,128)(2,1)S(1)} %copy-done.12, bf16[256,1280]{1,0:T(8,128)(2,1)S(1)} %copy-done.14, bf16[256,1280]{1,0:T(8,128)(2,1)} %collective-permute-done.7.refs_3_, ...), custom_call_target="tpu_custom_call" | custom-call | tf_op jit(solution)/shard_map/local_levels/pallas_call | solution.py:518
  121.5 6.5 %finish.1 = (bf16[2,256,1280]{2,1,0:T(8,128)(2,1)S(1)}, bf16[256,1280]{1,0:T(8,128)(2,1)S(1)}, bf16[256,1280]{1,0:T(8,128)(2,1)S(1)}) custom-call(s32[1]{0:T(128)} %bitcast.1.me_ref, f32[4,256,1280]{2,1,0:T(8,128)S(1)} %local_levels.1.pre_ref, bf16[4,256,128]{2,1,0:T(8,128)(2,1)S(1)} %bitcast.16, bf16[4,256,40]{2,1,0:T(8,128)(2,1)S(1)} %bitcast.19, ...), custom_call_target="tpu_custom_call" | custom-call | tf_op jit(solution)/shard_map/finish/pallas_call | solution.py:564
  131.1 4.7 %project.4 = (bf16[1,256,640]{2,1,0:T(8,128)(2,1)S(1)}, f32[256,640]{1,0:T(8,128)S(1)}) custom-call(s32[1]{0:T(128)} %bitcast.place_ref, bf16[2,256,1280]{2,1,0:T(8,128)(2,1)S(1)} %get-tuple-element.85.kept_ref, bf16[256,1280]{1,0:T(8,128)(2,1)S(1)} %collective-permute-done.15.refs_0_, bf16[256,1280]{1,0:T(8,128)(2,1)S(1)} %collective-permute-done.16.refs_1_, ...), custom_call_target="tpu_custom_call" | custom-call | tf_op jit(solution)/shard_map/project/pallas_call | solution.py:612
  137.4 12.5 %collective-permute-done.23.refs_3_ = bf16[320,1280]{1,0:T(8,128)(2,1)S(1)} collective-permute-done((bf16[320,1280]{1,0:T(8,128)(2,1)}, bf16[320,1280]{1,0:T(8,128)(2,1)S(1)}, u32[]{:S(2)}, u32[]{:S(2)}) %collective-permute-start.23) | collective-permute-done | bytes 819232 | tf_op jit(solution)/shard_map/ppermute | solution.py:32
  151.9 6.0 %collective-permute-done.28 = bf16[160,1280]{1,0:T(8,128)(2,1)S(1)} collective-permute-done((bf16[160,1280]{1,0:T(8,128)(2,1)S(1)}, bf16[160,1280]{1,0:T(8,128)(2,1)S(1)}, u32[]{:S(2)}, u32[]{:S(2)}) %collective-permute-start.28) | collective-permute-done | bytes 409632 | tf_op jit(solution)/shard_map/ppermute | solution.py:32
  157.9 2.3 %collective-permute-done.29 = bf16[160,1280]{1,0:T(8,128)(2,1)S(1)} collective-permute-done((bf16[160,1280]{1,0:T(8,128)(2,1)S(1)}, bf16[160,1280]{1,0:T(8,128)(2,1)S(1)}, u32[]{:S(2)}, u32[]{:S(2)}) %collective-permute-start.29) | collective-permute-done | bytes 409632 | tf_op jit(solution)/shard_map/ppermute | solution.py:32
  161.6 4.1 %project.5 = (bf16[1,256,640]{2,1,0:T(8,128)(2,1)S(1)}, f32[256,640]{1,0:T(8,128)S(1)}) custom-call(s32[1]{0:T(128)} %bitcast.place_ref, bf16[2,256,1280]{2,1,0:T(8,128)(2,1)S(1)} %get-tuple-element.85.kept_ref, bf16[256,1280]{1,0:T(8,128)(2,1)S(1)} %collective-permute-done.15.refs_0_, bf16[256,1280]{1,0:T(8,128)(2,1)S(1)} %collective-permute-done.16.refs_1_, ...), custom_call_target="tpu_custom_call" | custom-call | tf_op jit(solution)/shard_map/project/pallas_call | solution.py:612
  167.0 4.1 %project.6 = (bf16[1,256,640]{2,1,0:T(8,128)(2,1)S(1)}, f32[256,640]{1,0:T(8,128)S(1)}) custom-call(s32[1]{0:T(128)} %bitcast.place_ref, bf16[2,256,1280]{2,1,0:T(8,128)(2,1)S(1)} %get-tuple-element.85.kept_ref, bf16[256,1280]{1,0:T(8,128)(2,1)S(1)} %collective-permute-done.15.refs_0_, bf16[256,1280]{1,0:T(8,128)(2,1)S(1)} %collective-permute-done.16.refs_1_, ...), custom_call_target="tpu_custom_call" | custom-call | tf_op jit(solution)/shard_map/project/pallas_call | solution.py:612
  172.0 4.1 %project.7 = (bf16[1,256,640]{2,1,0:T(8,128)(2,1)S(1)}, f32[256,640]{1,0:T(8,128)S(1)}) custom-call(s32[1]{0:T(128)} %bitcast.place_ref, bf16[2,256,1280]{2,1,0:T(8,128)(2,1)S(1)} %get-tuple-element.85.kept_ref, bf16[256,1280]{1,0:T(8,128)(2,1)S(1)} %collective-permute-done.15.refs_0_, bf16[256,1280]{1,0:T(8,128)(2,1)S(1)} %collective-permute-done.16.refs_1_, ...), custom_call_target="tpu_custom_call" | custom-call | tf_op jit(solution)/shard_map/project/pallas_call | solution.py:612
  178.4 7.0 %collective-permute-done.26.refs_5_ = bf16[256,640]{1,0:T(8,128)(2,1)S(1)} collective-permute-done((bf16[256,640]{1,0:T(8,128)(2,1)S(1)}, bf16[256,640]{1,0:T(8,128)(2,1)S(1)}, u32[]{:S(2)}, u32[]{:S(2)}) %collective-permute-start.26) | collective-permute-done | bytes 327712 | tf_op jit(solution)/shard_map/ppermute | solution.py:32
  185.4 6.2 %collective-permute-done.32.refs_7_ = bf16[256,640]{1,0:T(8,128)(2,1)S(1)} collective-permute-done((bf16[256,640]{1,0:T(8,128)(2,1)S(1)}, bf16[256,640]{1,0:T(8,128)(2,1)S(1)}, u32[]{:S(2)}, u32[]{:S(2)}) %collective-permute-start.32) | collective-permute-done | bytes 327712 | tf_op jit(solution)/shard_map/ppermute | solution.py:32
  (134 shorter events, 47.0 us)
Async XLA Ops:
  11.9 17.0 %collective-permute-start.1 = (bf16[256,1280]{1,0:T(8,128)(2,1)S(1)}, bf16[256,1280]{1,0:T(8,128)(2,1)S(1)}, u32[]{:S(2)}, u32[]{:S(2)}) collective-permute-start(bf16[256,1280]{1,0:T(8,128)(2,1)S(1)} %copy-done.22), channel_id=1, source_target_pairs={{0,2},{1,3},{2,0},{3,1},{4,6},{5,7},{6,4},{7,5},{8,10},{9,11},{10,... | collective-permute-start | bytes 1966088 | tf_op jit(solution)/shard_map/ppermute | solution.py:32
  13.7 26.2 %collective-permute-start.8 = (bf16[320,1280]{1,0:T(8,128)(2,1)}, bf16[320,1280]{1,0:T(8,128)(2,1)S(1)}, u32[]{:S(2)}, u32[]{:S(2)}) collective-permute-start(bf16[320,1280]{1,0:T(8,128)(2,1)} %bitcast.9.refs_2_), channel_id=1, source_target_pairs={{0,4},{4,0},{8,12},{12,8},{16,20},{20,16},{24,28},{28,24},{1,5},{5... | collective-permute-start | bytes 2457608 | tf_op jit(solution)/shard_map/ppermute | solution.py:32
  15.1 24.8 %collective-permute-start.9 = (bf16[320,1280]{1,0:T(8,128)(2,1)}, bf16[320,1280]{1,0:T(8,128)(2,1)S(1)}, u32[]{:S(2)}, u32[]{:S(2)}) collective-permute-start(bf16[320,1280]{1,0:T(8,128)(2,1)} %bitcast.9.refs_2_), channel_id=1, source_target_pairs={{0,8},{4,12},{8,0},{12,4},{16,24},{20,28},{24,16},{28,20},{1,9},{5... | collective-permute-start | bytes 2457608 | tf_op jit(solution)/shard_map/ppermute | solution.py:32
  29.8 9.2 %collective-permute-start.6 = (bf16[128,1280]{1,0:T(8,128)(2,1)S(1)}, bf16[128,1280]{1,0:T(8,128)(2,1)S(1)}, u32[]{:S(2)}, u32[]{:S(2)}) collective-permute-start(bf16[128,1280]{1,0:T(8,128)(2,1)S(1)} %get-tuple-element.61), channel_id=1, source_target_pairs={{0,2},{1,3},{2,0},{3,1},{4,6},{5,7},{6,4},{7,5},{8,10},{9,11},{10,... | collective-permute-start | bytes 983048 | tf_op jit(solution)/shard_map/ppermute | solution.py:32
  41.1 9.1 %collective-permute-start.10 = (bf16[144,1280]{1,0:T(8,128)(2,1)S(1)}, bf16[144,1280]{1,0:T(8,128)(2,1)S(1)}, u32[]{:S(2)}, u32[]{:S(2)}) collective-permute-start(bf16[144,1280]{1,0:T(8,128)(2,1)S(1)} %get-tuple-element.74), channel_id=1, source_target_pairs={{0,4},{4,0},{8,12},{12,8},{16,20},{20,16},{24,28},{28,24},{1,5},{5... | collective-permute-start | bytes 1105928 | tf_op jit(solution)/shard_map/ppermute | solution.py:32
  42.8 31.3 %collective-permute-start.7 = (bf16[256,1280]{1,0:T(8,128)(2,1)}, bf16[256,1280]{1,0:T(8,128)(2,1)}, u32[]{:S(2)}, u32[]{:S(2)}) collective-permute-start(bf16[256,1280]{1,0:T(8,128)(2,1)} %get-tuple-element.62), channel_id=1, source_target_pairs={{0,3},{1,2},{2,1},{3,0},{4,7},{5,6},{6,5},{7,4},{8,11},{9,10},{10,... | collective-permute-start | bytes 1966088 | tf_op jit(solution)/shard_map/ppermute | solution.py:32
  42.8 47.2 %collective-permute-start.13 = (bf16[320,1280]{1,0:T(8,128)(2,1)}, bf16[320,1280]{1,0:T(8,128)(2,1)}, u32[]{:S(2)}, u32[]{:S(2)}) collective-permute-start(bf16[320,1280]{1,0:T(8,128)(2,1)} %bitcast.9.refs_2_), channel_id=1, source_target_pairs={{0,16},{4,20},{8,24},{12,28},{16,0},{20,4},{24,8},{28,12},{1,17},{... | collective-permute-start | bytes 2457608 | tf_op jit(solution)/shard_map/ppermute | solution.py:32
  53.3 18.4 %collective-permute-start.11 = (bf16[144,1280]{1,0:T(8,128)(2,1)}, bf16[144,1280]{1,0:T(8,128)(2,1)S(1)}, u32[]{:S(2)}, u32[]{:S(2)}) collective-permute-start(bf16[144,1280]{1,0:T(8,128)(2,1)} %get-tuple-element.76), channel_id=1, source_target_pairs={{0,8},{4,12},{8,0},{12,4},{16,24},{20,28},{24,16},{28,20},{1,9},{5... | collective-permute-start | bytes 1105928 | tf_op jit(solution)/shard_map/ppermute | solution.py:32
  55.1 66.4 %collective-permute-start.12 = (bf16[320,1280]{1,0:T(8,128)(2,1)}, bf16[320,1280]{1,0:T(8,128)(2,1)}, u32[]{:S(2)}, u32[]{:S(2)}) collective-permute-start(bf16[320,1280]{1,0:T(8,128)(2,1)} %copy-done.7), channel_id=1, source_target_pairs={{0,4},{4,0},{8,12},{12,8},{16,20},{20,16},{24,28},{28,24},{1,5},{5... | collective-permute-start | bytes 2457608 | tf_op jit(solution)/shard_map/ppermute | solution.py:32
  56.6 72.0 %collective-permute-start.17 = (bf16[320,1280]{1,0:T(8,128)(2,1)}, bf16[320,1280]{1,0:T(8,128)(2,1)}, u32[]{:S(2)}, u32[]{:S(2)}) collective-permute-start(bf16[320,1280]{1,0:T(8,128)(2,1)} %bitcast.9.refs_2_), channel_id=1, source_target_pairs={{0,1},{1,0},{2,3},{3,2},{4,5},{5,4},{6,7},{7,6},{8,9},{9,8},{10,11... | collective-permute-start | bytes 2457608 | tf_op jit(solution)/shard_map/ppermute | solution.py:32
  74.1 47.3 %collective-permute-start.14 = (bf16[144,1280]{1,0:T(8,128)(2,1)}, bf16[144,1280]{1,0:T(8,128)(2,1)}, u32[]{:S(2)}, u32[]{:S(2)}) collective-permute-start(bf16[144,1280]{1,0:T(8,128)(2,1)} %get-tuple-element.84), channel_id=1, source_target_pairs={{0,16},{4,20},{8,24},{12,28},{16,0},{20,4},{24,8},{28,12},{1,17},{... | collective-permute-start | bytes 1105928 | tf_op jit(solution)/shard_map/ppermute | solution.py:32
  77.1 51.9 %collective-permute-start.18 = (bf16[320,1280]{1,0:T(8,128)(2,1)}, bf16[320,1280]{1,0:T(8,128)(2,1)}, u32[]{:S(2)}, u32[]{:S(2)}) collective-permute-start(bf16[320,1280]{1,0:T(8,128)(2,1)} %copy-done.9), channel_id=1, source_target_pairs={{0,1},{1,0},{2,3},{3,2},{4,5},{5,4},{6,7},{7,6},{8,9},{9,8},{10,11... | collective-permute-start | bytes 2457608 | tf_op jit(solution)/shard_map/ppermute | solution.py:32
  89.9 45.8 %collective-permute-start.27 = (bf16[320,1280]{1,0:T(8,128)(2,1)}, bf16[320,1280]{1,0:T(8,128)(2,1)}, u32[]{:S(2)}, u32[]{:S(2)}) collective-permute-start(bf16[320,1280]{1,0:T(8,128)(2,1)} %collective-permute-done.13.refs_2_), channel_id=1, source_target_pairs={{0,8},{4,12},{8,0},{12,4},{16,24},{20,28},{24,16},{28,20},{1,9},{5... | collective-permute-start | bytes 2457608 | tf_op jit(solution)/shard_map/ppermute | solution.py:32
  128.6 21.3 %collective-permute-start.23 = (bf16[320,1280]{1,0:T(8,128)(2,1)}, bf16[320,1280]{1,0:T(8,128)(2,1)S(1)}, u32[]{:S(2)}, u32[]{:S(2)}) collective-permute-start(bf16[320,1280]{1,0:T(8,128)(2,1)} %collective-permute-done.13.refs_2_), channel_id=1, source_target_pairs={{0,4},{4,0},{8,12},{12,8},{16,20},{20,16},{24,28},{28,24},{1,5},{5... | collective-permute-start | bytes 2457608 | tf_op jit(solution)/shard_map/ppermute | solution.py:32
  136.8 21.0 %collective-permute-start.28 = (bf16[160,1280]{1,0:T(8,128)(2,1)S(1)}, bf16[160,1280]{1,0:T(8,128)(2,1)S(1)}, u32[]{:S(2)}, u32[]{:S(2)}) collective-permute-start(bf16[160,1280]{1,0:T(8,128)(2,1)S(1)} %slice.10), channel_id=1, source_target_pairs={{0,4},{4,0},{8,12},{12,8},{16,20},{20,16},{24,28},{28,24},{1,5},{5... | collective-permute-start | bytes 1228808 | tf_op jit(solution)/shard_map/ppermute | solution.py:32
  137.4 22.8 %collective-permute-start.20 = (bf16[320,1280]{1,0:T(8,128)(2,1)S(1)}, bf16[320,1280]{1,0:T(8,128)(2,1)S(1)}, u32[]{:S(2)}, u32[]{:S(2)}) collective-permute-start(bf16[320,1280]{1,0:T(8,128)(2,1)S(1)} %copy-done.8), channel_id=1, source_target_pairs={{0,1},{1,0},{2,3},{3,2},{4,5},{5,4},{6,7},{7,6},{8,9},{9,8},{10,11... | collective-permute-start | bytes 2457608 | tf_op jit(solution)/shard_map/ppermute | solution.py:32
  149.9 10.3 %collective-permute-start.29 = (bf16[160,1280]{1,0:T(8,128)(2,1)S(1)}, bf16[160,1280]{1,0:T(8,128)(2,1)S(1)}, u32[]{:S(2)}, u32[]{:S(2)}) collective-permute-start(bf16[160,1280]{1,0:T(8,128)(2,1)S(1)} %slice.11), channel_id=1, source_target_pairs={{0,8},{4,12},{8,0},{12,4},{16,24},{20,28},{24,16},{28,20},{1,9},{5... | collective-permute-start | bytes 1228808 | tf_op jit(solution)/shard_map/ppermute | solution.py:32
  151.4 15.7 %collective-permute-start.25 = (bf16[320,1280]{1,0:T(8,128)(2,1)S(1)}, bf16[320,1280]{1,0:T(8,128)(2,1)S(1)}, u32[]{:S(2)}, u32[]{:S(2)}) collective-permute-start(bf16[320,1280]{1,0:T(8,128)(2,1)S(1)} %collective-permute-done.23.refs_3_), channel_id=1, source_target_pairs={{0,1},{1,0},{2,3},{3,2},{4,5},{5,4},{6,7},{7,6},{8,9},{9,8},{10,11... | collective-permute-start | bytes 2457608 | tf_op jit(solution)/shard_map/ppermute | solution.py:32
  151.4 20.6 %collective-permute-start.30 = (bf16[320,1280]{1,0:T(8,128)(2,1)}, bf16[320,1280]{1,0:T(8,128)(2,1)S(1)}, u32[]{:S(2)}, u32[]{:S(2)}) collective-permute-start(bf16[320,1280]{1,0:T(8,128)(2,1)} %collective-permute-done.27.refs_2_), channel_id=1, source_target_pairs={{0,1},{1,0},{2,3},{3,2},{4,5},{5,4},{6,7},{7,6},{8,9},{9,8},{10,11... | collective-permute-start | bytes 2457608 | tf_op jit(solution)/shard_map/ppermute | solution.py:32
  160.3 11.7 %collective-permute-start.31 = (bf16[320,1280]{1,0:T(8,128)(2,1)S(1)}, bf16[320,1280]{1,0:T(8,128)(2,1)S(1)}, u32[]{:S(2)}, u32[]{:S(2)}) collective-permute-start(bf16[320,1280]{1,0:T(8,128)(2,1)S(1)} %constant_dynamic-update-slice_fusion.refs_3_), channel_id=1, source_target_pairs={{0,1},{1,0},{2,3},{3,2},{4,5},{5,4},{6,7},{7,6},{8,9},{9,8},{10,11... | collective-permute-start | bytes 2457608 | tf_op jit(solution)/shard_map/ppermute | solution.py:32
  160.8 16.6 %collective-permute-start.19 = (bf16[256,640]{1,0:T(8,128)(2,1)S(1)}, bf16[256,640]{1,0:T(8,128)(2,1)S(1)}, u32[]{:S(2)}, u32[]{:S(2)}) collective-permute-start(bf16[256,640]{1,0:T(8,128)(2,1)S(1)} %bitcast.22), channel_id=1, source_target_pairs={{0,2},{1,3},{2,0},{3,1},{4,6},{5,7},{6,4},{7,5},{8,10},{9,11},{10,... | collective-permute-start | bytes 983048 | tf_op jit(solution)/shard_map/ppermute | solution.py:32
  165.7 12.7 %collective-permute-start.22 = (bf16[256,640]{1,0:T(8,128)(2,1)S(1)}, bf16[256,640]{1,0:T(8,128)(2,1)S(1)}, u32[]{:S(2)}, u32[]{:S(2)}) collective-permute-start(bf16[256,640]{1,0:T(8,128)(2,1)S(1)} %bitcast.23), channel_id=1, source_target_pairs={{0,2},{1,3},{2,0},{3,1},{4,6},{5,7},{6,4},{7,5},{8,10},{9,11},{10,... | collective-permute-start | bytes 983048 | tf_op jit(solution)/shard_map/ppermute | solution.py:32
  171.2 14.3 %collective-permute-start.26 = (bf16[256,640]{1,0:T(8,128)(2,1)S(1)}, bf16[256,640]{1,0:T(8,128)(2,1)S(1)}, u32[]{:S(2)}, u32[]{:S(2)}) collective-permute-start(bf16[256,640]{1,0:T(8,128)(2,1)S(1)} %bitcast.24), channel_id=1, source_target_pairs={{0,2},{1,3},{2,0},{3,1},{4,6},{5,7},{6,4},{7,5},{8,10},{9,11},{10,... | collective-permute-start | bytes 983048 | tf_op jit(solution)/shard_map/ppermute | solution.py:32
  176.1 15.5 %collective-permute-start.32 = (bf16[256,640]{1,0:T(8,128)(2,1)S(1)}, bf16[256,640]{1,0:T(8,128)(2,1)S(1)}, u32[]{:S(2)}, u32[]{:S(2)}) collective-permute-start(bf16[256,640]{1,0:T(8,128)(2,1)S(1)} %bitcast.25), channel_id=1, source_target_pairs={{0,2},{1,3},{2,0},{3,1},{4,6},{5,7},{6,4},{7,5},{8,10},{9,11},{10,... | collective-permute-start | bytes 983048 | tf_op jit(solution)/shard_map/ppermute | solution.py:32
  (36 other events, 295.3 us)

commit v3 on v2

--- a/solution.py
+++ b/solution.py
@@ -80,27 +80,20 @@
     return within, starts
 
 
-def fade_kernel(me_ref, decay_ref, *refs):
-    fade_refs, total_ref = refs[:-1], refs[-1]
+def fade_kernel(me_ref, decay_ref, fade_ref, total_ref):
+    blocks, rows_dev, _ = fade_ref.shape
     head_count = decay_ref.shape[1]
-    rows_dev = fade_refs[0].shape[0]
     within, starts = stretch_sums(decay_ref)
     total = starts[-1]
     total_ref[...] = jnp.concatenate([total, total], axis=1)
-    blocks = len(fade_refs)
     per_block = rows_dev // CH
     me = me_ref[0]
     for block in range(blocks):
-        parts = []
         for c in range(block * per_block, (block + 1) * per_block):
             factor = jnp.exp(total - starts[c] - within[c])
-            parts.append(halves(jnp.concatenate([factor, factor], axis=1), head_count))
-        fade = jnp.concatenate(parts, axis=0)
-        for r, fade_ref in enumerate(fade_refs):
-
-            @pl.when((me ^ r) == block)
-            def _():
-                fade_ref[...] = fade
+            factor = halves(jnp.concatenate([factor, factor], axis=1), head_count)
+            first = (c - block * per_block) * CH
+            fade_ref[me ^ block, first : first + CH, :] = factor
 
 
 def factors_kernel(
@@ -222,13 +215,14 @@
 
 
 def local_kernel(me_ref, near, parts, *refs):
-    value_refs, refs = refs[:parts], refs[parts:]
+    count = 1 + max(at for pieces in parts for at, _, _ in pieces)
+    value_refs, refs = refs[:count], refs[count:]
     out_ref, lift_ref, read_ref, merge_ref, score_ref, masked_ref, spread_ref = refs[:7]
     skip_ref, cross_ref, *refs = refs[7:]
     factor_refs, state_refs, refs = refs[:near], refs[near : 2 * near], refs[2 * near :]
     pre_ref, nodes, sums, operand = refs
     group_rows = value_refs[0].shape[0]
-    groups = len(value_refs)
+    groups = len(parts)
     me = me_ref[0]
     per_group = group_rows // CH
     stretches = groups * per_group
@@ -241,9 +235,10 @@
         (state_ref[:state_size, :], dot(factor_ref[...], spread)[0:1, :])
         for state_ref, factor_ref in zip(state_refs, factor_refs)
     ]
-    for r, value_ref in enumerate(value_refs):
+    for r, pieces in enumerate(parts):
         g = me ^ r
-        value = value_ref[...].astype(F32)
+        value = [value_refs[at][first : first + rows, :] for at, first, rows in pieces]
+        value = jnp.concatenate(value, axis=0).astype(F32)
         high, low = two_parts(dot(lift_ref[g], spread) * value)
         direct = dot(score_ref[g, 0], high) + dot(score_ref[g, 0], low) + dot(score_ref[g, 1], high)
         total = dot(read_ref[0, g], spread) * direct + skip * value
@@ -285,7 +280,6 @@
 def finish_kernel(
     me_ref, pre_ref, out_ref, cross_ref, factor_ref, state_ref, spread_ref, same_ref, gain_ref, *refs
 ):
-    keep_ref, send_refs = refs[0], refs[1:]
     parts = pre_ref.shape[0]
     me = me_ref[0]
     spread = spread_ref[...]
@@ -298,33 +292,26 @@
         total = pre_ref[at] + dot(cross_ref[at], spread) * (dot(out_ref[at], state) * row)
         mean_square = dot((total * total).astype(BF16), same)
         normed = (total * lax.rsqrt(mean_square + EPSILON) * gain).astype(BF16)
-        if r % 2 == 0:
-            keep_ref[r // 2] = normed
-        else:
-            send_refs[r // 2][...] = normed
-
-
-def project_kernel(place_ref, kept_ref, *refs):
-    far_ref, own_ref = refs[-2:]
-    half = kept_ref.shape[0]
-    other_refs, refs = refs[:half], refs[half:-2]
+        refs[r][...] = normed
+
+
+def project_kernel(place_ref, *refs):
+    *refs, out_ref = refs
+    rows = out_ref.shape[0]
+    kept_refs, other_refs, refs = refs[:rows], refs[rows : 2 * rows], refs[2 * rows :]
     count = len(refs) // 2
     weights, partners = refs[:count], refs[count:]
     width = weights[0].shape[0]
-    for i in list(range(1, half)) + [0]:
-        kept, other = kept_ref[i], other_refs[i][...]
+    for i, (kept_ref, other_ref) in enumerate(zip(kept_refs, other_refs)):
         found = [
-            dot_nt(kept, weight[...]) + dot_nt(other, partner[...])
+            dot_nt(kept_ref[...], weight[...]) + dot_nt(other_ref[...], partner[...])
             for weight, partner in zip(weights, partners)
         ]
         for bit in range(count.bit_length() - 1):
             turn = place_ref[0] // 2**bit % 2 == 1
             found = [jnp.where(turn, found[j ^ 2**bit], found[j]) for j in range(count)]
         for j, result in enumerate(found):
-            if i > 0:
-                far_ref[i - 1, :, j * width : (j + 1) * width] = result.astype(BF16)
-            else:
-                own_ref[:, j * width : (j + 1) * width] = result
+            out_ref[i, :, j * width : (j + 1) * width] = result.astype(out_ref.dtype)
 
 
 def assemble_kernel(place_ref, *refs):
@@ -385,14 +372,6 @@
     params = pltpu.CompilerParams(vmem_limit_bytes=VMEM_LIMIT)
     cheap = pl.CostEstimate(flops=0, bytes_accessed=0, transcendentals=0)
 
-    spread = (
-        jnp.arange(wide)[:, None] % head_count == (jnp.arange(features) // head_width)[None, :]
-    ).astype(BF16)
-    same = (
-        (jnp.arange(tile)[:, None] // head_width == jnp.arange(tile)[None, :] // head_width)
-        / head_width
-    ).astype(BF16)
-
     def kernel_call(body, name, out_shape, **kwargs):
         return pl.pallas_call(
             body, out_shape=out_shape, compiler_params=params, cost_estimate=cheap, name=name, **kwargs
@@ -405,125 +384,178 @@
     vmem = pl.BlockSpec(memory_space=pltpu.VMEM)
     place1 = position.reshape(1).astype(jnp.int32)
 
-    *fades, total = kernel_call(
-        fade_kernel,
-        "fade",
-        tuple([shape((rows_dev, wide))] * heads_size + [shape((1, wide), F32)]),
-        in_specs=[smem, vmem],
-    )(me1, log_decay)
-    fades = [fades[0]] + [swap(fades[r], "head", r) for r in range(1, heads_size)]
+    def fenced(body, *operands):
+        shapes = jax.eval_shape(body, *operands)
+        zeros = lambda *_: jax.tree.map(lambda leaf: jnp.zeros(leaf.shape, leaf.dtype), shapes)
+        return lax.cond(position < ctx_size, body, zeros, *operands)
+
+    def spread_heads():
+        return (
+            jnp.arange(wide)[:, None] % head_count == (jnp.arange(features) // head_width)[None, :]
+        ).astype(BF16)
 
     held = {0: out_weight.T}
     for bit in range(ctx_bits):
         held[2**bit] = swap(held[0], "ctx", 2**bit)
 
-    def value_swap(r, after=None):
-        sent = lax.dynamic_slice_in_dim(values, (me ^ r) * features, features, 1)
-        return swap(sent if after is None else tie(sent, after), "head", r)
-
-    early = {r: value_swap(r) for r in range(1, heads_size) if r <= half}
-
-    in_turned = lax.dynamic_slice_in_dim(state_in, me * rows_dev, rows_dev, 0).T
-    keep, send = kernel_call(
-        partial_state_kernel,
-        "partial_states",
-        (shape((half, state_size, features), F32), shape((half, state_size, features))),
-        grid_spec=pltpu.PrefetchScalarGridSpec(
-            num_scalar_prefetch=1,
-            grid=(half,),
-            in_specs=[
-                pl.BlockSpec((rows_dev, features), lambda i, m: (0, m[0] ^ (2 * i))),
-                pl.BlockSpec((rows_dev, features), lambda i, m: (0, m[0] ^ (2 * i + 1))),
-            ]
-            + [whole((rows_dev, wide))] * heads_size
-            + [whole((state_size, rows_dev)), whole((wide, features))],
-            out_specs=[
-                pl.BlockSpec((1, state_size, features), lambda i, m: (i, 0, 0)),
-                pl.BlockSpec((1, state_size, features), lambda i, m: (i, 0, 0)),
-            ],
-        ),
-    )(me1, values, values, *fades, in_turned, spread)
-    own_state, *far_states = kernel_call(
-        fold_kernel,
-        "fold",
-        tuple(
-            [shape((state_size, features), F32)] + [shape((state_size, features))] * (half - 1)
-        ),
-    )(keep, swap(send, "head", 1))
-    got_states = [
-        swap(tie(far, *early.values()), "head", 2 * (i + 1)) for i, far in enumerate(far_states)
-    ]
+    def merge_step(bit, running, total, offset, got, spread):
+        return kernel_call(
+            functools.partial(merge_kernel, bit),
+            "merge",
+            (
+                shape((state_size, features), F32),
+                shape((1, wide), F32),
+                shape((1, wide), F32),
+                shape((EXTRA, wide)),
+                shape((state_size + EXTRA, features)),
+            ),
+            in_specs=[smem] + [vmem] * 5,
+        )(place1, running, total, offset, got, spread)
 
     merge_count = -(-len(merge_rows(stretches)) // 16) * 16
-    table = jnp.transpose(level_table, (1, 0, 2))
-    table = jnp.concatenate([table, table], axis=2)
-    lift, read, cross, merge, scores, masked = kernel_call(
-        factors_kernel,
-        "factors",
-        (
-            shape((tokens, wide)),
-            shape((local + 1, tokens, wide)),
-            shape((levels - local - 1, tokens, wide)),
-            shape((merge_count, wide)),
-            shape((heads_size, 2, rows_dev, rows_dev)),
-            shape((heads_size, rows_dev // CH * state_size, rows_dev)),
-        ),
-    )(
-        tie(log_decay, own_state), level_class.reshape(tokens, 1), table, state_in, state_out
+
+    def near_steps(running, total, sent, log_decay, level_class, level_table, state_in, state_out):
+        table = jnp.transpose(level_table, (1, 0, 2))
+        table = jnp.concatenate([table, table], axis=2)
+        tables = kernel_call(
+            factors_kernel,
+            "factors",
+            (
+                shape((tokens, wide)),
+                shape((local + 1, tokens, wide)),
+                shape((levels - local - 1, tokens, wide)),
+                shape((merge_count, wide)),
+                shape((heads_size, 2, rows_dev, rows_dev)),
+                shape((heads_size, rows_dev // CH * state_size, rows_dev)),
+            ),
+        )(log_decay, level_class.reshape(tokens, 1), table, state_in, state_out)
+        spread = spread_heads()
+        factor = jnp.broadcast_to((position % 2).astype(BF16), (EXTRA, wide))
+        factor = jnp.where(jnp.arange(wide)[None, :] < head_count, factor, 0)
+        offset = jnp.zeros((1, wide), F32)
+        states, factors = [], [factor]
+        for bit in range(ctx_bits - 1):
+            states.append(swap(sent, "ctx", 2**bit))
+            running, total, offset, factor, sent = merge_step(
+                bit, running, total, offset, states[-1], spread
+            )
+            factors.append(factor)
+        return states, factors, sent, tables, spread
+
+    def value_columns(values, r, first, count):
+        return lax.dynamic_slice(values, (first, (me ^ r) * features), (count, features))
+
+    early_rows = rows_dev // 2
+
+    def state_chain(values, log_decay, level_class, level_table, state_in, state_out):
+        fade, total = kernel_call(
+            fade_kernel,
+            "fade",
+            (shape((heads_size, rows_dev, wide)), shape((1, wide), F32)),
+            in_specs=[smem, vmem],
+        )(me1, log_decay)
+        near_fades, side_fades = [fade[0]], [fade[1]]
+        for d in range(2, heads_size, 2):
+            got = swap(tie(fade[d : d + 2], near_fades[-1]), "head", d)
+            near_fades.append(got[0])
+            side_fades.append(got[1])
+        sides = swap(jnp.stack(side_fades), "head", 1)
+        fades = []
+        for d in range(half):
+            fades += [near_fades[d], sides[d]]
+        in_turned = lax.dynamic_slice_in_dim(state_in, me * rows_dev, rows_dev, 0).T
+        across = jnp.stack([value_columns(values, d + 1, 0, rows_dev) for d in range(0, heads_size, 2)])
+        across = swap(across, "head", 1)
+        value_head = swap(tie(value_columns(values, 2, 0, early_rows), across), "head", 2)
+        keep, send = kernel_call(
+            partial_state_kernel,
+            "partial_states",
+            (shape((half, state_size, features), F32), shape((half, state_size, features))),
+            grid_spec=pltpu.PrefetchScalarGridSpec(
+                num_scalar_prefetch=1,
+                grid=(half,),
+                in_specs=[
+                    pl.BlockSpec((rows_dev, features), lambda i, m: (0, m[0] ^ (2 * i))),
+                    pl.BlockSpec((rows_dev, features), lambda i, m: (0, m[0] ^ (2 * i + 1))),
+                ]
+                + [whole((rows_dev, wide))] * heads_size
+                + [whole((state_size, rows_dev)), whole((wide, features))],
+                out_specs=[
+                    pl.BlockSpec((1, state_size, features), lambda i, m: (i, 0, 0)),
+                    pl.BlockSpec((1, state_size, features), lambda i, m: (i, 0, 0)),
+                ],
+            ),
+        )(me1, values, values, *fades, in_turned, spread_heads())
+        own_state, *far_states = kernel_call(
+            fold_kernel,
+            "fold",
+            tuple(
+                [shape((state_size, features), F32)] + [shape((state_size, features))] * (half - 1)
+            ),
+        )(keep, swap(tie(send, across), "head", 1))
+        got_states = []
+        for i, far in enumerate(far_states):
+            got_states.append(swap(tie(far, value_head, *got_states), "head", 2 * (i + 1)))
+        running, sent = kernel_call(
+            first_kernel,
+            "first_state",
+            (shape((state_size, features), F32), shape((state_size + EXTRA, features))),
+        )(own_state, total, *got_states)
+        others = []
+        for d in range(2, heads_size, 2):
+            first = early_rows if d == 2 else 0
+            own = value_columns(values, d, first, rows_dev - first)
+            both = jnp.concatenate([own, across[d // 2]], axis=0)
+            others.append(swap(tie(both, running, *others), "head", d))
+        states, factors, sent, tables, spread = fenced(
+            near_steps, running, total, sent, log_decay, level_class, level_table, state_in, state_out
+        )
+        return states, factors, sent, tables, spread, across[0], value_head, others
+
+    states, factors, sent, tables, spread, beside, value_head, other_values = fenced(
+        state_chain, values, log_decay, level_class, level_table, state_in, state_out
     )
-
-    running, sent = kernel_call(
-        first_kernel,
-        "first_state",
-        (shape((state_size, features), F32), shape((state_size + EXTRA, features))),
-    )(own_state, total, *got_states)
-    late = {r: value_swap(r, got_states[-1]) for r in range(1, heads_size) if r not in early}
-    offset = jnp.zeros((1, wide), F32)
-    factors = [jnp.broadcast_to((position % 2).astype(BF16), (EXTRA, wide))]
-    factors[0] = jnp.where(jnp.arange(wide)[None, :] < head_count, factors[0], 0)
-    states = []
-    for bit in range(ctx_bits):
-        if bit == 0:
-            sent = tie(sent, held[1], held[2])
-        if bit == ctx_bits - 1:
-            sent = tie(sent, *late.values())
-        states.append(swap(sent, "ctx", 2**bit))
-        if bit + 1 < ctx_bits:
-            running, total, offset, factor, sent = kernel_call(
-                functools.partial(merge_kernel, bit),
-                "merge",
-                (
-                    shape((state_size, features), F32),
-                    shape((1, wide), F32),
-                    shape((1, wide), F32),
-                    shape((EXTRA, wide)),
-                    shape((state_size + EXTRA, features)),
-                ),
-                in_specs=[smem] + [vmem] * 5,
-            )(place1, running, total, offset, states[-1], spread)
-            factors.append(factor)
+    lift, read, cross, merge, scores, masked = tables
+    states = list(states)
+    sent = tie(sent, *[held[2**bit] for bit in range(ctx_bits)])
+    states.append(swap(sent, "ctx", 2 ** (ctx_bits - 1)))
 
     columns = out_weight.shape[1]
     near = ctx_bits - 1
     for r in range(2, ctx_size):
         low = r & -r
         if r not in held and low > 1:
-            held[r] = swap(tie(held[r ^ low], states[min(low.bit_length() - 1, near - 1)]), "ctx", low)
+            held[r] = swap(tie(held[r ^ low], states[near - 1]), "ctx", low)
     for bit in range(1, ctx_bits):
         r = 2**bit
-        held[r + 1] = swap(tie(held[r], states[min(bit - 1, near - 1)]), "ctx", 1)
+        held[r + 1] = swap(tie(held[r], states[near - 1]), "ctx", 1)
+    same = (
+        (jnp.arange(tile)[:, None] // head_width == jnp.arange(tile)[None, :] // head_width)
+        / head_width
+    ).astype(BF16)
+
+    arrays = [values, beside, value_head] + list(other_values)
+    parts = [[(0, 0, rows_dev)], [(1, 0, rows_dev)]]
+    for i in range(half - 1):
+        if i == 0:
+            mine = [(2, 0, early_rows), (3, 0, rows_dev - early_rows)]
+        else:
+            mine = [(3 + i, 0, rows_dev)]
+        parts += [mine, [(3 + i, mine[-1][2], rows_dev)]]
 
     skip_row = jnp.repeat(skip_gain, head_width)[None, :]
     grouped = (heads_size, rows_dev)
     pre = kernel_call(
-        lambda me_ref, *refs: local_kernel(me_ref, near, heads_size, *refs),
+        lambda me_ref, *refs: local_kernel(me_ref, near, parts, *refs),
         "local_levels",
         shape((heads_size, rows_dev, features), F32),
         grid_spec=pltpu.PrefetchScalarGridSpec(
             num_scalar_prefetch=1,
             grid=(tiles,),
             in_specs=[pl.BlockSpec((rows_dev, tile), lambda f, m: (0, m[0] * tiles + f))]
-            + [pl.BlockSpec((rows_dev, tile), lambda f, m: (0, f))] * (heads_size - 1)
+            + [
+                pl.BlockSpec((array.shape[0], tile), lambda f, m: (0, f)) for array in arrays[1:]
+            ]
             + [
                 whole(grouped + (state_size,)),
                 whole(grouped + (wide,)),
@@ -546,8 +578,7 @@
         ),
     )(
         me1,
-        values,
-        *[early[r] if r in early else late[r] for r in range(1, heads_size)],
+        *arrays,
         state_out.reshape(grouped + (state_size,)),
         lift.reshape(grouped + (wide,)),
         read.reshape((local + 1,) + grouped + (wide,)),
@@ -561,10 +592,10 @@
         *states[:near],
     )
 
-    kept, *sends = kernel_call(
+    normed = kernel_call(
         finish_kernel,
         "finish",
-        tuple([shape((half, rows_dev, features))] + [shape((rows_dev, features))] * half),
+        tuple([shape((rows_dev, features))] * heads_size),
         grid_spec=pltpu.PrefetchScalarGridSpec(
             num_scalar_prefetch=1,
             grid=(tiles,),
@@ -578,48 +609,62 @@
                 whole((tile, tile)),
                 pl.BlockSpec((1, tile), lambda f, m: (0, f)),
             ],
-            out_specs=[pl.BlockSpec((half, rows_dev, tile), lambda f, m: (0, 0, f))]
-            + [pl.BlockSpec((rows_dev, tile), lambda f, m: (0, f))] * half,
+            out_specs=[pl.BlockSpec((rows_dev, tile), lambda f, m: (0, f))] * heads_size,
         ),
     )(
         me1,
         pre,
         state_out.reshape(grouped + (state_size,)),
         cross[-1].reshape(grouped + (wide,)),
-        tie(factors[-1], *[held[r] for r in range(2, ctx_size // 2 + 1) if r in held]),
+        factors[-1],
         states[-1],
         spread,
         same,
         norm_gain[None, :],
     )
-    others = [swap(array, "head", 1) for array in sends]
+    kept = normed[0::2]
+    others = [swap(array, "head", 1) for array in normed[1::2]]
 
     count = 1
     while count * columns % 128 and 2 * count <= ctx_size:
         count *= 2
-    partners = {r: swap(held[r], "head", 1) for r in range(count)}
-    pieces = []
+    def project(name, kept, others, blocks, partners, kind):
+        return kernel_call(
+            project_kernel,
+            name,
+            shape((len(kept), rows_dev, count * columns), kind),
+            in_specs=[smem] + [vmem] * (2 * len(kept) + 2 * count),
+        )(place1, *kept, *others, *blocks, *partners)
+
+    def far_part(kept, others, blocks):
+        partners = [swap(block, "head", 1) for block in blocks]
+        return project("project_far", kept, others, blocks, partners, BF16), partners
+
+    fars, arrived, owns = [], [], []
     for first in range(0, ctx_size, count):
         group = range(first, first + count)
         for r in group:
             if r not in held:
                 side = (r ^ 1) & -(r ^ 1)
-                top = lax.slice_in_dim(tie(held[r ^ 1], pieces[0]), 0, columns // 2, axis=0)
-                rest = lax.slice_in_dim(tie(held[r ^ side], pieces[0]), columns // 2, columns, axis=0)
+                ready = arrived[max(len(fars) - 3, 0)] + fars[max(len(fars) - 2, 0) :][:1]
+                top = lax.slice_in_dim(tie(held[r ^ 1], *ready), 0, columns // 2, axis=0)
+                rest = lax.slice_in_dim(tie(held[r ^ side], *ready), columns // 2, columns, axis=0)
                 held[r] = jnp.concatenate([swap(top, "ctx", 1), swap(rest, "ctx", side)], axis=0)
-            if r not in partners:
-                partners[r] = swap(tie(held[r], pieces[0]), "head", 1)
-        far, own = kernel_call(
-            project_kernel,
-            "project",
-            (
-                shape((half - 1, rows_dev, count * columns)),
-                shape((rows_dev, count * columns), F32),
-            ),
-            in_specs=[smem] + [vmem] * (1 + half + 2 * count),
-        )(place1, kept, *others, *[held[r] for r in group], *[partners[r] for r in group])
-        pieces.append(own)
-        pieces += [swap(far[i - 1], "head", 2 * i) for i in range(1, half)]
+        blocks = [held[r] for r in group]
+        if first == 0:
+            far, partners = far_part(kept[1:], others[1:], blocks)
+        else:
+            if len(owns) >= 3:
+                blocks[0] = tie(blocks[0], *owns[:-1])
+            far, partners = fenced(far_part, kept[1:], others[1:], blocks)
+        fars.append(far)
+        if len(arrived) >= 1:
+            far = tie(far, *arrived[-1])
+        arrived.append([swap(far[i - 1], "head", 2 * i) for i in range(1, half)])
+        owns.append(project("project_own", kept[:1], others[:1], blocks, partners, F32))
+    pieces = []
+    for own, got in zip(owns, arrived):
+        pieces += [own[0]] + got
     return kernel_call(
         assemble_kernel,
         "assemble",

time: 194 us -> 165 us (0.85)
  waiting for transfers between devices: 88.6 us -> 40.1 us
  Pallas kernels: 50.4 us -> 72 us
  starting transfers between devices: 30.4 us -> 26.3 us
  local copies, waits for them, and re-layouts: 19.9 us -> 22.4 us
    ppermute x33 -> x32, waiting for transfers between devices: 88.6 us -> 40.1 us  [swap(): return lax.ppermute(value, axis, pairs)]
    pallas_call x13 -> x17, Pallas kernels: 49.1 us -> 69.8 us  [the longest x8 28.2 us: project(): kernel_call(project_kernel, name, shape((len(kept), rows_dev, count * col...]
    unnamed x58 -> x27, local copies, waits for them, and re-layouts: 12 us -> 3.27 us
    ppermute x33 -> x32, starting transfers between devices: 30.4 us -> 26.3 us  [swap(): return lax.ppermute(value, axis, pairs)]
    another operation x0 -> x6, local copies, waits for them, and re-layouts: none -> 3.95 us
    cond x0 -> x17, local copies, waits for them, and re-layouts: none -> 3.14 us
    dynamic_slice x2 -> x1, local copies, waits for them, and re-layouts: 3.85 us -> 1.12 us  [value_columns(): lax.dynamic_slice(values, (first, (me ^ r) * features), (count, features))]
    slice x2 -> x4, local copies, waits for them, and re-layouts: 1.06 us -> 3.6 us  [the longest x1 1.79 us: on_device(): top = lax.slice_in_dim(tie(held[r ^ 1], *ready), 0, columns // 2, axis=0)]
  transfers between devices with their start and end apart: 33 -> 32, of which waited for: 13 -> 14; matrix products, arithmetic and copies ran while one was open for 7% -> 14% of each run, Pallas kernels for 24% -> 42%
where the time goes in v3:
time: 165 us
  Pallas kernels  72 us (44%)
  waiting for transfers between devices  40.1 us (24%)
  starting transfers between devices  26.3 us (16%)
  local copies, waits for them, and re-layouts  22.4 us (14%)
  other arithmetic  3.28 us (2%)
    ppermute x32, waiting for transfers between devices, swap(): return lax.ppermute(value, axis, pairs)  40.1 us
    pallas_call x8, Pallas kernels, project(): kernel_call(project_kernel, name, shape((len(kept), rows_dev, count * col...  28.2 us
    ppermute x32, starting transfers between devices, swap(): return lax.ppermute(value, axis, pairs)  26.3 us
    pallas_call x1, Pallas kernels, on_device(): kernel_call(lambda me_ref, *refs: local_kernel(me_ref, near, parts, *refs...  20.6 us
    pallas_call x1, Pallas kernels, on_device(): kernel_call(finish_kernel, 'finish', tuple([shape((rows_dev, features))]...  6.57 us
    pallas_call x1, Pallas kernels, near_steps(): kernel_call(factors_kernel, 'factors', (shape((tokens, wide)), shape((loc...  4.62 us
    pallas_call x2, Pallas kernels, merge_step(): kernel_call(functools.partial(merge_kernel, bit), 'merge', (shape((state_...  4.04 us
    pallas_call x1, Pallas kernels, state_chain(): kernel_call(partial_state_kernel, 'partial_states', (shape((half, state_s...  3.74 us
  transfers between devices with their start and end apart: 32, of which 14 were waited for; matrix products, arithmetic and copies ran while one was open for 14% of the time, Pallas kernels for 42%

profile of v3, /device:TPU:0, one launch (start us, length us, event | category | flops | bytes accessed | tf_op | source)
XLA Modules:
  0.0 164.7 jit_solution(14455113859632021394)
XLA Ops:
  0.0 2.9 %collective-permute-start.15 = (bf16[320,1280]{1,0:T(8,128)(2,1)}, bf16[320,1280]{1,0:T(8,128)(2,1)S(1)}, u32[]{:S(2)}, u32[]{:S(2)}) collective-permute-start(bf16[320,1280]{1,0:T(8,128)(2,1)} %bitcast.36), channel_id=1, source_target_pairs={{0,4},{4,0},{8,12},{12,8},{16,20},{20,16},{24,28},{28,24},{1,5},{5... | collective-permute-start | bytes 2457608 | tf_op jit(solution)/shard_map/ppermute | solution.py:32
  4.5 2.6 %collective-permute-start.17 = (bf16[320,1280]{1,0:T(8,128)(2,1)}, bf16[320,1280]{1,0:T(8,128)(2,1)}, u32[]{:S(2)}, u32[]{:S(2)}) collective-permute-start(bf16[320,1280]{1,0:T(8,128)(2,1)} %bitcast.38), channel_id=1, source_target_pairs={{0,16},{4,20},{8,24},{12,28},{16,0},{20,4},{24,8},{28,12},{1,17},{... | collective-permute-start | bytes 2457608 | tf_op jit(solution)/shard_map/ppermute | solution.py:32
  7.1 59.7 %conditional.5 = (bf16[144,1280]{1,0:T(8,128)(2,1)}, bf16[144,1280]{1,0:T(8,128)(2,1)}, bf16[16,40]{1,0:T(8,128)(2,1)}, bf16[16,40]{1,0:T(8,128)(2,1)}, bf16[16,...) conditional(s32[]{:T(128)} %convert_element_type.28, () %tuple.69, ...), branch_computations={%region_0.0_spmd, %region_1.4_spmd} | conditional | flops 2878033 | bytes 39677388 | solution.py:390
  16.5 3.7 %partial_states.1 = (f32[2,128,1280]{2,1,0:T(8,128)S(1)}, bf16[2,128,1280]{2,1,0:T(8,128)(2,1)}) custom-call(s32[1]{0:T(128)} %get-tuple-element.105.me_ref, bf16[256,5120]{1,0:T(8,128)(2,1)} %get-tuple-element.106.refs_0_.refs_1_, bf16[256,5120]{1,0:T(8,128)(2,1)} %get-tuple-element.106.refs_0_.refs_1_, bf16[256,40]{1,0:T(8,128)(2,1)S(1)} %get-tuple-element.331.refs_2_, ...), custom_call_target="tpu_custom_call" | custom-call | tf_op jit(solution)/shard_map/cond/branch_1_fun/partial_states/pallas_call | solution.py:470
  23.9 7.7 %collective-permute-done.12 = bf16[128,1280]{1,0:T(8,128)(2,1)} collective-permute-done((bf16[128,1280]{1,0:T(8,128)(2,1)S(1)}, bf16[128,1280]{1,0:T(8,128)(2,1)}, u32[]{:S(2)}, u32[]{:S(2)}) %collective-permute-start.12) | collective-permute-done | bytes 327712 | tf_op jit(solution)/shard_map/cond/branch_1_fun/ppermute | solution.py:32
  35.6 5.3 %collective-permute-done.13.refs_0_ = bf16[128,1280]{1,0:T(8,128)(2,1)S(1)} collective-permute-done((bf16[128,1280]{1,0:T(8,128)(2,1)S(1)}, bf16[128,1280]{1,0:T(8,128)(2,1)S(1)}, u32[]{:S(2)}, u32[]{:S(2)}) %collective-permute-start.13) | collective-permute-done | bytes 327712 | tf_op jit(solution)/shard_map/cond/branch_1_fun/ppermute | solution.py:32
  41.7 25.2 %conditional = (bf16[144,1280]{1,0:T(8,128)(2,1)}, bf16[144,1280]{1,0:T(8,128)(2,1)}, bf16[16,40]{1,0:T(8,128)(2,1)}, bf16[16,40]{1,0:T(8,128)(2,1)}, bf16[16,40...) conditional(s32[]{:T(128)} %convert_element_type.24, () %tuple.38, ...), branch_computations={%region_2.2_spmd, %region_3.3_spmd} | conditional | flops 123212 | bytes 9597177 | solution.py:390
  43.0 7.8 %collective-permute-done.6.got_ref = bf16[144,1280]{1,0:T(8,128)(2,1)} collective-permute-done((bf16[144,1280]{1,0:T(8,128)(2,1)S(1)}, bf16[144,1280]{1,0:T(8,128)(2,1)}, u32[]{:S(2)}, u32[]{:S(2)}) %collective-permute-start.6) | collective-permute-done | bytes 368672 | tf_op jit(solution)/shard_map/cond/branch_1_fun/cond/branch_1_fun/ppermute | solution.py:32
  55.5 4.6 %factors.1 = (bf16[1024,40]{1,0:T(8,128)(2,1)}, bf16[5,1024,40]{2,1,0:T(8,128)(2,1)}, bf16[3,1024,40]{2,1,0:T(8,128)(2,1)}, bf16[32,40]{1,0:T(8,128)(2,1)}, bf16...) custom-call(f32[1024,20]{1,0:T(8,128)S(1)} %get-tuple-element.93.decay_ref, s32[1024,1]{1,0:T(8,128)S(1)} %copy.31.class_ref, ...), custom_call_target="tpu_custom_call" | custom-call | tf_op jit(solution)/shard_map/cond/branch_1_fun/cond/branch_1_fun/factors/pallas_call | solution.py:420
  68.8 20.6 %local_levels.1.pre_ref = f32[4,256,1280]{2,1,0:T(8,128)S(1)} custom-call(s32[1]{0:T(128)} %bitcast.16.me_ref, bf16[256,5120]{1,0:T(8,128)(2,1)} %refs_0_.1, bf16[256,1280]{1,0:T(8,128)(2,1)} %get-tuple-element.194.refs_1_, bf16[128,1280]{1,0:T(8,128)(2,1)} %get-tuple-element.195.refs_2_, bf16[384,1280]{1,0:T(8,128)(2,1)} %get-tuple-element.196.refs_3_, ...), custom_call_target="tpu_custom_call" | custom-call | tf_op jit(solution)/shard_map/local_levels/pallas_call | solution.py:548
  89.4 6.6 %finish.1 = (bf16[256,1280]{1,0:T(8,128)(2,1)S(1)}, bf16[256,1280]{1,0:T(8,128)(2,1)S(1)}, bf16[256,1280]{1,0:T(8,128)(2,1)S(1)}, bf16[256,1280]{1,0:T(8,128)(2,1)S(1)}) custom-call(s32[1]{0:T(128)} %bitcast.16.me_ref, f32[4,256,1280]{2,1,0:T(8,128)S(1)} %local_levels.1.pre_ref, bf16[4,256,128]{2,1,0:T(8,128)(2,1)S(1)} %bitcast.48, ...), custom_call_target="tpu_custom_call" | custom-call | tf_op jit(solution)/shard_map/finish/pallas_call | solution.py:595
  99.7 3.2 %project_far.7 = bf16[1,256,640]{2,1,0:T(8,128)(2,1)S(1)} custom-call(s32[1]{0:T(128)} %bitcast.15.place_ref, bf16[256,1280]{1,0:T(8,128)(2,1)S(1)} %get-tuple-element.214.refs_0_, bf16[256,1280]{1,0:T(8,128)(2,1)S(1)} %collective-permute-done.22.refs_1_, bf16[320,1280]{1,0:T(8,128)(2,1)S(1)} %bitcast.40, ...), custom_call_target="tpu_custom_call" | custom-call | tf_op jit(solution)/shard_map/project_far/pallas_call | solution.py:632
  104.4 7.4 %conditional.6 = (bf16[1,256,640]{2,1,0:T(8,128)(2,1)S(1)}, bf16[320,1280]{1,0:T(8,128)(2,1)}, bf16[320,1280]{1,0:T(8,128)(2,1)}) conditional(s32[]{:T(128)} %convert_element_type.28, () %tuple.73, (bf16[320,1280]{1,0:T(8,128)(2,1)}, bf16[320,1280]{1,0:T(8,128)(2,1)}, s32[1]{0:T(128)}, bf16[256,1280]{1,0:T(8,128)(2,1)S(1)}, ...), branch_computations={%region_4.5_spmd, %region_5.6_spmd} | conditional | bytes 6553704 | solution.py:390
  108.3 3.5 %project_far.4 = bf16[1,256,640]{2,1,0:T(8,128)(2,1)S(1)} custom-call(s32[1]{0:T(128)} %get-tuple-element.140.place_ref, bf16[256,1280]{1,0:T(8,128)(2,1)S(1)} %get-tuple-element.141.refs_0_, bf16[256,1280]{1,0:T(8,128)(2,1)S(1)} %get-tuple-element.142.refs_1_, bf16[320,1280]{1,0:T(8,128)(2,1)} %get-tuple-element.143.refs_2_, ...), custom_call_target="tpu_custom_call" | custom-call | tf_op jit(solution)/shard_map/cond/branch_1_fun/project_far/pallas_call | solution.py:632
  112.6 4.5 %collective-permute-done.28.refs_2_ = bf16[320,1280]{1,0:T(8,128)(2,1)} collective-permute-done((bf16[320,1280]{1,0:T(8,128)(2,1)}, bf16[320,1280]{1,0:T(8,128)(2,1)}, u32[]{:S(2)}, u32[]{:S(2)}) %collective-permute-start.28) | collective-permute-done | bytes 819232 | tf_op jit(solution)/shard_map/ppermute | solution.py:32
  125.2 3.0 %project_own.4 = f32[1,256,640]{2,1,0:T(8,128)S(1)} custom-call(s32[1]{0:T(128)} %bitcast.15.place_ref, bf16[256,1280]{1,0:T(8,128)(2,1)S(1)} %get-tuple-element.212.refs_0_, bf16[256,1280]{1,0:T(8,128)(2,1)S(1)} %collective-permute-done.19.refs_1_, bf16[320,1280]{1,0:T(8,128)(2,1)S(1)} %bitcast.41, bf16[320,1280]{1,0:T(8,128)(2,1)S(1)} %collective-permute-done.15.refs_3_, ...), custom_call_target="tpu_custom_call" | custom-call | tf_op jit(solution)/shard_map/project_own/pallas_call | solution.py:632
  128.2 3.7 %project_own.5 = f32[1,256,640]{2,1,0:T(8,128)S(1)} custom-call(s32[1]{0:T(128)} %bitcast.15.place_ref, bf16[256,1280]{1,0:T(8,128)(2,1)S(1)} %get-tuple-element.212.refs_0_, bf16[256,1280]{1,0:T(8,128)(2,1)S(1)} %collective-permute-done.19.refs_1_, bf16[320,1280]{1,0:T(8,128)(2,1)} %collective-permute-done.16.refs_2_, ...), custom_call_target="tpu_custom_call" | custom-call | tf_op jit(solution)/shard_map/project_own/pallas_call | solution.py:632
  132.0 7.4 %conditional.7 = (bf16[1,256,640]{2,1,0:T(8,128)(2,1)S(1)}, bf16[320,1280]{1,0:T(8,128)(2,1)}, bf16[320,1280]{1,0:T(8,128)(2,1)}) conditional(s32[]{:T(128)} %convert_element_type.28, () %tuple.77, (bf16[320,1280]{1,0:T(8,128)(2,1)}, bf16[320,1280]{1,0:T(8,128)(2,1)}, s32[1]{0:T(128)}, bf16[256,1280]{1,0:T(8,128)(2,1)S(1)}, ...), branch_computations={%region_6.7_spmd, %region_7.8_spmd} | conditional | bytes 6553704 | solution.py:390
  135.9 3.5 %project_far.5 = bf16[1,256,640]{2,1,0:T(8,128)(2,1)S(1)} custom-call(s32[1]{0:T(128)} %get-tuple-element.145.place_ref, bf16[256,1280]{1,0:T(8,128)(2,1)S(1)} %get-tuple-element.146.refs_0_, bf16[256,1280]{1,0:T(8,128)(2,1)S(1)} %get-tuple-element.147.refs_1_, bf16[320,1280]{1,0:T(8,128)(2,1)} %get-tuple-element.148.refs_2_, ...), custom_call_target="tpu_custom_call" | custom-call | tf_op jit(solution)/shard_map/cond/branch_1_fun/project_far/pallas_call | solution.py:632
  144.4 8.1 %conditional.8 = (bf16[1,256,640]{2,1,0:T(8,128)(2,1)}, bf16[320,1280]{1,0:T(8,128)(2,1)}, bf16[320,1280]{1,0:T(8,128)(2,1)}) conditional(s32[]{:T(128)} %convert_element_type.28, () %tuple.83, (bf16[320,1280]{1,0:T(8,128)(2,1)}, bf16[320,1280]{1,0:T(8,128)(2,1)}, s32[1]{0:T(128)}, bf16[256,1280]{1,0:T(8,128)(2,1)S(1)}, ...), branch_computations={%region_8.9_spmd, %region_9.10_spmd} | conditional | bytes 6553704 | solution.py:390
  148.2 4.2 %project_far.6 = bf16[1,256,640]{2,1,0:T(8,128)(2,1)} custom-call(s32[1]{0:T(128)} %get-tuple-element.150.place_ref, bf16[256,1280]{1,0:T(8,128)(2,1)S(1)} %get-tuple-element.151.refs_0_, bf16[256,1280]{1,0:T(8,128)(2,1)S(1)} %get-tuple-element.152.refs_1_, bf16[320,1280]{1,0:T(8,128)(2,1)} %get-tuple-element.153.refs_2_, ...), custom_call_target="tpu_custom_call" | custom-call | tf_op jit(solution)/shard_map/cond/branch_1_fun/project_far/pallas_call | solution.py:632
  153.8 3.5 %project_own.6 = f32[1,256,640]{2,1,0:T(8,128)S(1)} custom-call(s32[1]{0:T(128)} %bitcast.15.place_ref, bf16[256,1280]{1,0:T(8,128)(2,1)S(1)} %get-tuple-element.212.refs_0_, bf16[256,1280]{1,0:T(8,128)(2,1)S(1)} %collective-permute-done.19.refs_1_, bf16[320,1280]{1,0:T(8,128)(2,1)} %collective-permute-done.17.refs_2_, ...), custom_call_target="tpu_custom_call" | custom-call | tf_op jit(solution)/shard_map/project_own/pallas_call | solution.py:632
  157.3 3.6 %project_own.7 = f32[1,256,640]{2,1,0:T(8,128)S(1)} custom-call(s32[1]{0:T(128)} %bitcast.15.place_ref, bf16[256,1280]{1,0:T(8,128)(2,1)S(1)} %get-tuple-element.212.refs_0_, bf16[256,1280]{1,0:T(8,128)(2,1)S(1)} %collective-permute-done.19.refs_1_, bf16[320,1280]{1,0:T(8,128)(2,1)} %collective-permute-done.28.refs_2_, ...), custom_call_target="tpu_custom_call" | custom-call | tf_op jit(solution)/shard_map/project_own/pallas_call | solution.py:632
  162.4 2.3 %assemble.1 = bf16[256,2560]{1,0:T(8,128)(2,1)} custom-call(s32[1]{0:T(128)S(6)} %select_n.92.place_ref, f32[256,640]{1,0:T(8,128)S(1)} %bitcast.42, bf16[256,640]{1,0:T(8,128)(2,1)} %collective-permute-done.23.refs_1_, f32[256,640]{1,0:T(8,128)S(1)} %bitcast.43, bf16[256,640]{1,0:T(8,128)(2,1)S(1)} %collective-permute-done.25.refs_3_, ...), custom_call_target="tpu_custom_call" | custom-call | tf_op jit(solution)/shard_map/assemble/pallas_call | solution.py:668
  (142 shorter events, 67.3 us)
Async XLA Ops:
  0.0 66.9 %collective-permute-start.15 = (bf16[320,1280]{1,0:T(8,128)(2,1)}, bf16[320,1280]{1,0:T(8,128)(2,1)S(1)}, u32[]{:S(2)}, u32[]{:S(2)}) collective-permute-start(bf16[320,1280]{1,0:T(8,128)(2,1)} %bitcast.36), channel_id=1, source_target_pairs={{0,4},{4,0},{8,12},{12,8},{16,20},{20,16},{24,28},{28,24},{1,5},{5... | collective-permute-start | bytes 2457608 | tf_op jit(solution)/shard_map/ppermute | solution.py:32
  2.9 63.9 %collective-permute-start.16 = (bf16[320,1280]{1,0:T(8,128)(2,1)}, bf16[320,1280]{1,0:T(8,128)(2,1)}, u32[]{:S(2)}, u32[]{:S(2)}) collective-permute-start(bf16[320,1280]{1,0:T(8,128)(2,1)} %bitcast.37), channel_id=1, source_target_pairs={{0,8},{4,12},{8,0},{12,4},{16,24},{20,28},{24,16},{28,20},{1,9},{5... | collective-permute-start | bytes 2457608 | tf_op jit(solution)/shard_map/ppermute | solution.py:32
  4.5 62.4 %collective-permute-start.17 = (bf16[320,1280]{1,0:T(8,128)(2,1)}, bf16[320,1280]{1,0:T(8,128)(2,1)}, u32[]{:S(2)}, u32[]{:S(2)}) collective-permute-start(bf16[320,1280]{1,0:T(8,128)(2,1)} %bitcast.38), channel_id=1, source_target_pairs={{0,16},{4,20},{8,24},{12,28},{16,0},{20,4},{24,8},{28,12},{1,17},{... | collective-permute-start | bytes 2457608 | tf_op jit(solution)/shard_map/ppermute | solution.py:32
  9.1 5.0 %collective-permute-start.8 = (bf16[2,256,40]{2,1,0:T(8,128)(2,1)S(1)}, bf16[2,256,40]{2,1,0:T(8,128)(2,1)S(1)}, u32[]{:S(2)}, u32[]{:S(2)}) collective-permute-start(bf16[2,256,40]{2,1,0:T(8,128)(2,1)S(1)} %slice.28), channel_id=1, source_target_pairs={{0,2},{1,3},{2,0},{3,1},{4,6},{5,7},{6,4},{7,5},{8,10},{9,11},{10,... | collective-permute-start | bytes 122888 | tf_op jit(solution)/shard_map/cond/branch_1_fun/ppermute | solution.py:32
  13.3 7.0 %collective-permute-start.10 = (bf16[2,256,1280]{2,1,0:T(8,128)(2,1)}, bf16[2,256,1280]{2,1,0:T(8,128)(2,1)}, u32[]{:S(2)}, u32[]{:S(2)}) collective-permute-start(bf16[2,256,1280]{2,1,0:T(8,128)(2,1)} %pad_maximum_fusion.1), channel_id=1, source_target_pairs={{0,1},{1,0},{2,3},{3,2},{4,5},{5,4},{6,7},{7,6},{8,9},{9,8},{10,11... | collective-permute-start | bytes 3932168 | tf_op jit(solution)/shard_map/cond/branch_1_fun/ppermute | solution.py:32
  21.5 10.2 %collective-permute-start.12 = (bf16[128,1280]{1,0:T(8,128)(2,1)S(1)}, bf16[128,1280]{1,0:T(8,128)(2,1)}, u32[]{:S(2)}, u32[]{:S(2)}) collective-permute-start(bf16[128,1280]{1,0:T(8,128)(2,1)S(1)} %get-tuple-element.118), channel_id=1, source_target_pairs={{0,2},{1,3},{2,0},{3,1},{4,6},{5,7},{6,4},{7,5},{8,10},{9,11},{10,... | collective-permute-start | bytes 983048 | tf_op jit(solution)/shard_map/cond/branch_1_fun/ppermute | solution.py:32
  31.7 9.2 %collective-permute-start.13 = (bf16[128,1280]{1,0:T(8,128)(2,1)S(1)}, bf16[128,1280]{1,0:T(8,128)(2,1)S(1)}, u32[]{:S(2)}, u32[]{:S(2)}) collective-permute-start(bf16[128,1280]{1,0:T(8,128)(2,1)S(1)} %get-tuple-element.119), channel_id=1, source_target_pairs={{0,2},{1,3},{2,0},{3,1},{4,6},{5,7},{6,4},{7,5},{8,10},{9,11},{10,... | collective-permute-start | bytes 983048 | tf_op jit(solution)/shard_map/cond/branch_1_fun/ppermute | solution.py:32
  41.0 25.9 %collective-permute-start.14 = (bf16[384,1280]{1,0:T(8,128)(2,1)}, bf16[384,1280]{1,0:T(8,128)(2,1)}, u32[]{:S(2)}, u32[]{:S(2)}) collective-permute-start(bf16[384,1280]{1,0:T(8,128)(2,1)} %pad_maximum_fusion.2), channel_id=1, source_target_pairs={{0,2},{1,3},{2,0},{3,1},{4,6},{5,7},{6,4},{7,5},{8,10},{9,11},{10,... | collective-permute-start | bytes 2949128 | tf_op jit(solution)/shard_map/cond/branch_1_fun/ppermute | solution.py:32
  41.7 9.1 %collective-permute-start.6 = (bf16[144,1280]{1,0:T(8,128)(2,1)S(1)}, bf16[144,1280]{1,0:T(8,128)(2,1)}, u32[]{:S(2)}, u32[]{:S(2)}) collective-permute-start(bf16[144,1280]{1,0:T(8,128)(2,1)S(1)} %get-tuple-element.81), channel_id=1, source_target_pairs={{0,4},{4,0},{8,12},{12,8},{16,20},{20,16},{24,28},{28,24},{1,5},{5... | collective-permute-start | bytes 1105928 | tf_op jit(solution)/shard_map/cond/branch_1_fun/cond/branch_1_fun/ppermute | solution.py:32
  53.5 10.6 %collective-permute-start.7 = (bf16[144,1280]{1,0:T(8,128)(2,1)S(1)}, bf16[144,1280]{1,0:T(8,128)(2,1)}, u32[]{:S(2)}, u32[]{:S(2)}) collective-permute-start(bf16[144,1280]{1,0:T(8,128)(2,1)S(1)} %get-tuple-element.85), channel_id=1, source_target_pairs={{0,8},{4,12},{8,0},{12,4},{16,24},{20,28},{24,16},{28,20},{1,9},{5... | collective-permute-start | bytes 1105928 | tf_op jit(solution)/shard_map/cond/branch_1_fun/cond/branch_1_fun/ppermute | solution.py:32
  66.9 31.3 %collective-permute-start.20 = (bf16[320,1280]{1,0:T(8,128)(2,1)S(1)}, bf16[320,1280]{1,0:T(8,128)(2,1)}, u32[]{:S(2)}, u32[]{:S(2)}) collective-permute-start(bf16[320,1280]{1,0:T(8,128)(2,1)S(1)} %bitcast.39), channel_id=1, source_target_pairs={{0,1},{1,0},{2,3},{3,2},{4,5},{5,4},{6,7},{7,6},{8,9},{9,8},{10,11... | collective-permute-start | bytes 2457608 | tf_op jit(solution)/shard_map/ppermute | solution.py:32
  66.9 22.5 %collective-permute-start.18 = (bf16[144,1280]{1,0:T(8,128)(2,1)}, bf16[144,1280]{1,0:T(8,128)(2,1)S(1)}, u32[]{:S(2)}, u32[]{:S(2)}) collective-permute-start(bf16[144,1280]{1,0:T(8,128)(2,1)} %get-tuple-element.211), channel_id=1, source_target_pairs={{0,16},{4,20},{8,24},{12,28},{16,0},{20,4},{24,8},{28,12},{1,17},{... | collective-permute-start | bytes 1105928 | tf_op jit(solution)/shard_map/ppermute | solution.py:32
  67.3 37.1 %collective-permute-start.24 = (bf16[320,1280]{1,0:T(8,128)(2,1)}, bf16[320,1280]{1,0:T(8,128)(2,1)}, u32[]{:S(2)}, u32[]{:S(2)}) collective-permute-start(bf16[320,1280]{1,0:T(8,128)(2,1)} %collective-permute-done.16.refs_2_), channel_id=1, source_target_pairs={{0,4},{4,0},{8,12},{12,8},{16,20},{20,16},{24,28},{28,24},{1,5},{5... | collective-permute-start | bytes 2457608 | tf_op jit(solution)/shard_map/ppermute | solution.py:32
  67.9 31.8 %collective-permute-start.21 = (bf16[320,1280]{1,0:T(8,128)(2,1)S(1)}, bf16[320,1280]{1,0:T(8,128)(2,1)}, u32[]{:S(2)}, u32[]{:S(2)}) collective-permute-start(bf16[320,1280]{1,0:T(8,128)(2,1)S(1)} %collective-permute-done.15.refs_3_), channel_id=1, source_target_pairs={{0,1},{1,0},{2,3},{3,2},{4,5},{5,4},{6,7},{7,6},{8,9},{9,8},{10,11... | collective-permute-start | bytes 2457608 | tf_op jit(solution)/shard_map/ppermute | solution.py:32
  96.6 20.5 %collective-permute-start.28 = (bf16[320,1280]{1,0:T(8,128)(2,1)}, bf16[320,1280]{1,0:T(8,128)(2,1)}, u32[]{:S(2)}, u32[]{:S(2)}) collective-permute-start(bf16[320,1280]{1,0:T(8,128)(2,1)} %collective-permute-done.17.refs_2_), channel_id=1, source_target_pairs={{0,8},{4,12},{8,0},{12,4},{16,24},{20,28},{24,16},{28,20},{1,9},{5... | collective-permute-start | bytes 2457608 | tf_op jit(solution)/shard_map/ppermute | solution.py:32
  98.2 23.6 %collective-permute-start.26 = (bf16[320,1280]{1,0:T(8,128)(2,1)}, bf16[320,1280]{1,0:T(8,128)(2,1)}, u32[]{:S(2)}, u32[]{:S(2)}) collective-permute-start(bf16[320,1280]{1,0:T(8,128)(2,1)} %collective-permute-done.17.refs_2_), channel_id=1, source_target_pairs={{0,4},{4,0},{8,12},{12,8},{16,20},{20,16},{24,28},{28,24},{1,5},{5... | collective-permute-start | bytes 2457608 | tf_op jit(solution)/shard_map/ppermute | solution.py:32
  102.9 14.2 %collective-permute-start.23 = (bf16[256,640]{1,0:T(8,128)(2,1)S(1)}, bf16[256,640]{1,0:T(8,128)(2,1)}, u32[]{:S(2)}, u32[]{:S(2)}) collective-permute-start(bf16[256,640]{1,0:T(8,128)(2,1)S(1)} %bitcast.46), channel_id=1, source_target_pairs={{0,2},{1,3},{2,0},{3,1},{4,6},{5,7},{6,4},{7,5},{8,10},{9,11},{10,... | collective-permute-start | bytes 983048 | tf_op jit(solution)/shard_map/ppermute | solution.py:32
  112.5 12.7 %collective-permute-start.19 = (bf16[256,1280]{1,0:T(8,128)(2,1)}, bf16[256,1280]{1,0:T(8,128)(2,1)S(1)}, u32[]{:S(2)}, u32[]{:S(2)}) collective-permute-start(bf16[256,1280]{1,0:T(8,128)(2,1)} %copy-done.5), channel_id=1, source_target_pairs={{0,1},{1,0},{2,3},{3,2},{4,5},{5,4},{6,7},{7,6},{8,9},{9,8},{10,11... | collective-permute-start | bytes 1966088 | tf_op jit(solution)/shard_map/ppermute | solution.py:32
  119.0 21.8 %collective-permute-start.29 = (bf16[160,1280]{1,0:T(8,128)(2,1)}, bf16[160,1280]{1,0:T(8,128)(2,1)}, u32[]{:S(2)}, u32[]{:S(2)}) collective-permute-start(bf16[160,1280]{1,0:T(8,128)(2,1)} %slice.38), channel_id=1, source_target_pairs={{0,4},{4,0},{8,12},{12,8},{16,20},{20,16},{24,28},{28,24},{1,5},{5... | collective-permute-start | bytes 1228808 | tf_op jit(solution)/shard_map/ppermute | solution.py:32
  120.4 19.0 %collective-permute-start.25 = (bf16[256,640]{1,0:T(8,128)(2,1)}, bf16[256,640]{1,0:T(8,128)(2,1)S(1)}, u32[]{:S(2)}, u32[]{:S(2)}) collective-permute-start(bf16[256,640]{1,0:T(8,128)(2,1)} %bitcast.50), channel_id=1, source_target_pairs={{0,2},{1,3},{2,0},{3,1},{4,6},{5,7},{6,4},{7,5},{8,10},{9,11},{10,... | collective-permute-start | bytes 983048 | tf_op jit(solution)/shard_map/ppermute | solution.py:32
  123.6 19.0 %collective-permute-start.30 = (bf16[160,1280]{1,0:T(8,128)(2,1)}, bf16[160,1280]{1,0:T(8,128)(2,1)}, u32[]{:S(2)}, u32[]{:S(2)}) collective-permute-start(bf16[160,1280]{1,0:T(8,128)(2,1)} %slice.39), channel_id=1, source_target_pairs={{0,8},{4,12},{8,0},{12,4},{16,24},{20,28},{24,16},{28,20},{1,9},{5... | collective-permute-start | bytes 1228808 | tf_op jit(solution)/shard_map/ppermute | solution.py:32
  140.1 12.3 %collective-permute-start.27 = (bf16[256,640]{1,0:T(8,128)(2,1)}, bf16[256,640]{1,0:T(8,128)(2,1)S(1)}, u32[]{:S(2)}, u32[]{:S(2)}) collective-permute-start(bf16[256,640]{1,0:T(8,128)(2,1)} %bitcast.51), channel_id=1, source_target_pairs={{0,2},{1,3},{2,0},{3,1},{4,6},{5,7},{6,4},{7,5},{8,10},{9,11},{10,... | collective-permute-start | bytes 983048 | tf_op jit(solution)/shard_map/ppermute | solution.py:32
  144.4 3.8 %collective-permute-start.5 = (bf16[320,1280]{1,0:T(8,128)(2,1)}, bf16[320,1280]{1,0:T(8,128)(2,1)}, u32[]{:S(2)}, u32[]{:S(2)}) collective-permute-start(bf16[320,1280]{1,0:T(8,128)(2,1)} %get-tuple-element.154.refs_3_), channel_id=1, source_target_pairs={{0,1},{1,0},{2,3},{3,2},{4,5},{5,4},{6,7},{7,6},{8,9},{9,8},{10,11... | collective-permute-start | bytes 2457608 | tf_op jit(solution)/shard_map/cond/branch_1_fun/ppermute | solution.py:32
  152.4 10.0 %collective-permute-start.31 = (bf16[256,640]{1,0:T(8,128)(2,1)}, bf16[256,640]{1,0:T(8,128)(2,1)S(1)}, u32[]{:S(2)}, u32[]{:S(2)}) collective-permute-start(bf16[256,640]{1,0:T(8,128)(2,1)} %bitcast.26), channel_id=1, source_target_pairs={{0,2},{1,3},{2,0},{3,1},{4,6},{5,7},{6,4},{7,5},{8,10},{9,11},{10,... | collective-permute-start | bytes 983048 | tf_op jit(solution)/shard_map/ppermute | solution.py:32
  (29 other events, 240.2 us)

commit v4 on v3

--- a/solution.py
+++ b/solution.py
@@ -289,7 +289,7 @@
     row = dot(factor_ref[...], spread)[0:1, :]
     for r in range(parts):
         at = me ^ r
-        total = pre_ref[at] + dot(cross_ref[at], spread) * (dot(out_ref[at], state) * row)
+        total = pre_ref[at] + dot(cross_ref[0, at], spread) * (dot(out_ref[at], state) * row)
         mean_square = dot((total * total).astype(BF16), same)
         normed = (total * lax.rsqrt(mean_square + EPSILON) * gain).astype(BF16)
         refs[r][...] = normed
@@ -389,32 +389,82 @@
         zeros = lambda *_: jax.tree.map(lambda leaf: jnp.zeros(leaf.shape, leaf.dtype), shapes)
         return lax.cond(position < ctx_size, body, zeros, *operands)
 
-    def spread_heads():
-        return (
-            jnp.arange(wide)[:, None] % head_count == (jnp.arange(features) // head_width)[None, :]
-        ).astype(BF16)
-
-    held = {0: out_weight.T}
+    columns = out_weight.shape[1]
+    near = ctx_bits - 1
+    grouped = (heads_size, rows_dev)
+    spread = (
+        jnp.arange(wide)[:, None] % head_count == (jnp.arange(features) // head_width)[None, :]
+    ).astype(BF16)
+    same = (
+        (jnp.arange(tile)[:, None] // head_width == jnp.arange(tile)[None, :] // head_width)
+        / head_width
+    ).astype(BF16)
+
+    held, partners = {0: out_weight.T}, {}
     for bit in range(ctx_bits):
         held[2**bit] = swap(held[0], "ctx", 2**bit)
 
-    def merge_step(bit, running, total, offset, got, spread):
-        return kernel_call(
-            functools.partial(merge_kernel, bit),
-            "merge",
-            (
-                shape((state_size, features), F32),
-                shape((1, wide), F32),
-                shape((1, wide), F32),
-                shape((EXTRA, wide)),
-                shape((state_size + EXTRA, features)),
+    def value_columns(values, r):
+        return lax.dynamic_slice_in_dim(values, (me ^ r) * features, features, 1)
+
+    value_head = swap(value_columns(values, 2), "head", 2)
+
+    fade, total = kernel_call(
+        fade_kernel,
+        "fade",
+        (shape(grouped + (wide,)), shape((1, wide), F32)),
+        in_specs=[smem, vmem],
+    )(me1, log_decay)
+    near_fades, side_fades = [fade[0]], [fade[1]]
+    for d in range(2, heads_size, 2):
+        got = swap(tie(fade[d : d + 2], near_fades[-1]), "head", d)
+        near_fades.append(got[0])
+        side_fades.append(got[1])
+    sides = swap(jnp.stack(side_fades), "head", 1)
+    fades = []
+    for d in range(half):
+        fades += [near_fades[d], sides[d]]
+
+    in_turned = lax.dynamic_slice_in_dim(state_in, me * rows_dev, rows_dev, 0).T
+    keep, send = kernel_call(
+        partial_state_kernel,
+        "partial_states",
+        (shape((half, state_size, features), F32), shape((half, state_size, features))),
+        grid_spec=pltpu.PrefetchScalarGridSpec(
+            num_scalar_prefetch=1,
+            grid=(half,),
+            in_specs=[
+                pl.BlockSpec((rows_dev, features), lambda i, m: (0, m[0] ^ (2 * i))),
+                pl.BlockSpec((rows_dev, features), lambda i, m: (0, m[0] ^ (2 * i + 1))),
+            ]
+            + [whole((rows_dev, wide))] * heads_size
+            + [whole((state_size, rows_dev)), whole((wide, features))],
+            out_specs=[
+                pl.BlockSpec((1, state_size, features), lambda i, m: (i, 0, 0)),
+                pl.BlockSpec((1, state_size, features), lambda i, m: (i, 0, 0)),
+            ],
+        ),
+    )(me1, values, values, *fades, in_turned, spread)
+
+    def core_sum(keep, send):
+        own_state, *far_states = kernel_call(
+            fold_kernel,
+            "fold",
+            tuple(
+                [shape((state_size, features), F32)] + [shape((state_size, features))] * (half - 1)
             ),
-            in_specs=[smem] + [vmem] * 5,
-        )(place1, running, total, offset, got, spread)
+        )(keep, swap(send, "head", 1))
+        return own_state, far_states
+
+    own_state, far_states = fenced(core_sum, keep, send)
 
     merge_count = -(-len(merge_rows(stretches)) // 16) * 16
 
-    def near_steps(running, total, sent, log_decay, level_class, level_table, state_in, state_out):
+    def chip_sum(
+        own_state, far_states, total, log_decay, level_class, level_table, state_in, state_out, values
+    ):
+        across = jnp.stack([value_columns(values, d + 1) for d in range(0, heads_size, 2)])
+        across = swap(across, "head", 1)
         table = jnp.transpose(level_table, (1, 0, 2))
         table = jnp.concatenate([table, table], axis=2)
         tables = kernel_call(
@@ -429,205 +479,171 @@
                 shape((heads_size, rows_dev // CH * state_size, rows_dev)),
             ),
         )(log_decay, level_class.reshape(tokens, 1), table, state_in, state_out)
-        spread = spread_heads()
-        factor = jnp.broadcast_to((position % 2).astype(BF16), (EXTRA, wide))
-        factor = jnp.where(jnp.arange(wide)[None, :] < head_count, factor, 0)
-        offset = jnp.zeros((1, wide), F32)
-        states, factors = [], [factor]
-        for bit in range(ctx_bits - 1):
-            states.append(swap(sent, "ctx", 2**bit))
-            running, total, offset, factor, sent = merge_step(
-                bit, running, total, offset, states[-1], spread
-            )
-            factors.append(factor)
-        return states, factors, sent, tables, spread
-
-    def value_columns(values, r, first, count):
-        return lax.dynamic_slice(values, (first, (me ^ r) * features), (count, features))
-
-    early_rows = rows_dev // 2
-
-    def state_chain(values, log_decay, level_class, level_table, state_in, state_out):
-        fade, total = kernel_call(
-            fade_kernel,
-            "fade",
-            (shape((heads_size, rows_dev, wide)), shape((1, wide), F32)),
-            in_specs=[smem, vmem],
-        )(me1, log_decay)
-        near_fades, side_fades = [fade[0]], [fade[1]]
-        for d in range(2, heads_size, 2):
-            got = swap(tie(fade[d : d + 2], near_fades[-1]), "head", d)
-            near_fades.append(got[0])
-            side_fades.append(got[1])
-        sides = swap(jnp.stack(side_fades), "head", 1)
-        fades = []
-        for d in range(half):
-            fades += [near_fades[d], sides[d]]
-        in_turned = lax.dynamic_slice_in_dim(state_in, me * rows_dev, rows_dev, 0).T
-        across = jnp.stack([value_columns(values, d + 1, 0, rows_dev) for d in range(0, heads_size, 2)])
-        across = swap(across, "head", 1)
-        value_head = swap(tie(value_columns(values, 2, 0, early_rows), across), "head", 2)
-        keep, send = kernel_call(
-            partial_state_kernel,
-            "partial_states",
-            (shape((half, state_size, features), F32), shape((half, state_size, features))),
-            grid_spec=pltpu.PrefetchScalarGridSpec(
-                num_scalar_prefetch=1,
-                grid=(half,),
-                in_specs=[
-                    pl.BlockSpec((rows_dev, features), lambda i, m: (0, m[0] ^ (2 * i))),
-                    pl.BlockSpec((rows_dev, features), lambda i, m: (0, m[0] ^ (2 * i + 1))),
-                ]
-                + [whole((rows_dev, wide))] * heads_size
-                + [whole((state_size, rows_dev)), whole((wide, features))],
-                out_specs=[
-                    pl.BlockSpec((1, state_size, features), lambda i, m: (i, 0, 0)),
-                    pl.BlockSpec((1, state_size, features), lambda i, m: (i, 0, 0)),
-                ],
-            ),
-        )(me1, values, values, *fades, in_turned, spread_heads())
-        own_state, *far_states = kernel_call(
-            fold_kernel,
-            "fold",
-            tuple(
-                [shape((state_size, features), F32)] + [shape((state_size, features))] * (half - 1)
-            ),
-        )(keep, swap(tie(send, across), "head", 1))
         got_states = []
         for i, far in enumerate(far_states):
-            got_states.append(swap(tie(far, value_head, *got_states), "head", 2 * (i + 1)))
+            got_states.append(swap(tie(far, *got_states), "head", 2 * (i + 1)))
         running, sent = kernel_call(
             first_kernel,
             "first_state",
             (shape((state_size, features), F32), shape((state_size + EXTRA, features))),
         )(own_state, total, *got_states)
-        others = []
-        for d in range(2, heads_size, 2):
-            first = early_rows if d == 2 else 0
-            own = value_columns(values, d, first, rows_dev - first)
-            both = jnp.concatenate([own, across[d // 2]], axis=0)
-            others.append(swap(tie(both, running, *others), "head", d))
-        states, factors, sent, tables, spread = fenced(
-            near_steps, running, total, sent, log_decay, level_class, level_table, state_in, state_out
-        )
-        return states, factors, sent, tables, spread, across[0], value_head, others
-
-    states, factors, sent, tables, spread, beside, value_head, other_values = fenced(
-        state_chain, values, log_decay, level_class, level_table, state_in, state_out
+        return running, sent, tables, across
+
+    running, sent, tables, across = fenced(
+        chip_sum, own_state, tie(far_states, value_head), total, log_decay, level_class, level_table,
+        state_in, state_out, values,
     )
     lift, read, cross, merge, scores, masked = tables
-    states = list(states)
-    sent = tie(sent, *[held[2**bit] for bit in range(ctx_bits)])
-    states.append(swap(sent, "ctx", 2 ** (ctx_bits - 1)))
-
-    columns = out_weight.shape[1]
-    near = ctx_bits - 1
+
+    def step(bit, running, total, offset, sent, spread, passing):
+        passed = [swap(array, "head", d) for array, d in zip(passing, distances[bit])]
+        got = swap(sent, "ctx", 2**bit)
+        merged = kernel_call(
+            functools.partial(merge_kernel, bit),
+            "merge",
+            (
+                shape((state_size, features), F32),
+                shape((1, wide), F32),
+                shape((1, wide), F32),
+                shape((EXTRA, wide)),
+                shape((state_size + EXTRA, features)),
+            ),
+            in_specs=[smem] + [vmem] * 5,
+        )(place1, running, total, offset, got, spread)
+        return got, merged, passed
+
+    pending = [(d, across[d // 2]) for d in range(2, heads_size, 2)]
+    pending += [(d, value_columns(values, d)) for d in range(4, heads_size, 2)]
+    pieces = max(near, 1)
+    cut = rows_dev // pieces // 16 * 16
+    cuts = [(i * cut, rows_dev if i + 1 == pieces else (i + 1) * cut) for i in range(pieces)]
+    distances = [[d for d, _ in pending]] * pieces
+    factor = jnp.broadcast_to((position % 2).astype(BF16), (EXTRA, wide))
+    factors = [jnp.where(jnp.arange(wide)[None, :] < head_count, factor, 0)]
+    offset = jnp.zeros((1, wide), F32)
+    states, passed = [], []
+    for bit in range(near):
+        if bit == 0:
+            sent = tie(sent, held[1])
+        if bit == 1:
+            sent = tie(sent, held[2])
+        passing = [array[cuts[bit][0] : cuts[bit][1]] for _, array in pending]
+        got, merged, moved = fenced(
+            functools.partial(step, bit), running, total, offset, sent, spread, passing
+        )
+        running, total, offset, factor, sent = merged
+        states.append(got)
+        factors.append(factor)
+        passed.append(moved)
+
+    sent = tie(sent, *[held[2**bit] for bit in range(1, ctx_bits)])
     for r in range(2, ctx_size):
         low = r & -r
         if r not in held and low > 1:
-            held[r] = swap(tie(held[r ^ low], states[near - 1]), "ctx", low)
-    for bit in range(1, ctx_bits):
-        r = 2**bit
-        held[r + 1] = swap(tie(held[r], states[near - 1]), "ctx", 1)
-    same = (
-        (jnp.arange(tile)[:, None] // head_width == jnp.arange(tile)[None, :] // head_width)
-        / head_width
-    ).astype(BF16)
-
-    arrays = [values, beside, value_head] + list(other_values)
-    parts = [[(0, 0, rows_dev)], [(1, 0, rows_dev)]]
-    for i in range(half - 1):
-        if i == 0:
-            mine = [(2, 0, early_rows), (3, 0, rows_dev - early_rows)]
-        else:
-            mine = [(3 + i, 0, rows_dev)]
-        parts += [mine, [(3 + i, mine[-1][2], rows_dev)]]
+            held[r] = swap(tie(held[r ^ low], sent), "ctx", low)
+    for bit in range(2, ctx_bits):
+        held[2**bit + 1] = swap(tie(held[2**bit], sent), "ctx", 1)
+    for r in (0, 1):
+        partners[r] = swap(tie(held[r], sent), "head", 1)
+
+    arrays = [values, across[0], value_head]
+    parts = [[(0, 0, rows_dev)], [(1, 0, rows_dev)], [(2, 0, rows_dev)]]
+    order = {}
+    for i, (d, _) in enumerate(pending):
+        r = d + 1 if i < half - 1 else d
+        order[r] = []
+        for step_index, (start, end) in enumerate(cuts):
+            order[r].append((len(arrays), 0, end - start))
+            arrays.append(passed[step_index][i])
+    parts += [order[r] for r in range(3, heads_size)]
 
     skip_row = jnp.repeat(skip_gain, head_width)[None, :]
-    grouped = (heads_size, rows_dev)
-    pre = kernel_call(
-        lambda me_ref, *refs: local_kernel(me_ref, near, parts, *refs),
-        "local_levels",
-        shape((heads_size, rows_dev, features), F32),
-        grid_spec=pltpu.PrefetchScalarGridSpec(
-            num_scalar_prefetch=1,
-            grid=(tiles,),
-            in_specs=[pl.BlockSpec((rows_dev, tile), lambda f, m: (0, m[0] * tiles + f))]
-            + [
-                pl.BlockSpec((array.shape[0], tile), lambda f, m: (0, f)) for array in arrays[1:]
-            ]
-            + [
-                whole(grouped + (state_size,)),
-                whole(grouped + (wide,)),
-                whole((local + 1,) + grouped + (wide,)),
-                whole((merge_count, wide)),
-                whole(scores.shape),
-                whole(masked.shape),
-                pl.BlockSpec((wide, tile), lambda f, m: (0, f)),
-                pl.BlockSpec((1, tile), lambda f, m: (0, f)),
-                whole((ctx_bits,) + grouped + (wide,)),
-            ]
-            + [whole((EXTRA, wide))] * near
-            + [pl.BlockSpec((state_size + EXTRA, tile), lambda f, m: (0, f))] * near,
-            out_specs=pl.BlockSpec(grouped + (tile,), lambda f, m: (0, 0, f)),
-            scratch_shapes=[
-                pltpu.VMEM((heads_size, rows_dev // CH * state_size, tile), F32),
-                pltpu.VMEM((max(local, 1), state_size, tile), F32),
-                pltpu.VMEM((max(local, 1), 2 * state_size, tile), BF16),
-            ],
-        ),
-    )(
-        me1,
-        *arrays,
-        state_out.reshape(grouped + (state_size,)),
-        lift.reshape(grouped + (wide,)),
-        read.reshape((local + 1,) + grouped + (wide,)),
-        merge,
-        scores,
-        masked,
-        spread,
-        skip_row,
-        cross.reshape((ctx_bits,) + grouped + (wide,)),
-        *factors[:near],
-        *states[:near],
-    )
-
-    normed = kernel_call(
-        finish_kernel,
-        "finish",
-        tuple([shape((rows_dev, features))] * heads_size),
-        grid_spec=pltpu.PrefetchScalarGridSpec(
-            num_scalar_prefetch=1,
-            grid=(tiles,),
-            in_specs=[
-                pl.BlockSpec(grouped + (tile,), lambda f, m: (0, 0, f)),
-                whole(grouped + (state_size,)),
-                whole(grouped + (wide,)),
-                whole((EXTRA, wide)),
-                pl.BlockSpec((state_size + EXTRA, tile), lambda f, m: (0, f)),
-                pl.BlockSpec((wide, tile), lambda f, m: (0, f)),
-                whole((tile, tile)),
-                pl.BlockSpec((1, tile), lambda f, m: (0, f)),
-            ],
-            out_specs=[pl.BlockSpec((rows_dev, tile), lambda f, m: (0, f))] * heads_size,
-        ),
-    )(
-        me1,
-        pre,
-        state_out.reshape(grouped + (state_size,)),
-        cross[-1].reshape(grouped + (wide,)),
-        factors[-1],
-        states[-1],
-        spread,
-        same,
+
+    def read_levels(sent, state_out, tables, factors, states, arrays, spread, same, skip_row, norm_row):
+        lift, read, cross, merge, scores, masked = tables
+        state = swap(sent, "ctx", 2**near)
+        readers = state_out.reshape(grouped + (state_size,))
+        cross = cross.reshape((ctx_bits,) + grouped + (wide,))
+        pre = kernel_call(
+            lambda me_ref, *refs: local_kernel(me_ref, near, parts, *refs),
+            "local_levels",
+            shape(grouped + (features,), F32),
+            grid_spec=pltpu.PrefetchScalarGridSpec(
+                num_scalar_prefetch=1,
+                grid=(tiles,),
+                in_specs=[pl.BlockSpec((rows_dev, tile), lambda f, m: (0, m[0] * tiles + f))]
+                + [pl.BlockSpec((array.shape[0], tile), lambda f, m: (0, f)) for array in arrays[1:]]
+                + [
+                    whole(readers.shape),
+                    whole(grouped + (wide,)),
+                    whole((local + 1,) + grouped + (wide,)),
+                    whole((merge_count, wide)),
+                    whole(scores.shape),
+                    whole(masked.shape),
+                    pl.BlockSpec((wide, tile), lambda f, m: (0, f)),
+                    pl.BlockSpec((1, tile), lambda f, m: (0, f)),
+                    whole(cross.shape),
+                ]
+                + [whole((EXTRA, wide))] * near
+                + [pl.BlockSpec((state_size + EXTRA, tile), lambda f, m: (0, f))] * near,
+                out_specs=pl.BlockSpec(grouped + (tile,), lambda f, m: (0, 0, f)),
+                scratch_shapes=[
+                    pltpu.VMEM((heads_size, rows_dev // CH * state_size, tile), F32),
+                    pltpu.VMEM((max(local, 1), state_size, tile), F32),
+                    pltpu.VMEM((max(local, 1), 2 * state_size, tile), BF16),
+                ],
+            ),
+        )(
+            me1,
+            *arrays,
+            readers,
+            lift.reshape(grouped + (wide,)),
+            read.reshape((local + 1,) + grouped + (wide,)),
+            merge,
+            scores,
+            masked,
+            spread,
+            skip_row,
+            cross,
+            *factors[:near],
+            *states,
+        )
+        return kernel_call(
+            finish_kernel,
+            "finish",
+            tuple([shape((rows_dev, features))] * heads_size),
+            grid_spec=pltpu.PrefetchScalarGridSpec(
+                num_scalar_prefetch=1,
+                grid=(tiles,),
+                in_specs=[
+                    pl.BlockSpec(grouped + (tile,), lambda f, m: (0, 0, f)),
+                    whole(readers.shape),
+                    pl.BlockSpec((1,) + grouped + (wide,), lambda f, m: (near, 0, 0, 0)),
+                    whole((EXTRA, wide)),
+                    pl.BlockSpec((state_size + EXTRA, tile), lambda f, m: (0, f)),
+                    pl.BlockSpec((wide, tile), lambda f, m: (0, f)),
+                    whole((tile, tile)),
+                    pl.BlockSpec((1, tile), lambda f, m: (0, f)),
+                ],
+                out_specs=[pl.BlockSpec((rows_dev, tile), lambda f, m: (0, f))] * heads_size,
+            ),
+        )(me1, pre, readers, cross, factors[near], state, spread, same, norm_row)
+
+    normed = fenced(
+        read_levels, sent, state_out, tables, factors, states, arrays, spread, same, skip_row,
         norm_gain[None, :],
     )
-    kept = normed[0::2]
-    others = [swap(array, "head", 1) for array in normed[1::2]]
+    early_blocks = set(held)
+    done = [held[r] for r in held if r not in (0, 1)] + list(normed)
+    held[3] = swap(tie(held[1], *done), "ctx", 2)
+    for r in range(5, ctx_size, 2):
+        if r not in held:
+            held[r] = swap(tie(held[r ^ 1], *done), "ctx", 1)
 
     count = 1
     while count * columns % 128 and 2 * count <= ctx_size:
         count *= 2
+
     def project(name, kept, others, blocks, partners, kind):
         return kernel_call(
             project_kernel,
@@ -636,35 +652,53 @@
             in_specs=[smem] + [vmem] * (2 * len(kept) + 2 * count),
         )(place1, *kept, *others, *blocks, *partners)
 
-    def far_part(kept, others, blocks):
-        partners = [swap(block, "head", 1) for block in blocks]
-        return project("project_far", kept, others, blocks, partners, BF16), partners
-
-    fars, arrived, owns = [], [], []
-    for first in range(0, ctx_size, count):
-        group = range(first, first + count)
-        for r in group:
-            if r not in held:
-                side = (r ^ 1) & -(r ^ 1)
-                ready = arrived[max(len(fars) - 3, 0)] + fars[max(len(fars) - 2, 0) :][:1]
-                top = lax.slice_in_dim(tie(held[r ^ 1], *ready), 0, columns // 2, axis=0)
-                rest = lax.slice_in_dim(tie(held[r ^ side], *ready), columns // 2, columns, axis=0)
-                held[r] = jnp.concatenate([swap(top, "ctx", 1), swap(rest, "ctx", side)], axis=0)
-        blocks = [held[r] for r in group]
-        if first == 0:
-            far, partners = far_part(kept[1:], others[1:], blocks)
-        else:
-            if len(owns) >= 3:
-                blocks[0] = tie(blocks[0], *owns[:-1])
-            far, partners = fenced(far_part, kept[1:], others[1:], blocks)
-        fars.append(far)
-        if len(arrived) >= 1:
-            far = tie(far, *arrived[-1])
-        arrived.append([swap(far[i - 1], "head", 2 * i) for i in range(1, half)])
-        owns.append(project("project_own", kept[:1], others[:1], blocks, partners, F32))
-    pieces = []
-    for own, got in zip(owns, arrived):
-        pieces += [own[0]] + got
+    kept = list(normed[0::2])
+    sides = list(normed[1::2])
+    group_of = lambda first: range(first, first + count)
+
+    def project_groups(firsts, kept, others, blocks, partners, arrived):
+        partners, results = dict(partners), {}
+        for first in firsts:
+            for r in group_of(first):
+                if r not in partners:
+                    partners[r] = swap(blocks[r], "head", 1)
+            weights = [blocks[r] for r in group_of(first)]
+            given = [partners[r] for r in group_of(first)]
+            far = project("project_far", kept[1:], others[1:], weights, given, BF16)
+            if arrived:
+                far = tie(far, arrived[-1])
+            got = [swap(far[i - 1], "head", 2 * i) for i in range(1, half)]
+            own = project("project_own", kept[:1], others[:1], weights, given, F32)
+            results[first] = [own[0]] + got
+            arrived = arrived + got[-1:]
+        return results
+
+    def first_groups(kept, sides, blocks, partners):
+        others = [swap(side, "head", 1) for side in sides[1:]]
+        partners = dict(partners)
+        for r in first_blocks:
+            if r not in partners:
+                partners[r] = swap(blocks[r], "head", 1)
+        others = [swap(tie(sides[0], *others, partners[first_blocks[-1]]), "head", 1)] + others
+        return project_groups(early_groups, kept, others, blocks, partners, []), others
+
+    def last_groups(kept, others, blocks, partners):
+        return project_groups(late_groups, kept, others, blocks, partners, [])
+
+    firsts = list(range(0, ctx_size, count))
+    early_groups = [f for f in firsts if all(r in early_blocks for r in group_of(f))]
+    early_groups = early_groups or firsts[:1]
+    late_groups = [f for f in firsts if f not in early_groups]
+    first_blocks = [r for f in early_groups for r in group_of(f)]
+    last_blocks = [r for f in late_groups for r in group_of(f)]
+    results, others = fenced(
+        first_groups, kept, sides, {r: held[r] for r in first_blocks}, partners
+    )
+    if late_groups:
+        results.update(
+            fenced(last_groups, kept, others, {r: held[r] for r in last_blocks}, {})
+        )
+    pieces = [piece for first in firsts for piece in results[first]]
     return kernel_call(
         assemble_kernel,
         "assemble",

time: 165 us -> 167 us (1.012)
  waiting for transfers between devices: 40.1 us -> 49 us
  local copies, waits for them, and re-layouts: 22.4 us -> 15.2 us
  starting transfers between devices: 26.3 us -> 28.2 us
  other arithmetic: 3.28 us -> 1.54 us
    ppermute x32, waiting for transfers between devices: 40.1 us -> 49 us  [swap(): return lax.ppermute(value, axis, pairs)]
    another operation x6 -> x4, local copies, waits for them, and re-layouts: 3.95 us -> 0.45 us
    ppermute x32, starting transfers between devices: 26.3 us -> 28.2 us  [swap(): return lax.ppermute(value, axis, pairs)]
    concatenate x1 -> x0, local copies, waits for them, and re-layouts: 1.78 us -> none  [on_device(): jnp.concatenate([swap(top, 'ctx', 1), swap(rest, 'ctx', side)], axis=0)]
    dynamic_slice x1 -> x2, local copies, waits for them, and re-layouts: 1.12 us -> 2.88 us  [the longest x1 2.03 us: value_columns(): return lax.dynamic_slice_in_dim(values, (me ^ r) * features, features, 1)]
    slice x5 -> x4, local copies, waits for them, and re-layouts: 5.34 us -> 3.95 us  [the longest x1 1.98 us: on_device(): arrays = [values, across[0], value_head]]
    cond x17 -> x18, local copies, waits for them, and re-layouts: 3.14 us -> 4.31 us
  transfers between devices with their start and end apart: 32 -> 32, of which waited for: 14 -> 15; matrix products, arithmetic and copies ran while one was open for 14% -> 9% of each run, Pallas kernels for 42% -> 42%
where the time goes in v4:
time: 167 us; the launch traced here: 166 us
  Pallas kernels  71.9 us (43%)
  waiting for transfers between devices  49 us (29%)
  starting transfers between devices  28.2 us (17%)
  local copies, waits for them, and re-layouts  15.2 us (9%)
    ppermute x32, waiting for transfers between devices, swap(): return lax.ppermute(value, axis, pairs)  49 us
    ppermute x32, starting transfers between devices, swap(): return lax.ppermute(value, axis, pairs)  28.2 us
    pallas_call x8, Pallas kernels, project(): kernel_call(project_kernel, name, shape((len(kept), rows_dev, count * col...  26.6 us
    pallas_call x1, Pallas kernels, read_levels(): kernel_call(lambda me_ref, *refs: local_kernel(me_ref, near, parts, *refs...  20.4 us
    pallas_call x1, Pallas kernels, read_levels(): kernel_call(finish_kernel, 'finish', tuple([shape((rows_dev, features))]...  6.95 us
    pallas_call x2, Pallas kernels, step(): kernel_call(functools.partial(merge_kernel, bit), 'merge', (shape((state_...  4.74 us
    cond x18, local copies, waits for them, and re-layouts  4.31 us
    pallas_call x1, Pallas kernels, chip_sum(): kernel_call(factors_kernel, 'factors', (shape((tokens, wide)), shape((loc...  3.71 us
  transfers between devices with their start and end apart: 32, of which 15 were waited for; matrix products, arithmetic and copies ran while one was open for 9% of the time, Pallas kernels for 42%

profile of v4, /device:TPU:0, one launch (start us, length us, event | category | flops | bytes accessed | tf_op | source)
XLA Modules:
  0.0 166.3 jit_solution(10111239144830338121)
XLA Ops:
  0.0 2.9 %collective-permute-start.23 = (bf16[320,1280]{1,0:T(8,128)(2,1)}, bf16[320,1280]{1,0:T(8,128)(2,1)}, u32[]{:S(2)}, u32[]{:S(2)}) collective-permute-start(bf16[320,1280]{1,0:T(8,128)(2,1)} %bitcast.27), channel_id=1, source_target_pairs={{0,4},{4,0},{8,12},{12,8},{16,20},{20,16},{24,28},{28,24},{1,5},{5... | collective-permute-start | bytes 2457608 | tf_op jit(solution)/shard_map/ppermute | solution.py:32
  18.3 4.5 %conditional.7 = ((f32[128,1280]{1,0:T(8,128)S(1)}, bf16[128,1280]{1,0:T(8,128)(2,1)})) conditional(s32[]{:T(128)} %convert_element_type.29, () %tuple.79, (bf16[2,128,1280]{2,1,0:T(8,128)(2,1)}, f32[2,128,1280]{2,1,0:T(8,128)}) %tuple.81), branch_computations={%region_0.1_spmd, %region_1.2_spmd} | conditional | bytes 2621488 | solution.py:390
  22.8 5.4 %collective-permute-done.22 = bf16[256,1280]{1,0:T(8,128)(2,1)} collective-permute-done((bf16[256,1280]{1,0:T(8,128)(2,1)}, bf16[256,1280]{1,0:T(8,128)(2,1)}, u32[]{:S(2)}, u32[]{:S(2)}) %collective-permute-start.22) | collective-permute-done | bytes 655392 | tf_op jit(solution)/shard_map/ppermute | solution.py:32
  28.2 21.1 %conditional.8 = (f32[128,1280]{1,0:T(8,128)}, bf16[144,1280]{1,0:T(8,128)(2,1)}, bf16[1024,40]{1,0:T(8,128)(2,1)}, bf16[5,1024,40]{2,1,0:T(8,128)(2,1)}, bf16[3...) conditional(s32[]{:T(128)} %convert_element_type.29, () %tuple.78, ...), branch_computations={%region_2.3_spmd, %region_3.4_spmd} | conditional | flops 665610 | bytes 20804020 | solution.py:390
  31.8 3.7 %factors.1 = (bf16[1024,40]{1,0:T(8,128)(2,1)}, bf16[5,1024,40]{2,1,0:T(8,128)(2,1)}, bf16[3,1024,40]{2,1,0:T(8,128)(2,1)}, bf16[32,40]{1,0:T(8,128)(2,1)S(1)}, ...) custom-call(f32[1024,20]{1,0:T(8,128)S(1)} %copy.35.decay_ref, s32[1024,1]{1,0:T(8,128)S(1)} %copy.31.class_ref, ...), custom_call_target="tpu_custom_call" | custom-call | tf_op jit(solution)/shard_map/cond/branch_1_fun/factors/pallas_call | solution.py:470
  35.5 4.2 %collective-permute-done.18.refs_0_ = bf16[128,1280]{1,0:T(8,128)(2,1)S(1)} collective-permute-done((bf16[128,1280]{1,0:T(8,128)(2,1)S(1)}, bf16[128,1280]{1,0:T(8,128)(2,1)S(1)}, u32[]{:S(2)}, u32[]{:S(2)}) %collective-permute-start.18) | collective-permute-done | bytes 327712 | tf_op jit(solution)/shard_map/cond/branch_1_fun/ppermute | solution.py:32
  49.3 12.9 %conditional.9 = (bf16[144,1280]{1,0:T(8,128)(2,1)}, f32[128,1280]{1,0:T(8,128)}, f32[1,40]{1,0:T(1,128)S(1)}, f32[1,40]{1,0:T(1,128)S(1)}, bf16[16,40]{1,0:T(8,...) conditional(s32[]{:T(128)} %convert_element_type.29, () %tuple.84, ...), branch_computations={%region_4.5_spmd, %region_5.6_spmd} | conditional | bytes 2785580 | solution.py:390
  51.4 8.6 %collective-permute-done.1.got_ref = bf16[144,1280]{1,0:T(8,128)(2,1)} collective-permute-done((bf16[144,1280]{1,0:T(8,128)(2,1)}, bf16[144,1280]{1,0:T(8,128)(2,1)}, u32[]{:S(2)}, u32[]{:S(2)}) %collective-permute-start.1) | collective-permute-done | bytes 368672 | tf_op jit(solution)/shard_map/cond/branch_1_fun/ppermute | solution.py:32
  62.3 12.0 %conditional.10 = (bf16[144,1280]{1,0:T(8,128)(2,1)}, bf16[16,40]{1,0:T(8,128)(2,1)S(1)}, bf16[144,1280]{1,0:T(8,128)(2,1)}, bf16[128,1280]{1,0:T(8,128)(2,1)}) conditional(s32[]{:T(128)} %convert_element_type.29, () %tuple.87, (bf16[144,1280]{1,0:T(8,128)(2,1)S(1)}, s32[1]{0:T(128)}, f32[128,1280]{1,0:T(8,128)}, f32[1,40]{1,0:T(1,128)S(1)}, ...), branch_computations={%region_6.7_spmd, %region_7.8_spmd} | conditional | bytes 2785392 | solution.py:390
  64.2 7.6 %collective-permute-done.3.got_ref = bf16[144,1280]{1,0:T(8,128)(2,1)} collective-permute-done((bf16[144,1280]{1,0:T(8,128)(2,1)S(1)}, bf16[144,1280]{1,0:T(8,128)(2,1)}, u32[]{:S(2)}, u32[]{:S(2)}) %collective-permute-start.3) | collective-permute-done | bytes 368672 | tf_op jit(solution)/shard_map/cond/branch_1_fun/ppermute | solution.py:32
  76.0 29.8 %conditional.11 = ((bf16[256,1280]{1,0:T(8,128)(2,1)}, bf16[256,1280]{1,0:T(8,128)(2,1)S(1)}, bf16[256,1280]{1,0:T(8,128)(2,1)}, bf16[256,1280]{1,0:T(8,128)(2,1)})) conditional(s32[]{:T(128)} %convert_element_type.29, () %tuple.77, (bf16[1024,128]{1,0:T(8,128)(2,1)}, bf16[1024,40]{1,0:T(8,128)(2,1)}, bf16[5,1024,40]{2,1,0:T(8,128)(2,1)}, ...), branch_computations={%region_8.9_spmd, %region_9.10_spmd} | conditional | flops 80 | bytes 5171962 | solution.py:390
  77.4 20.4 %local_levels.1.pre_ref = f32[4,256,1280]{2,1,0:T(8,128)S(1)} custom-call(s32[1]{0:T(128)} %get-tuple-element.202.me_ref, bf16[256,5120]{1,0:T(8,128)(2,1)S(1)} %get-tuple-element.203.refs_0_, bf16[256,1280]{1,0:T(8,128)(2,1)} %copy-done.4, bf16[256,1280]{1,0:T(8,128)(2,1)} %get-tuple-element.205.refs_2_, bf16[128,1280]{1,0:T(8,128)(2,1)} %get-tuple-element.206.refs_3_, ...), custom_call_target="tpu_custom_call" | custom-call | tf_op jit(solution)/shard_map/cond/branch_1_fun/local_levels/pallas_call | solution.py:567
  98.9 7.0 %finish.1 = (bf16[256,1280]{1,0:T(8,128)(2,1)}, bf16[256,1280]{1,0:T(8,128)(2,1)S(1)}, bf16[256,1280]{1,0:T(8,128)(2,1)}, bf16[256,1280]{1,0:T(8,128)(2,1)}) custom-call(s32[1]{0:T(128)} %get-tuple-element.202.me_ref, f32[4,256,1280]{2,1,0:T(8,128)S(1)} %local_levels.1.pre_ref, bf16[4,256,128]{2,1,0:T(8,128)(2,1)S(1)} %bitcast.47, ...), custom_call_target="tpu_custom_call" | custom-call | tf_op jit(solution)/shard_map/cond/branch_1_fun/finish/pallas_call | solution.py:611
  109.7 26.3 %conditional.12 = (f32[256,640]{1,0:T(8,128)S(1)}, bf16[256,640]{1,0:T(8,128)(2,1)}, f32[256,640]{1,0:T(8,128)S(1)}, bf16[256,640]{1,0:T(8,128)(2,1)}, bf16[256,...) conditional(s32[]{:T(128)} %convert_element_type.29, () %tuple.76, (bf16[256,1280]{1,0:T(8,128)(2,1)}, ...), branch_computations={%region_10.11_spmd, %region_11.12_spmd} | conditional | bytes 19661144 | solution.py:390
  113.2 3.9 %project_far.4 = bf16[1,256,640]{2,1,0:T(8,128)(2,1)S(1)} custom-call(s32[1]{0:T(128)} %get-tuple-element.227.place_ref, bf16[256,1280]{1,0:T(8,128)(2,1)} %get-tuple-element.237.refs_0_, bf16[256,1280]{1,0:T(8,128)(2,1)S(1)} %collective-permute-done.5.refs_1_, bf16[320,1280]{1,0:T(8,128)(2,1)} %get-tuple-element.233.refs_2_, ...), custom_call_target="tpu_custom_call" | custom-call | tf_op jit(solution)/shard_map/cond/branch_1_fun/project_far/pallas_call | solution.py:648
  118.6 3.2 %project_far.5 = bf16[1,256,640]{2,1,0:T(8,128)(2,1)S(1)} custom-call(s32[1]{0:T(128)} %get-tuple-element.227.place_ref, bf16[256,1280]{1,0:T(8,128)(2,1)} %get-tuple-element.237.refs_0_, bf16[256,1280]{1,0:T(8,128)(2,1)S(1)} %collective-permute-done.5.refs_1_, bf16[320,1280]{1,0:T(8,128)(2,1)} %get-tuple-element.238.refs_2_, ...), custom_call_target="tpu_custom_call" | custom-call | tf_op jit(solution)/shard_map/cond/branch_1_fun/project_far/pallas_call | solution.py:648
  121.8 5.2 %collective-permute-done.8 = bf16[256,640]{1,0:T(8,128)(2,1)} collective-permute-done((bf16[256,640]{1,0:T(8,128)(2,1)S(1)}, bf16[256,640]{1,0:T(8,128)(2,1)}, u32[]{:S(2)}, u32[]{:S(2)}) %collective-permute-start.8) | collective-permute-done | bytes 327712 | tf_op jit(solution)/shard_map/cond/branch_1_fun/ppermute | solution.py:32
  128.4 3.4 %project_own.5 = f32[1,256,640]{2,1,0:T(8,128)S(1)} custom-call(s32[1]{0:T(128)} %get-tuple-element.227.place_ref, bf16[256,1280]{1,0:T(8,128)(2,1)} %get-tuple-element.228.refs_0_, bf16[256,1280]{1,0:T(8,128)(2,1)} %collective-permute-done.7.refs_1_, bf16[320,1280]{1,0:T(8,128)(2,1)} %get-tuple-element.238.refs_2_, ...), custom_call_target="tpu_custom_call" | custom-call | tf_op jit(solution)/shard_map/cond/branch_1_fun/project_own/pallas_call | solution.py:648
  131.8 4.0 %project_own.4 = f32[1,256,640]{2,1,0:T(8,128)S(1)} custom-call(s32[1]{0:T(128)} %get-tuple-element.227.place_ref, bf16[256,1280]{1,0:T(8,128)(2,1)} %get-tuple-element.228.refs_0_, bf16[256,1280]{1,0:T(8,128)(2,1)} %collective-permute-done.7.refs_1_, bf16[320,1280]{1,0:T(8,128)(2,1)} %get-tuple-element.233.refs_2_, ...), custom_call_target="tpu_custom_call" | custom-call | tf_op jit(solution)/shard_map/cond/branch_1_fun/project_own/pallas_call | solution.py:648
  136.9 26.7 %conditional.13 = (f32[256,640]{1,0:T(8,128)S(1)}, bf16[256,640]{1,0:T(8,128)(2,1)}, f32[256,640]{1,0:T(8,128)S(1)}, bf16[256,640]{1,0:T(8,128)(2,1)}) conditional(s32[]{:T(128)} %convert_element_type.29, () %tuple.96, (bf16[320,1280]{1,0:T(8,128)(2,1)}, bf16[320,1280]{1,0:T(8,128)(2,1)S(1)}, s32[1]{0:T(128)}, bf16[256,1280]{1,0:T(8,128)(2,1)}, ...), branch_computations={%region_12.13_spmd, %region_13.14_spmd} | conditional | bytes 15728912 | solution.py:390
  145.6 2.9 %project_far.7 = bf16[1,256,640]{2,1,0:T(8,128)(2,1)S(1)} custom-call(s32[1]{0:T(128)} %get-tuple-element.240.place_ref, bf16[256,1280]{1,0:T(8,128)(2,1)} %get-tuple-element.245.refs_0_, bf16[256,1280]{1,0:T(8,128)(2,1)S(1)} %get-tuple-element.246.refs_1_, bf16[320,1280]{1,0:T(8,128)(2,1)} %get-tuple-element.247.refs_2_, ...), custom_call_target="tpu_custom_call" | custom-call | tf_op jit(solution)/shard_map/cond/branch_1_fun/project_far/pallas_call | solution.py:648
  148.5 5.7 %collective-permute-done.13 = bf16[256,640]{1,0:T(8,128)(2,1)} collective-permute-done((bf16[256,640]{1,0:T(8,128)(2,1)S(1)}, bf16[256,640]{1,0:T(8,128)(2,1)}, u32[]{:S(2)}, u32[]{:S(2)}) %collective-permute-start.13) | collective-permute-done | bytes 327712 | tf_op jit(solution)/shard_map/cond/branch_1_fun/ppermute | solution.py:32
  155.7 3.2 %project_own.6 = f32[1,256,640]{2,1,0:T(8,128)S(1)} custom-call(s32[1]{0:T(128)} %get-tuple-element.240.place_ref, bf16[256,1280]{1,0:T(8,128)(2,1)} %get-tuple-element.241.refs_0_, bf16[256,1280]{1,0:T(8,128)(2,1)} %get-tuple-element.242.refs_1_, bf16[320,1280]{1,0:T(8,128)(2,1)} %get-tuple-element.243.refs_2_, ...), custom_call_target="tpu_custom_call" | custom-call | tf_op jit(solution)/shard_map/cond/branch_1_fun/project_own/pallas_call | solution.py:648
  158.8 3.2 %project_own.7 = f32[1,256,640]{2,1,0:T(8,128)S(1)} custom-call(s32[1]{0:T(128)} %get-tuple-element.240.place_ref, bf16[256,1280]{1,0:T(8,128)(2,1)} %get-tuple-element.241.refs_0_, bf16[256,1280]{1,0:T(8,128)(2,1)} %get-tuple-element.242.refs_1_, bf16[320,1280]{1,0:T(8,128)(2,1)} %get-tuple-element.247.refs_2_, ...), custom_call_target="tpu_custom_call" | custom-call | tf_op jit(solution)/shard_map/cond/branch_1_fun/project_own/pallas_call | solution.py:648
  (127 shorter events, 71.5 us)
Async XLA Ops:
  0.0 49.3 %collective-permute-start.23 = (bf16[320,1280]{1,0:T(8,128)(2,1)}, bf16[320,1280]{1,0:T(8,128)(2,1)}, u32[]{:S(2)}, u32[]{:S(2)}) collective-permute-start(bf16[320,1280]{1,0:T(8,128)(2,1)} %bitcast.27), channel_id=1, source_target_pairs={{0,4},{4,0},{8,12},{12,8},{16,20},{20,16},{24,28},{28,24},{1,5},{5... | collective-permute-start | bytes 2457608 | tf_op jit(solution)/shard_map/ppermute | solution.py:32
  2.9 59.3 %collective-permute-start.24 = (bf16[320,1280]{1,0:T(8,128)(2,1)}, bf16[320,1280]{1,0:T(8,128)(2,1)}, u32[]{:S(2)}, u32[]{:S(2)}) collective-permute-start(bf16[320,1280]{1,0:T(8,128)(2,1)} %bitcast.27), channel_id=1, source_target_pairs={{0,8},{4,12},{8,0},{12,4},{16,24},{20,28},{24,16},{28,20},{1,9},{5... | collective-permute-start | bytes 2457608 | tf_op jit(solution)/shard_map/ppermute | solution.py:32
  4.5 69.8 %collective-permute-start.25 = (bf16[320,1280]{1,0:T(8,128)(2,1)}, bf16[320,1280]{1,0:T(8,128)(2,1)}, u32[]{:S(2)}, u32[]{:S(2)}) collective-permute-start(bf16[320,1280]{1,0:T(8,128)(2,1)} %bitcast.27), channel_id=1, source_target_pairs={{0,16},{4,20},{8,24},{12,28},{16,0},{20,4},{24,8},{28,12},{1,17},{... | collective-permute-start | bytes 2457608 | tf_op jit(solution)/shard_map/ppermute | solution.py:32
  12.6 15.7 %collective-permute-start.22 = (bf16[256,1280]{1,0:T(8,128)(2,1)}, bf16[256,1280]{1,0:T(8,128)(2,1)}, u32[]{:S(2)}, u32[]{:S(2)}) collective-permute-start(bf16[256,1280]{1,0:T(8,128)(2,1)} %constant_dynamic-slice_fusion), channel_id=1, source_target_pairs={{0,2},{1,3},{2,0},{3,1},{4,6},{5,7},{6,4},{7,5},{8,10},{9,11},{10,... | collective-permute-start | bytes 1966088 | tf_op jit(solution)/shard_map/ppermute | solution.py:32
  29.6 11.2 %collective-permute-start.19 = (bf16[2,256,1280]{2,1,0:T(8,128)(2,1)}, bf16[2,256,1280]{2,1,0:T(8,128)(2,1)}, u32[]{:S(2)}, u32[]{:S(2)}) collective-permute-start(bf16[2,256,1280]{2,1,0:T(8,128)(2,1)} %pad_maximum_fusion), channel_id=1, source_target_pairs={{0,1},{1,0},{2,3},{3,2},{4,5},{5,4},{6,7},{7,6},{8,9},{9,8},{10,11... | collective-permute-start | bytes 3932168 | tf_op jit(solution)/shard_map/cond/branch_1_fun/ppermute | solution.py:32
  29.6 10.1 %collective-permute-start.18 = (bf16[128,1280]{1,0:T(8,128)(2,1)S(1)}, bf16[128,1280]{1,0:T(8,128)(2,1)S(1)}, u32[]{:S(2)}, u32[]{:S(2)}) collective-permute-start(bf16[128,1280]{1,0:T(8,128)(2,1)S(1)} %copy-done.10), channel_id=1, source_target_pairs={{0,2},{1,3},{2,0},{3,1},{4,6},{5,7},{6,4},{7,5},{8,10},{9,11},{10,... | collective-permute-start | bytes 983048 | tf_op jit(solution)/shard_map/cond/branch_1_fun/ppermute | solution.py:32
  49.4 10.6 %collective-permute-start.1 = (bf16[144,1280]{1,0:T(8,128)(2,1)}, bf16[144,1280]{1,0:T(8,128)(2,1)}, u32[]{:S(2)}, u32[]{:S(2)}) collective-permute-start(bf16[144,1280]{1,0:T(8,128)(2,1)} %get-tuple-element.182), channel_id=1, source_target_pairs={{0,4},{4,0},{8,12},{12,8},{16,20},{20,16},{24,28},{28,24},{1,5},{5... | collective-permute-start | bytes 1105928 | tf_op jit(solution)/shard_map/cond/branch_1_fun/ppermute | solution.py:32
  49.9 12.3 %collective-permute-start.2 = (bf16[128,1280]{1,0:T(8,128)(2,1)}, bf16[128,1280]{1,0:T(8,128)(2,1)}, u32[]{:S(2)}, u32[]{:S(2)}) collective-permute-start(bf16[128,1280]{1,0:T(8,128)(2,1)} %get-tuple-element.192), channel_id=1, source_target_pairs={{0,2},{1,3},{2,0},{3,1},{4,6},{5,7},{6,4},{7,5},{8,10},{9,11},{10,... | collective-permute-start | bytes 983048 | tf_op jit(solution)/shard_map/cond/branch_1_fun/ppermute | solution.py:32
  62.3 9.5 %collective-permute-start.3 = (bf16[144,1280]{1,0:T(8,128)(2,1)S(1)}, bf16[144,1280]{1,0:T(8,128)(2,1)}, u32[]{:S(2)}, u32[]{:S(2)}) collective-permute-start(bf16[144,1280]{1,0:T(8,128)(2,1)S(1)} %get-tuple-element.193), channel_id=1, source_target_pairs={{0,8},{4,12},{8,0},{12,4},{16,24},{20,28},{24,16},{28,20},{1,9},{5... | collective-permute-start | bytes 1105928 | tf_op jit(solution)/shard_map/cond/branch_1_fun/ppermute | solution.py:32
  62.8 11.5 %collective-permute-start.4 = (bf16[128,1280]{1,0:T(8,128)(2,1)}, bf16[128,1280]{1,0:T(8,128)(2,1)}, u32[]{:S(2)}, u32[]{:S(2)}) collective-permute-start(bf16[128,1280]{1,0:T(8,128)(2,1)} %get-tuple-element.201), channel_id=1, source_target_pairs={{0,2},{1,3},{2,0},{3,1},{4,6},{5,7},{6,4},{7,5},{8,10},{9,11},{10,... | collective-permute-start | bytes 983048 | tf_op jit(solution)/shard_map/cond/branch_1_fun/ppermute | solution.py:32
  74.3 31.6 %collective-permute-start.26 = (bf16[320,1280]{1,0:T(8,128)(2,1)}, bf16[320,1280]{1,0:T(8,128)(2,1)}, u32[]{:S(2)}, u32[]{:S(2)}) collective-permute-start(bf16[320,1280]{1,0:T(8,128)(2,1)} %collective-permute-done.25), channel_id=1, source_target_pairs={{0,4},{4,0},{8,12},{12,8},{16,20},{20,16},{24,28},{28,24},{1,5},{5... | collective-permute-start | bytes 2457608 | tf_op jit(solution)/shard_map/ppermute | solution.py:32
  74.9 31.0 %collective-permute-start.29 = (bf16[320,1280]{1,0:T(8,128)(2,1)}, bf16[320,1280]{1,0:T(8,128)(2,1)}, u32[]{:S(2)}, u32[]{:S(2)}) collective-permute-start(bf16[320,1280]{1,0:T(8,128)(2,1)} %collective-permute-done.25), channel_id=1, source_target_pairs={{0,8},{4,12},{8,0},{12,4},{16,24},{20,28},{24,16},{28,20},{1,9},{5... | collective-permute-start | bytes 2457608 | tf_op jit(solution)/shard_map/ppermute | solution.py:32
  75.5 34.2 %collective-permute-start.28 = (bf16[320,1280]{1,0:T(8,128)(2,1)}, bf16[320,1280]{1,0:T(8,128)(2,1)}, u32[]{:S(2)}, u32[]{:S(2)}) collective-permute-start(bf16[320,1280]{1,0:T(8,128)(2,1)} %collective-permute-done.23), channel_id=1, source_target_pairs={{0,1},{1,0},{2,3},{3,2},{4,5},{5,4},{6,7},{7,6},{8,9},{9,8},{10,11... | collective-permute-start | bytes 2457608 | tf_op jit(solution)/shard_map/ppermute | solution.py:32
  75.5 34.2 %collective-permute-start.27 = (bf16[320,1280]{1,0:T(8,128)(2,1)}, bf16[320,1280]{1,0:T(8,128)(2,1)}, u32[]{:S(2)}, u32[]{:S(2)}) collective-permute-start(bf16[320,1280]{1,0:T(8,128)(2,1)} %bitcast.27), channel_id=1, source_target_pairs={{0,1},{1,0},{2,3},{3,2},{4,5},{5,4},{6,7},{7,6},{8,9},{9,8},{10,11... | collective-permute-start | bytes 2457608 | tf_op jit(solution)/shard_map/ppermute | solution.py:32
  76.9 22.0 %collective-permute-start.17 = (bf16[144,1280]{1,0:T(8,128)(2,1)}, bf16[144,1280]{1,0:T(8,128)(2,1)S(1)}, u32[]{:S(2)}, u32[]{:S(2)}) collective-permute-start(bf16[144,1280]{1,0:T(8,128)(2,1)} %get-tuple-element.223), channel_id=1, source_target_pairs={{0,16},{4,20},{8,24},{12,28},{16,0},{20,4},{24,8},{28,12},{1,17},{... | collective-permute-start | bytes 1105928 | tf_op jit(solution)/shard_map/cond/branch_1_fun/ppermute | solution.py:32
  105.9 30.2 %collective-permute-start.31 = (bf16[320,1280]{1,0:T(8,128)(2,1)}, bf16[320,1280]{1,0:T(8,128)(2,1)S(1)}, u32[]{:S(2)}, u32[]{:S(2)}) collective-permute-start(bf16[320,1280]{1,0:T(8,128)(2,1)} %collective-permute-done.29), channel_id=1, source_target_pairs={{0,4},{4,0},{8,12},{12,8},{16,20},{20,16},{24,28},{28,24},{1,5},{5... | collective-permute-start | bytes 2457608 | tf_op jit(solution)/shard_map/ppermute | solution.py:32
  107.4 28.6 %collective-permute-start.30 = (bf16[320,1280]{1,0:T(8,128)(2,1)}, bf16[320,1280]{1,0:T(8,128)(2,1)S(1)}, u32[]{:S(2)}, u32[]{:S(2)}) collective-permute-start(bf16[320,1280]{1,0:T(8,128)(2,1)} %collective-permute-done.23), channel_id=1, source_target_pairs={{0,8},{4,12},{8,0},{12,4},{16,24},{20,28},{24,16},{28,20},{1,9},{5... | collective-permute-start | bytes 2457608 | tf_op jit(solution)/shard_map/ppermute | solution.py:32
  109.7 8.9 %collective-permute-start.6 = (bf16[320,1280]{1,0:T(8,128)(2,1)}, bf16[320,1280]{1,0:T(8,128)(2,1)S(1)}, u32[]{:S(2)}, u32[]{:S(2)}) collective-permute-start(bf16[320,1280]{1,0:T(8,128)(2,1)} %get-tuple-element.231.refs_3_), channel_id=1, source_target_pairs={{0,1},{1,0},{2,3},{3,2},{4,5},{5,4},{6,7},{7,6},{8,9},{9,8},{10,11... | collective-permute-start | bytes 2457608 | tf_op jit(solution)/shard_map/cond/branch_1_fun/ppermute | solution.py:32
  110.2 8.4 %collective-permute-start.9 = (bf16[320,1280]{1,0:T(8,128)(2,1)}, bf16[320,1280]{1,0:T(8,128)(2,1)S(1)}, u32[]{:S(2)}, u32[]{:S(2)}) collective-permute-start(bf16[320,1280]{1,0:T(8,128)(2,1)} %get-tuple-element.238.refs_2_), channel_id=1, source_target_pairs={{0,1},{1,0},{2,3},{3,2},{4,5},{5,4},{6,7},{7,6},{8,9},{9,8},{10,11... | collective-permute-start | bytes 2457608 | tf_op jit(solution)/shard_map/cond/branch_1_fun/ppermute | solution.py:32
  117.1 9.9 %collective-permute-start.8 = (bf16[256,640]{1,0:T(8,128)(2,1)S(1)}, bf16[256,640]{1,0:T(8,128)(2,1)}, u32[]{:S(2)}, u32[]{:S(2)}) collective-permute-start(bf16[256,640]{1,0:T(8,128)(2,1)S(1)} %bitcast.36), channel_id=1, source_target_pairs={{0,2},{1,3},{2,0},{3,1},{4,6},{5,7},{6,4},{7,5},{8,10},{9,11},{10,... | collective-permute-start | bytes 983048 | tf_op jit(solution)/shard_map/cond/branch_1_fun/ppermute | solution.py:32
  118.6 9.9 %collective-permute-start.7 = (bf16[256,1280]{1,0:T(8,128)(2,1)S(1)}, bf16[256,1280]{1,0:T(8,128)(2,1)}, u32[]{:S(2)}, u32[]{:S(2)}) collective-permute-start(bf16[256,1280]{1,0:T(8,128)(2,1)S(1)} %get-tuple-element.232), channel_id=1, source_target_pairs={{0,1},{1,0},{2,3},{3,2},{4,5},{5,4},{6,7},{7,6},{8,9},{9,8},{10,11... | collective-permute-start | bytes 1966088 | tf_op jit(solution)/shard_map/cond/branch_1_fun/ppermute | solution.py:32
  127.0 9.0 %collective-permute-start.10 = (bf16[256,640]{1,0:T(8,128)(2,1)S(1)}, bf16[256,640]{1,0:T(8,128)(2,1)}, u32[]{:S(2)}, u32[]{:S(2)}) collective-permute-start(bf16[256,640]{1,0:T(8,128)(2,1)S(1)} %bitcast.37), channel_id=1, source_target_pairs={{0,2},{1,3},{2,0},{3,1},{4,6},{5,7},{6,4},{7,5},{8,10},{9,11},{10,... | collective-permute-start | bytes 983048 | tf_op jit(solution)/shard_map/cond/branch_1_fun/ppermute | solution.py:32
  144.1 10.2 %collective-permute-start.13 = (bf16[256,640]{1,0:T(8,128)(2,1)S(1)}, bf16[256,640]{1,0:T(8,128)(2,1)}, u32[]{:S(2)}, u32[]{:S(2)}) collective-permute-start(bf16[256,640]{1,0:T(8,128)(2,1)S(1)} %bitcast.39), channel_id=1, source_target_pairs={{0,2},{1,3},{2,0},{3,1},{4,6},{5,7},{6,4},{7,5},{8,10},{9,11},{10,... | collective-permute-start | bytes 983048 | tf_op jit(solution)/shard_map/cond/branch_1_fun/ppermute | solution.py:32
  154.3 9.3 %collective-permute-start.16 = (bf16[256,640]{1,0:T(8,128)(2,1)S(1)}, bf16[256,640]{1,0:T(8,128)(2,1)}, u32[]{:S(2)}, u32[]{:S(2)}) collective-permute-start(bf16[256,640]{1,0:T(8,128)(2,1)S(1)} %bitcast.38), channel_id=1, source_target_pairs={{0,2},{1,3},{2,0},{3,1},{4,6},{5,7},{6,4},{7,5},{8,10},{9,11},{10,... | collective-permute-start | bytes 983048 | tf_op jit(solution)/shard_map/cond/branch_1_fun/ppermute | solution.py:32
  (23 other events, 158.8 us)

commit v5 on v4

--- a/solution.py
+++ b/solution.py
@@ -163,10 +163,16 @@
             keep_ref[0] = dot(turned, even)
 
 
-def fold_kernel(keep_ref, got_ref, own_ref, *far_refs):
-    own_ref[...] = keep_ref[0] + got_ref[0].astype(F32)
-    for i, far_ref in enumerate(far_refs):
-        far_ref[...] = (keep_ref[i + 1] + got_ref[i + 1].astype(F32)).astype(BF16)
+def split_kernel(me_ref, *refs):
+    half = len(refs) // 2
+    for value_ref, part_ref in zip(refs[:half], refs[half:]):
+        part_ref[...] = value_ref[...]
+
+
+def fold_kernel(*refs):
+    count = len(refs) // 3
+    for keep_ref, got_ref, far_ref in zip(refs[:count], refs[count : 2 * count], refs[2 * count :]):
+        far_ref[...] = (keep_ref[0] + got_ref[0].astype(F32)).astype(BF16)
 
 
 def pack_state(sent_ref, state, total):
@@ -178,9 +184,9 @@
     sent_ref[rows:, :width] = jnp.concatenate(parts, axis=0)
 
 
-def first_kernel(own_ref, total_ref, *refs):
+def first_kernel(own_ref, core_ref, total_ref, *refs):
     *far_refs, running_ref, sent_ref = refs
-    running = own_ref[...]
+    running = own_ref[0] + core_ref[0].astype(F32)
     for far_ref in far_refs:
         running = running + far_ref[...].astype(F32)
     running_ref[...] = running
@@ -215,14 +221,13 @@
 
 
 def local_kernel(me_ref, near, parts, *refs):
-    count = 1 + max(at for pieces in parts for at, _, _ in pieces)
-    value_refs, refs = refs[:count], refs[count:]
+    value_refs, refs = refs[:parts], refs[parts:]
     out_ref, lift_ref, read_ref, merge_ref, score_ref, masked_ref, spread_ref = refs[:7]
     skip_ref, cross_ref, *refs = refs[7:]
     factor_refs, state_refs, refs = refs[:near], refs[near : 2 * near], refs[2 * near :]
     pre_ref, nodes, sums, operand = refs
     group_rows = value_refs[0].shape[0]
-    groups = len(parts)
+    groups = parts
     me = me_ref[0]
     per_group = group_rows // CH
     stretches = groups * per_group
@@ -235,10 +240,9 @@
         (state_ref[:state_size, :], dot(factor_ref[...], spread)[0:1, :])
         for state_ref, factor_ref in zip(state_refs, factor_refs)
     ]
-    for r, pieces in enumerate(parts):
+    for r, value_ref in enumerate(value_refs):
         g = me ^ r
-        value = [value_refs[at][first : first + rows, :] for at, first, rows in pieces]
-        value = jnp.concatenate(value, axis=0).astype(F32)
+        value = value_ref[...].astype(F32)
         high, low = two_parts(dot(lift_ref[g], spread) * value)
         direct = dot(score_ref[g, 0], high) + dot(score_ref[g, 0], low) + dot(score_ref[g, 1], high)
         total = dot(read_ref[0, g], spread) * direct + skip * value
@@ -280,6 +284,7 @@
 def finish_kernel(
     me_ref, pre_ref, out_ref, cross_ref, factor_ref, state_ref, spread_ref, same_ref, gain_ref, *refs
 ):
+    *keep_refs, send_ref = refs
     parts = pre_ref.shape[0]
     me = me_ref[0]
     spread = spread_ref[...]
@@ -292,7 +297,10 @@
         total = pre_ref[at] + dot(cross_ref[0, at], spread) * (dot(out_ref[at], state) * row)
         mean_square = dot((total * total).astype(BF16), same)
         normed = (total * lax.rsqrt(mean_square + EPSILON) * gain).astype(BF16)
-        refs[r][...] = normed
+        if r % 2 == 0:
+            keep_refs[r // 2][...] = normed
+        else:
+            send_ref[r // 2] = normed
 
 
 def project_kernel(place_ref, *refs):
@@ -304,7 +312,7 @@
     width = weights[0].shape[0]
     for i, (kept_ref, other_ref) in enumerate(zip(kept_refs, other_refs)):
         found = [
-            dot_nt(kept_ref[...], weight[...]) + dot_nt(other_ref[...], partner[...])
+            dot_nt(kept_ref[...], weight[...]) + dot_nt(other_ref[0], partner[...])
             for weight, partner in zip(weights, partners)
         ]
         for bit in range(count.bit_length() - 1):
@@ -404,10 +412,22 @@
     for bit in range(ctx_bits):
         held[2**bit] = swap(held[0], "ctx", 2**bit)
 
-    def value_columns(values, r):
-        return lax.dynamic_slice_in_dim(values, (me ^ r) * features, features, 1)
-
-    value_head = swap(value_columns(values, 2), "head", 2)
+    portions = kernel_call(
+        split_kernel,
+        "split_values",
+        tuple([shape((rows_dev, features))] * (heads_size - 1)),
+        grid_spec=pltpu.PrefetchScalarGridSpec(
+            num_scalar_prefetch=1,
+            grid=(1,),
+            in_specs=[
+                pl.BlockSpec((rows_dev, features), lambda i, m, r=r: (0, m[0] ^ r))
+                for r in range(1, heads_size)
+            ],
+            out_specs=[whole((rows_dev, features))] * (heads_size - 1),
+        ),
+    )(me1, *[values] * (heads_size - 1))
+    portion = dict(zip(range(1, heads_size), portions))
+    value_head = swap(portion[2], "head", 2)
 
     fade, total = kernel_call(
         fade_kernel,
@@ -447,58 +467,27 @@
     )(me1, values, values, *fades, in_turned, spread)
 
     def core_sum(keep, send):
-        own_state, *far_states = kernel_call(
+        got = swap(send, "head", 1)
+        far = kernel_call(
             fold_kernel,
             "fold",
-            tuple(
-                [shape((state_size, features), F32)] + [shape((state_size, features))] * (half - 1)
-            ),
-        )(keep, swap(send, "head", 1))
-        return own_state, far_states
-
-    own_state, far_states = fenced(core_sum, keep, send)
+            tuple([shape((state_size, features))] * (half - 1)),
+            in_specs=[
+                pl.BlockSpec((1, state_size, features), lambda _, i=i: (i, 0, 0))
+                for i in range(1, half)
+            ]
+            * 2,
+            out_specs=tuple([whole((state_size, features))] * (half - 1)),
+            grid=(1,),
+        )(*[keep] * (half - 1), *[got] * (half - 1))
+        return got, far
+
+    core_states, far_states = fenced(core_sum, keep, send)
 
     merge_count = -(-len(merge_rows(stretches)) // 16) * 16
 
-    def chip_sum(
-        own_state, far_states, total, log_decay, level_class, level_table, state_in, state_out, values
-    ):
-        across = jnp.stack([value_columns(values, d + 1) for d in range(0, heads_size, 2)])
-        across = swap(across, "head", 1)
-        table = jnp.transpose(level_table, (1, 0, 2))
-        table = jnp.concatenate([table, table], axis=2)
-        tables = kernel_call(
-            factors_kernel,
-            "factors",
-            (
-                shape((tokens, wide)),
-                shape((local + 1, tokens, wide)),
-                shape((levels - local - 1, tokens, wide)),
-                shape((merge_count, wide)),
-                shape((heads_size, 2, rows_dev, rows_dev)),
-                shape((heads_size, rows_dev // CH * state_size, rows_dev)),
-            ),
-        )(log_decay, level_class.reshape(tokens, 1), table, state_in, state_out)
-        got_states = []
-        for i, far in enumerate(far_states):
-            got_states.append(swap(tie(far, *got_states), "head", 2 * (i + 1)))
-        running, sent = kernel_call(
-            first_kernel,
-            "first_state",
-            (shape((state_size, features), F32), shape((state_size + EXTRA, features))),
-        )(own_state, total, *got_states)
-        return running, sent, tables, across
-
-    running, sent, tables, across = fenced(
-        chip_sum, own_state, tie(far_states, value_head), total, log_decay, level_class, level_table,
-        state_in, state_out, values,
-    )
-    lift, read, cross, merge, scores, masked = tables
-
-    def step(bit, running, total, offset, sent, spread, passing):
-        passed = [swap(array, "head", d) for array, d in zip(passing, distances[bit])]
-        got = swap(sent, "ctx", 2**bit)
-        merged = kernel_call(
+    def step(bit, running, total, offset, got):
+        return kernel_call(
             functools.partial(merge_kernel, bit),
             "merge",
             (
@@ -510,33 +499,72 @@
             ),
             in_specs=[smem] + [vmem] * 5,
         )(place1, running, total, offset, got, spread)
-        return got, merged, passed
-
-    pending = [(d, across[d // 2]) for d in range(2, heads_size, 2)]
-    pending += [(d, value_columns(values, d)) for d in range(4, heads_size, 2)]
-    pieces = max(near, 1)
-    cut = rows_dev // pieces // 16 * 16
-    cuts = [(i * cut, rows_dev if i + 1 == pieces else (i + 1) * cut) for i in range(pieces)]
-    distances = [[d for d, _ in pending]] * pieces
-    factor = jnp.broadcast_to((position % 2).astype(BF16), (EXTRA, wide))
-    factors = [jnp.where(jnp.arange(wide)[None, :] < head_count, factor, 0)]
-    offset = jnp.zeros((1, wide), F32)
-    states, passed = [], []
-    for bit in range(near):
-        if bit == 0:
-            sent = tie(sent, held[1])
-        if bit == 1:
-            sent = tie(sent, held[2])
-        passing = [array[cuts[bit][0] : cuts[bit][1]] for _, array in pending]
-        got, merged, moved = fenced(
-            functools.partial(step, bit), running, total, offset, sent, spread, passing
+
+    def near_chain(
+        keep, core_states, far_states, total, log_decay, level_class, level_table, state_in, state_out, portion
+    ):
+        table = jnp.transpose(level_table, (1, 0, 2))
+        table = jnp.concatenate([table, table], axis=2)
+        tables_call = kernel_call(
+            factors_kernel,
+            "factors",
+            (
+                shape((tokens, wide)),
+                shape((local + 1, tokens, wide)),
+                shape((levels - local - 1, tokens, wide)),
+                shape((merge_count, wide)),
+                shape((heads_size, 2, rows_dev, rows_dev)),
+                shape((heads_size, rows_dev // CH * state_size, rows_dev)),
+            ),
         )
-        running, total, offset, factor, sent = merged
-        states.append(got)
-        factors.append(factor)
-        passed.append(moved)
-
-    sent = tie(sent, *[held[2**bit] for bit in range(1, ctx_bits)])
+        got_states, latest = [], []
+        for i, far in enumerate(far_states):
+            latest = [swap(tie(far, *latest), "head", 2 * (i + 1))]
+            got_states += latest
+        running, sent = kernel_call(
+            first_kernel,
+            "first_state",
+            (shape((state_size, features), F32), shape((state_size + EXTRA, features))),
+            grid_spec=pl.GridSpec(
+                grid=(1,),
+                in_specs=[pl.BlockSpec((1, state_size, features), lambda i: (0, 0, 0))] * 2
+                + [whole((1, wide))]
+                + [whole((state_size, features))] * len(got_states),
+                out_specs=(whole((state_size, features)), whole((state_size + EXTRA, features))),
+            ),
+        )(keep, core_states, total, *got_states)
+        moved, passed, after = {}, {}, []
+        for r, array in portion.items():
+            moved[r] = swap(tie(array, *after), "head", 1)
+            after = [moved[r]]
+        after = [running]
+        for r, array in moved.items():
+            passed[r] = swap(tie(array, *after), "head", r - 1)
+            after = [passed[r]]
+        tables = tables_call(
+            tie(log_decay, running), level_class.reshape(tokens, 1), table, state_in, state_out
+        )
+        factor = jnp.broadcast_to((position % 2).astype(BF16), (EXTRA, wide))
+        factors = [jnp.where(jnp.arange(wide)[None, :] < head_count, factor, 0)]
+        offset = jnp.zeros((1, wide), F32)
+        states = []
+        for bit in range(near):
+            got = swap(sent, "ctx", 2**bit)
+            states.append(tie(got, tables[0]) if bit == 0 else got)
+            running, total, offset, factor, sent = step(bit, running, total, offset, states[-1])
+            factors.append(factor)
+        return states, factors, sent, tables, passed
+
+    states, factors, sent, tables, passed = fenced(
+        near_chain, keep, core_states, tie(far_states, value_head), total, log_decay, level_class,
+        level_table, state_in, state_out, {r: portion[r] for r in range(3, heads_size, 2)},
+    )
+    states, passed = list(states), dict(passed)
+    passed[2] = value_head
+    sent = tie(sent, *[held[2**bit] for bit in range(ctx_bits)])
+    for r in range(4, heads_size, 2):
+        passed[r] = swap(tie(portion[r], sent), "head", r)
+
     for r in range(2, ctx_size):
         low = r & -r
         if r not in held and low > 1:
@@ -546,26 +574,18 @@
     for r in (0, 1):
         partners[r] = swap(tie(held[r], sent), "head", 1)
 
-    arrays = [values, across[0], value_head]
-    parts = [[(0, 0, rows_dev)], [(1, 0, rows_dev)], [(2, 0, rows_dev)]]
-    order = {}
-    for i, (d, _) in enumerate(pending):
-        r = d + 1 if i < half - 1 else d
-        order[r] = []
-        for step_index, (start, end) in enumerate(cuts):
-            order[r].append((len(arrays), 0, end - start))
-            arrays.append(passed[step_index][i])
-    parts += [order[r] for r in range(3, heads_size)]
+    arrays = [values, portion[1]] + [passed[r] for r in range(2, heads_size)]
 
     skip_row = jnp.repeat(skip_gain, head_width)[None, :]
 
     def read_levels(sent, state_out, tables, factors, states, arrays, spread, same, skip_row, norm_row):
         lift, read, cross, merge, scores, masked = tables
         state = swap(sent, "ctx", 2**near)
+        arrays = [arrays[0], swap(arrays[1], "head", 1)] + arrays[2:]
         readers = state_out.reshape(grouped + (state_size,))
         cross = cross.reshape((ctx_bits,) + grouped + (wide,))
         pre = kernel_call(
-            lambda me_ref, *refs: local_kernel(me_ref, near, parts, *refs),
+            lambda me_ref, *refs: local_kernel(me_ref, near, heads_size, *refs),
             "local_levels",
             shape(grouped + (features,), F32),
             grid_spec=pltpu.PrefetchScalarGridSpec(
@@ -611,7 +631,7 @@
         return kernel_call(
             finish_kernel,
             "finish",
-            tuple([shape((rows_dev, features))] * heads_size),
+            tuple([shape((rows_dev, features))] * half + [shape((half, rows_dev, features))]),
             grid_spec=pltpu.PrefetchScalarGridSpec(
                 num_scalar_prefetch=1,
                 grid=(tiles,),
@@ -625,16 +645,17 @@
                     whole((tile, tile)),
                     pl.BlockSpec((1, tile), lambda f, m: (0, f)),
                 ],
-                out_specs=[pl.BlockSpec((rows_dev, tile), lambda f, m: (0, f))] * heads_size,
+                out_specs=[pl.BlockSpec((rows_dev, tile), lambda f, m: (0, f))] * half
+                + [pl.BlockSpec((half, rows_dev, tile), lambda f, m: (0, 0, f))],
             ),
         )(me1, pre, readers, cross, factors[near], state, spread, same, norm_row)
 
-    normed = fenced(
+    *kept, sides = fenced(
         read_levels, sent, state_out, tables, factors, states, arrays, spread, same, skip_row,
         norm_gain[None, :],
     )
     early_blocks = set(held)
-    done = [held[r] for r in held if r not in (0, 1)] + list(normed)
+    done = [held[r] for r in held if r not in (0, 1)] + [kept[0]]
     held[3] = swap(tie(held[1], *done), "ctx", 2)
     for r in range(5, ctx_size, 2):
         if r not in held:
@@ -644,60 +665,75 @@
     while count * columns % 128 and 2 * count <= ctx_size:
         count *= 2
 
-    def project(name, kept, others, blocks, partners, kind):
+    others = swap(sides, "head", 1)
+    firsts = list(range(0, ctx_size, count))
+    group_of = lambda first: range(first, first + count)
+
+    def project(name, first, kept, others, blocks, partners, kind):
+        rows = len(kept)
         return kernel_call(
             project_kernel,
             name,
-            shape((len(kept), rows_dev, count * columns), kind),
-            in_specs=[smem] + [vmem] * (2 * len(kept) + 2 * count),
-        )(place1, *kept, *others, *blocks, *partners)
-
-    kept = list(normed[0::2])
-    sides = list(normed[1::2])
-    group_of = lambda first: range(first, first + count)
-
-    def project_groups(firsts, kept, others, blocks, partners, arrived):
-        partners, results = dict(partners), {}
-        for first in firsts:
+            shape((rows, rows_dev, count * columns), kind),
+            in_specs=[smem] + [vmem] * rows
+            + [
+                pl.BlockSpec((1,) + others.shape[1:], lambda _, i=i: (first + i, 0, 0))
+                for i in range(rows)
+            ]
+            + [whole((columns, features))] * (2 * count),
+            out_specs=whole((rows, rows_dev, count * columns)),
+            grid=(1,),
+        )(place1, *kept, *[others] * rows, *blocks, *partners)
+
+    def far_rows(first, kept, others, blocks, partners):
+        return project(
+            "project_far", 1, kept[1:], others,
+            [blocks[r] for r in group_of(first)], [partners[r] for r in group_of(first)], BF16,
+        )
+
+    def own_rows(first, kept, others, blocks, partners):
+        return project(
+            "project_own", 0, kept[:1], others,
+            [blocks[r] for r in group_of(first)], [partners[r] for r in group_of(first)], F32,
+        )[0]
+
+    def send_rows(far, *after):
+        far = tie(far, *after)
+        return [swap(far[i - 1], "head", 2 * i) for i in range(1, half)]
+
+    def first_groups(kept, others, blocks, partners):
+        more = {r: swap(blocks[r], "head", 1) for r in blocks if r not in partners}
+        partners = {**partners, **more}
+        fars = [far_rows(first, kept, others, blocks, partners) for first in early_groups]
+        return fars[1:], send_rows(fars[0]), more
+
+    def last_groups(kept, others, blocks, partners, early):
+        partners, results, arrived = dict(partners), {}, []
+        for first in late_groups:
             for r in group_of(first):
                 if r not in partners:
                     partners[r] = swap(blocks[r], "head", 1)
-            weights = [blocks[r] for r in group_of(first)]
-            given = [partners[r] for r in group_of(first)]
-            far = project("project_far", kept[1:], others[1:], weights, given, BF16)
-            if arrived:
-                far = tie(far, arrived[-1])
-            got = [swap(far[i - 1], "head", 2 * i) for i in range(1, half)]
-            own = project("project_own", kept[:1], others[:1], weights, given, F32)
-            results[first] = [own[0]] + got
-            arrived = arrived + got[-1:]
-        return results
-
-    def first_groups(kept, sides, blocks, partners):
-        others = [swap(side, "head", 1) for side in sides[1:]]
-        partners = dict(partners)
-        for r in first_blocks:
-            if r not in partners:
-                partners[r] = swap(blocks[r], "head", 1)
-        others = [swap(tie(sides[0], *others, partners[first_blocks[-1]]), "head", 1)] + others
-        return project_groups(early_groups, kept, others, blocks, partners, []), others
-
-    def last_groups(kept, others, blocks, partners):
-        return project_groups(late_groups, kept, others, blocks, partners, [])
-
-    firsts = list(range(0, ctx_size, count))
-    early_groups = [f for f in firsts if all(r in early_blocks for r in group_of(f))]
-    early_groups = early_groups or firsts[:1]
+            got = send_rows(far_rows(first, kept, others, blocks, partners), *arrived)
+            results[first] = [own_rows(first, kept, others, blocks, partners)] + got
+            arrived = got
+        owns = [own_rows(first, kept, others, early, partners) for first in early_groups[1:]]
+        return results, owns
+
+    early_groups = [f for f in firsts if all(r in early_blocks for r in group_of(f))] or firsts[:1]
     late_groups = [f for f in firsts if f not in early_groups]
-    first_blocks = [r for f in early_groups for r in group_of(f)]
-    last_blocks = [r for f in late_groups for r in group_of(f)]
-    results, others = fenced(
-        first_groups, kept, sides, {r: held[r] for r in first_blocks}, partners
-    )
+    early = {r: held[r] for f in early_groups for r in group_of(f)}
+    late = {r: held[r] for f in late_groups for r in group_of(f)}
+    fars, got, more = fenced(first_groups, kept, others, early, partners)
+    partners = {**partners, **more}
+    sent_groups = [got]
+    for far in fars:
+        sent_groups.append(send_rows(far, *sent_groups[-1]))
+    own = own_rows(early_groups[0], [tie(kept[0], *fars)], others, early, partners)
     if late_groups:
-        results.update(
-            fenced(last_groups, kept, others, {r: held[r] for r in last_blocks}, {})
-        )
+        late[late_groups[0]] = tie(late[late_groups[0]], own)
+    results, owns = fenced(last_groups, kept, others, late, partners, early)
+    for first, own, got in zip(early_groups, [own] + owns, sent_groups):
+        results[first] = [own] + got
     pieces = [piece for first in firsts for piece in results[first]]
     return kernel_call(
         assemble_kernel,

time: 167 us -> 150 us (0.90)
  local copies, waits for them, and re-layouts: 15.2 us -> 6.28 us
  waiting for transfers between devices: 49 us -> 44.2 us
  starting transfers between devices: 28.2 us -> 24.3 us
    ppermute x32 -> x31, waiting for transfers between devices: 49 us -> 44.2 us  [swap(): return lax.ppermute(value, axis, pairs)]
    cond x18 -> x8, local copies, waits for them, and re-layouts: 4.31 us -> 0.02 us
    ppermute x32 -> x31, starting transfers between devices: 28.2 us -> 24.3 us  [swap(): return lax.ppermute(value, axis, pairs)]
    slice x2 -> x0, local copies, waits for them, and re-layouts: 3.93 us -> none  [the longest x1 1.98 us: on_device(): arrays = [values, across[0], value_head]]
    pallas_call x12 -> x13, Pallas kernels: 53.9 us -> 56.2 us  [the longest x8 27.2 us: project(): kernel_call(project_kernel, name, shape((rows, rows_dev, count * columns)...]
    dynamic_slice x1 -> x0, local copies, waits for them, and re-layouts: 2.03 us -> none  [value_columns(): return lax.dynamic_slice_in_dim(values, (me ^ r) * features, features, 1)]
  transfers between devices with their start and end apart: 32 -> 31, of which waited for: 15 -> 14; matrix products, arithmetic and copies ran while one was open for 9% -> 5% of each run, Pallas kernels for 42% -> 46%
where the time goes in v5:
time: 150 us; the launch traced here: 149 us
  Pallas kernels  71.4 us (48%)
  waiting for transfers between devices  44.2 us (29%)
  starting transfers between devices  24.3 us (16%)
  local copies, waits for them, and re-layouts  6.28 us (4%)
  other arithmetic  2.3 us (2%)
    ppermute x31, waiting for transfers between devices, swap(): return lax.ppermute(value, axis, pairs)  44.2 us
    pallas_call x8, Pallas kernels, project(): kernel_call(project_kernel, name, shape((rows, rows_dev, count * columns)...  27.2 us
    ppermute x31, starting transfers between devices, swap(): return lax.ppermute(value, axis, pairs)  24.3 us
    pallas_call x1, Pallas kernels, read_levels(): kernel_call(lambda me_ref, *refs: local_kernel(me_ref, near, heads_size,...  19.7 us
    pallas_call x1, Pallas kernels, read_levels(): kernel_call(finish_kernel, 'finish', tuple([shape((rows_dev, features))]...  6.11 us
    pallas_call x1, Pallas kernels, near_chain(): tables_call(tie(log_decay, running), level_class.reshape(tokens, 1), tabl...  4.17 us
    pallas_call x2, Pallas kernels, step(): kernel_call(functools.partial(merge_kernel, bit), 'merge', (shape((state_...  3.36 us
  transfers between devices with their start and end apart: 31, of which 14 were waited for; matrix products, arithmetic and copies ran while one was open for 5% of the time, Pallas kernels for 46%

profile of v5, /device:TPU:0, one launch (start us, length us, event | category | flops | bytes accessed | tf_op | source)
XLA Modules:
  0.0 148.8 jit_solution(14582672214217262926)
XLA Ops:
  0.0 4.0 %collective-permute-start.22 = (bf16[320,1280]{1,0:T(8,128)(2,1)}, bf16[320,1280]{1,0:T(8,128)(2,1)}, u32[]{:S(2)}, u32[]{:S(2)}) collective-permute-start(bf16[320,1280]{1,0:T(8,128)(2,1)} %bitcast.33), channel_id=1, source_target_pairs={{0,16},{4,20},{8,24},{12,28},{16,0},{20,4},{24,8},{28,12},{1,17},{... | collective-permute-start | bytes 2457608 | tf_op jit(solution)/shard_map/ppermute | solution.py:32
  11.1 2.8 %split_values.1 = (bf16[256,1280]{1,0:T(8,128)(2,1)}, bf16[256,1280]{1,0:T(8,128)(2,1)S(1)}, bf16[256,1280]{1,0:T(8,128)(2,1)}) custom-call(s32[1]{0:T(128)} %bitcast.13.me_ref, bf16[256,5120]{1,0:T(8,128)(2,1)} %refs_1_.3, bf16[256,5120]{1,0:T(8,128)(2,1)} %refs_1_.3, bf16[256,5120]{1,0:T(8,128)(2,1)} %refs_1_.3), custom_call_target="tpu_custom_call" | custom-call | tf_op jit(solution)/shard_map/split_values/pallas_call | solution.py:415
  20.1 2.7 %partial_states.1 = (f32[2,128,1280]{2,1,0:T(8,128)S(1)}, bf16[2,128,1280]{2,1,0:T(8,128)(2,1)S(1)}) custom-call(s32[1]{0:T(128)} %bitcast.13.me_ref, bf16[256,5120]{1,0:T(8,128)(2,1)S(1)} %copy-done, bf16[256,5120]{1,0:T(8,128)(2,1)S(1)} %copy-done, bf16[256,40]{1,0:T(8,128)(2,1)S(1)} %get-tuple-element.360.refs_2_, ...), custom_call_target="tpu_custom_call" | custom-call | tf_op jit(solution)/shard_map/partial_states/pallas_call | solution.py:449
  23.9 3.3 %conditional.5 = (bf16[2,128,1280]{2,1,0:T(8,128)(2,1)}, bf16[128,1280]{1,0:T(8,128)(2,1)S(1)}) conditional(s32[]{:T(128)} %convert_element_type.27, () %tuple.61, (bf16[2,128,1280]{2,1,0:T(8,128)(2,1)S(1)}, f32[2,128,1280]{2,1,0:T(8,128)S(1)}) %tuple.63), branch_computations={%region_0.1_spmd, %region_1.2_spmd} | conditional | bytes 2621496 | solution.py:398
  29.4 34.9 %conditional.6 = (bf16[144,1280]{1,0:T(8,128)(2,1)}, bf16[144,1280]{1,0:T(8,128)(2,1)}, bf16[16,40]{1,0:T(8,128)(2,1)S(1)}, bf16[16,40]{1,0:T(8,128)(2,1)S(1)}, ...) conditional(s32[]{:T(128)} %convert_element_type.27, () %tuple.60, ...), branch_computations={%region_2.3_spmd, %region_3.4_spmd} | conditional | flops 10332 | bytes 9861125 | solution.py:398
  30.6 9.0 %collective-permute-done.12.refs_0_ = bf16[128,1280]{1,0:T(8,128)(2,1)S(1)} collective-permute-done((bf16[128,1280]{1,0:T(8,128)(2,1)S(1)}, bf16[128,1280]{1,0:T(8,128)(2,1)S(1)}, u32[]{:S(2)}, u32[]{:S(2)}) %collective-permute-start.12) | collective-permute-done | bytes 327712 | tf_op jit(solution)/shard_map/cond/branch_1_fun/ppermute | solution.py:32
  43.3 4.2 %factors.1 = (bf16[1024,40]{1,0:T(8,128)(2,1)S(1)}, bf16[5,1024,40]{2,1,0:T(8,128)(2,1)}, bf16[3,1024,40]{2,1,0:T(8,128)(2,1)S(1)}, bf16[32,40]{1,0:T(8,128)(2,1...) custom-call(f32[1024,20]{1,0:T(8,128)S(1)} %copy.34.decay_ref, s32[1024,1]{1,0:T(8,128)S(1)} %copy.31.class_ref, ...), custom_call_target="tpu_custom_call" | custom-call | tf_op jit(solution)/shard_map/cond/branch_1_fun/factors/pallas_call | solution.py:544
  47.5 3.9 %collective-permute-done.13.got_ref = bf16[144,1280]{1,0:T(8,128)(2,1)} collective-permute-done((bf16[144,1280]{1,0:T(8,128)(2,1)S(1)}, bf16[144,1280]{1,0:T(8,128)(2,1)}, u32[]{:S(2)}, u32[]{:S(2)}) %collective-permute-start.13) | collective-permute-done | bytes 368672 | tf_op jit(solution)/shard_map/cond/branch_1_fun/ppermute | solution.py:32
  53.1 9.0 %collective-permute-done.14.got_ref = bf16[144,1280]{1,0:T(8,128)(2,1)} collective-permute-done((bf16[144,1280]{1,0:T(8,128)(2,1)S(1)}, bf16[144,1280]{1,0:T(8,128)(2,1)}, u32[]{:S(2)}, u32[]{:S(2)}) %collective-permute-start.14) | collective-permute-done | bytes 368672 | tf_op jit(solution)/shard_map/cond/branch_1_fun/ppermute | solution.py:32
  65.4 29.7 %conditional.7 = ((bf16[256,1280]{1,0:T(8,128)(2,1)S(1)}, bf16[256,1280]{1,0:T(8,128)(2,1)}, bf16[2,256,1280]{2,1,0:T(8,128)(2,1)})) conditional(s32[]{:T(128)} %convert_element_type.27, () %tuple.59, (bf16[256,1280]{1,0:T(8,128)(2,1)}, bf16[1024,128]{1,0:T(8,128)(2,1)S(1)}, bf16[1024,40]{1,0:T(8,128)(2,1)S(1)}, bf16[5,1024,40]{2,1,0:T(8,128)(2,1)}, ...), branch_computations={%region_4.5_spmd, %region_5.6_spmd} | conditional | bytes 4646084 | solution.py:398
  67.8 19.7 %local_levels.1.pre_ref = f32[4,256,1280]{2,1,0:T(8,128)S(1)} custom-call(s32[1]{0:T(128)} %get-tuple-element.160.me_ref, bf16[256,5120]{1,0:T(8,128)(2,1)} %get-tuple-element.161.refs_0_, bf16[256,1280]{1,0:T(8,128)(2,1)S(1)} %collective-permute-done.1.refs_1_, bf16[256,1280]{1,0:T(8,128)(2,1)} %get-tuple-element.163.refs_2_, ...), custom_call_target="tpu_custom_call" | custom-call | tf_op jit(solution)/shard_map/cond/branch_1_fun/local_levels/pallas_call | solution.py:587
  89.0 6.1 %finish.1 = (bf16[256,1280]{1,0:T(8,128)(2,1)S(1)}, bf16[256,1280]{1,0:T(8,128)(2,1)}, bf16[2,256,1280]{2,1,0:T(8,128)(2,1)}) custom-call(s32[1]{0:T(128)} %get-tuple-element.160.me_ref, f32[4,256,1280]{2,1,0:T(8,128)S(1)} %local_levels.1.pre_ref, bf16[4,256,128]{2,1,0:T(8,128)(2,1)S(1)} %bitcast.43, bf16[3,4,256,40]{3,2,1,0:T(8,128)(2,1)S(1)} %bitcast.32, ...), custom_call_target="tpu_custom_call" | custom-call | tf_op jit(solution)/shard_map/cond/branch_1_fun/finish/pallas_call | solution.py:631
  100.6 13.9 %conditional.8 = (bf16[1,256,640]{2,1,0:T(8,128)(2,1)}, bf16[256,640]{1,0:T(8,128)(2,1)}, bf16[320,1280]{1,0:T(8,128)(2,1)}, bf16[320,1280]{1,0:T(8,128)(2,1)}) conditional(s32[]{:T(128)} %convert_element_type.27, () %tuple.68, (bf16[320,1280]{1,0:T(8,128)(2,1)}, bf16[320,1280]{1,0:T(8,128)(2,1)}, s32[1]{0:T(128)}, bf16[256,1280]{1,0:T(8,128)(2,1)}, ...), branch_computations={%region_6.7_spmd, %region_7.8_spmd} | conditional | bytes 7864472 | solution.py:398
  101.1 3.4 %project_far.5 = bf16[1,256,640]{2,1,0:T(8,128)(2,1)S(1)} custom-call(s32[1]{0:T(128)} %get-tuple-element.183.place_ref, bf16[256,1280]{1,0:T(8,128)(2,1)} %get-tuple-element.184.refs_0_, bf16[2,256,1280]{2,1,0:T(8,128)(2,1)S(1)} %get-tuple-element.185.refs_1_, bf16[320,1280]{1,0:T(8,128)(2,1)S(1)} %get-tuple-element.188.refs_2_, ...), custom_call_target="tpu_custom_call" | custom-call | tf_op jit(solution)/shard_map/cond/branch_1_fun/project_far/pallas_call | solution.py:674
  105.6 4.4 %project_far.4 = bf16[1,256,640]{2,1,0:T(8,128)(2,1)} custom-call(s32[1]{0:T(128)} %get-tuple-element.183.place_ref, bf16[256,1280]{1,0:T(8,128)(2,1)} %get-tuple-element.184.refs_0_, bf16[2,256,1280]{2,1,0:T(8,128)(2,1)S(1)} %get-tuple-element.185.refs_1_, bf16[320,1280]{1,0:T(8,128)(2,1)} %get-tuple-element.186.refs_2_, ...), custom_call_target="tpu_custom_call" | custom-call | tf_op jit(solution)/shard_map/cond/branch_1_fun/project_far/pallas_call | solution.py:674
  110.0 4.5 %collective-permute-done.5 = bf16[256,640]{1,0:T(8,128)(2,1)} collective-permute-done((bf16[256,640]{1,0:T(8,128)(2,1)S(1)}, bf16[256,640]{1,0:T(8,128)(2,1)}, u32[]{:S(2)}, u32[]{:S(2)}) %collective-permute-start.5) | collective-permute-done | bytes 327712 | tf_op jit(solution)/shard_map/cond/branch_1_fun/ppermute | solution.py:32
  115.6 3.5 %project_own.7 = f32[1,256,640]{2,1,0:T(8,128)S(1)} custom-call(s32[1]{0:T(128)} %bitcast.12.place_ref, bf16[256,1280]{1,0:T(8,128)(2,1)S(1)} %get-tuple-element.282.refs_0_, bf16[2,256,1280]{2,1,0:T(8,128)(2,1)S(1)} %collective-permute-done.24.refs_1_, bf16[320,1280]{1,0:T(8,128)(2,1)} %bitcast.36, bf16[320,1280]{1,0:T(8,128)(2,1)} %collective-permute-done.20.refs_3_, ...), custom_call_target="tpu_custom_call" | custom-call | tf_op jit(solution)/shard_map/project_own/pallas_call | solution.py:674
  119.1 27.3 %conditional.9 = (f32[256,640]{1,0:T(8,128)S(1)}, bf16[256,640]{1,0:T(8,128)(2,1)S(1)}, f32[256,640]{1,0:T(8,128)S(1)}, bf16[256,640]{1,0:T(8,128)(2,1)}, f32[256,640]{1,0:T(8,128)S(1)}) conditional(s32[]{:T(128)} %convert_element_type.27, () %tuple.74, (bf16[320,1280]{1,0:T(8,128)(2,1)}, bf16[320,1280]{1,0:T(8,128)(2,1)}, s32[1]{0:T(128)}, ...), branch_computations={%region_8.9_spmd, %region_9.10_spmd} | conditional | bytes 18350416 | solution.py:398
  122.9 3.2 %project_far.6 = bf16[1,256,640]{2,1,0:T(8,128)(2,1)S(1)} custom-call(s32[1]{0:T(128)} %get-tuple-element.192.place_ref, bf16[256,1280]{1,0:T(8,128)(2,1)} %get-tuple-element.197.refs_0_, bf16[2,256,1280]{2,1,0:T(8,128)(2,1)S(1)} %get-tuple-element.194.refs_1_, bf16[320,1280]{1,0:T(8,128)(2,1)} %get-tuple-element.195.refs_2_, ...), custom_call_target="tpu_custom_call" | custom-call | tf_op jit(solution)/shard_map/cond/branch_1_fun/project_far/pallas_call | solution.py:674
  127.1 3.2 %project_far.7 = bf16[1,256,640]{2,1,0:T(8,128)(2,1)S(1)} custom-call(s32[1]{0:T(128)} %get-tuple-element.192.place_ref, bf16[256,1280]{1,0:T(8,128)(2,1)} %get-tuple-element.197.refs_0_, bf16[2,256,1280]{2,1,0:T(8,128)(2,1)S(1)} %get-tuple-element.194.refs_1_, bf16[320,1280]{1,0:T(8,128)(2,1)} %get-tuple-element.198.refs_2_, ...), custom_call_target="tpu_custom_call" | custom-call | tf_op jit(solution)/shard_map/cond/branch_1_fun/project_far/pallas_call | solution.py:674
  130.3 5.6 %collective-permute-done.8 = bf16[256,640]{1,0:T(8,128)(2,1)S(1)} collective-permute-done((bf16[256,640]{1,0:T(8,128)(2,1)S(1)}, bf16[256,640]{1,0:T(8,128)(2,1)S(1)}, u32[]{:S(2)}, u32[]{:S(2)}) %collective-permute-start.8) | collective-permute-done | bytes 327712 | tf_op jit(solution)/shard_map/cond/branch_1_fun/ppermute | solution.py:32
  136.8 3.5 %project_own.6 = f32[1,256,640]{2,1,0:T(8,128)S(1)} custom-call(s32[1]{0:T(128)} %get-tuple-element.192.place_ref, bf16[256,1280]{1,0:T(8,128)(2,1)S(1)} %get-tuple-element.193.refs_0_, bf16[2,256,1280]{2,1,0:T(8,128)(2,1)S(1)} %get-tuple-element.194.refs_1_, bf16[320,1280]{1,0:T(8,128)(2,1)} %get-tuple-element.201.refs_2_, ...), custom_call_target="tpu_custom_call" | custom-call | tf_op jit(solution)/shard_map/cond/branch_1_fun/project_own/pallas_call | solution.py:674
  140.4 3.0 %project_own.4 = f32[1,256,640]{2,1,0:T(8,128)S(1)} custom-call(s32[1]{0:T(128)} %get-tuple-element.192.place_ref, bf16[256,1280]{1,0:T(8,128)(2,1)S(1)} %get-tuple-element.193.refs_0_, bf16[2,256,1280]{2,1,0:T(8,128)(2,1)S(1)} %get-tuple-element.194.refs_1_, bf16[320,1280]{1,0:T(8,128)(2,1)} %get-tuple-element.195.refs_2_, ...), custom_call_target="tpu_custom_call" | custom-call | tf_op jit(solution)/shard_map/cond/branch_1_fun/project_own/pallas_call | solution.py:674
  143.4 3.0 %project_own.5 = f32[1,256,640]{2,1,0:T(8,128)S(1)} custom-call(s32[1]{0:T(128)} %get-tuple-element.192.place_ref, bf16[256,1280]{1,0:T(8,128)(2,1)S(1)} %get-tuple-element.193.refs_0_, bf16[2,256,1280]{2,1,0:T(8,128)(2,1)S(1)} %get-tuple-element.194.refs_1_, bf16[320,1280]{1,0:T(8,128)(2,1)} %get-tuple-element.198.refs_2_, ...), custom_call_target="tpu_custom_call" | custom-call | tf_op jit(solution)/shard_map/cond/branch_1_fun/project_own/pallas_call | solution.py:674
  (111 shorter events, 49.7 us)
Async XLA Ops:
  0.0 64.3 %collective-permute-start.22 = (bf16[320,1280]{1,0:T(8,128)(2,1)}, bf16[320,1280]{1,0:T(8,128)(2,1)}, u32[]{:S(2)}, u32[]{:S(2)}) collective-permute-start(bf16[320,1280]{1,0:T(8,128)(2,1)} %bitcast.33), channel_id=1, source_target_pairs={{0,16},{4,20},{8,24},{12,28},{16,0},{20,4},{24,8},{28,12},{1,17},{... | collective-permute-start | bytes 2457608 | tf_op jit(solution)/shard_map/ppermute | solution.py:32
  4.0 60.3 %collective-permute-start.20 = (bf16[320,1280]{1,0:T(8,128)(2,1)}, bf16[320,1280]{1,0:T(8,128)(2,1)}, u32[]{:S(2)}, u32[]{:S(2)}) collective-permute-start(bf16[320,1280]{1,0:T(8,128)(2,1)} %bitcast.34), channel_id=1, source_target_pairs={{0,4},{4,0},{8,12},{12,8},{16,20},{20,16},{24,28},{28,24},{1,5},{5... | collective-permute-start | bytes 2457608 | tf_op jit(solution)/shard_map/ppermute | solution.py:32
  5.5 58.8 %collective-permute-start.21 = (bf16[320,1280]{1,0:T(8,128)(2,1)}, bf16[320,1280]{1,0:T(8,128)(2,1)}, u32[]{:S(2)}, u32[]{:S(2)}) collective-permute-start(bf16[320,1280]{1,0:T(8,128)(2,1)} %bitcast.35), channel_id=1, source_target_pairs={{0,8},{4,12},{8,0},{12,4},{16,24},{20,28},{24,16},{28,20},{1,9},{5... | collective-permute-start | bytes 2457608 | tf_op jit(solution)/shard_map/ppermute | solution.py:32
  9.6 6.4 %collective-permute-start.17 = (bf16[2,256,40]{2,1,0:T(8,128)(2,1)}, bf16[2,256,40]{2,1,0:T(8,128)(2,1)}, u32[]{:S(2)}, u32[]{:S(2)}) collective-permute-start(bf16[2,256,40]{2,1,0:T(8,128)(2,1)} %slice.23), channel_id=1, source_target_pairs={{0,2},{1,3},{2,0},{3,1},{4,6},{5,7},{6,4},{7,5},{8,10},{9,11},{10,... | collective-permute-start | bytes 122888 | tf_op jit(solution)/shard_map/ppermute | solution.py:32
  13.9 15.5 %collective-permute-start.19 = (bf16[256,1280]{1,0:T(8,128)(2,1)S(1)}, bf16[256,1280]{1,0:T(8,128)(2,1)}, u32[]{:S(2)}, u32[]{:S(2)}) collective-permute-start(bf16[256,1280]{1,0:T(8,128)(2,1)S(1)} %get-tuple-element.256), channel_id=1, source_target_pairs={{0,2},{1,3},{2,0},{3,1},{4,6},{5,7},{6,4},{7,5},{8,10},{9,11},{10,... | collective-permute-start | bytes 1966088 | tf_op jit(solution)/shard_map/ppermute | solution.py:32
  29.4 12.1 %collective-permute-start.15 = (bf16[256,1280]{1,0:T(8,128)(2,1)}, bf16[256,1280]{1,0:T(8,128)(2,1)}, u32[]{:S(2)}, u32[]{:S(2)}) collective-permute-start(bf16[256,1280]{1,0:T(8,128)(2,1)} %get-tuple-element.158), channel_id=1, source_target_pairs={{0,1},{1,0},{2,3},{3,2},{4,5},{5,4},{6,7},{7,6},{8,9},{9,8},{10,11... | collective-permute-start | bytes 1966088 | tf_op jit(solution)/shard_map/cond/branch_1_fun/ppermute | solution.py:32
  29.5 10.1 %collective-permute-start.12 = (bf16[128,1280]{1,0:T(8,128)(2,1)S(1)}, bf16[128,1280]{1,0:T(8,128)(2,1)S(1)}, u32[]{:S(2)}, u32[]{:S(2)}) collective-permute-start(bf16[128,1280]{1,0:T(8,128)(2,1)S(1)} %get-tuple-element.131), channel_id=1, source_target_pairs={{0,2},{1,3},{2,0},{3,1},{4,6},{5,7},{6,4},{7,5},{8,10},{9,11},{10,... | collective-permute-start | bytes 983048 | tf_op jit(solution)/shard_map/cond/branch_1_fun/ppermute | solution.py:32
  41.0 10.4 %collective-permute-start.13 = (bf16[144,1280]{1,0:T(8,128)(2,1)S(1)}, bf16[144,1280]{1,0:T(8,128)(2,1)}, u32[]{:S(2)}, u32[]{:S(2)}) collective-permute-start(bf16[144,1280]{1,0:T(8,128)(2,1)S(1)} %get-tuple-element.132), channel_id=1, source_target_pairs={{0,4},{4,0},{8,12},{12,8},{16,20},{20,16},{24,28},{28,24},{1,5},{5... | collective-permute-start | bytes 1105928 | tf_op jit(solution)/shard_map/cond/branch_1_fun/ppermute | solution.py:32
  41.6 22.7 %collective-permute-start.16 = (bf16[256,1280]{1,0:T(8,128)(2,1)}, bf16[256,1280]{1,0:T(8,128)(2,1)}, u32[]{:S(2)}, u32[]{:S(2)}) collective-permute-start(bf16[256,1280]{1,0:T(8,128)(2,1)} %collective-permute-done.15), channel_id=1, source_target_pairs={{0,2},{1,3},{2,0},{3,1},{4,6},{5,7},{6,4},{7,5},{8,10},{9,11},{10,... | collective-permute-start | bytes 1966088 | tf_op jit(solution)/shard_map/cond/branch_1_fun/ppermute | solution.py:32
  52.6 9.5 %collective-permute-start.14 = (bf16[144,1280]{1,0:T(8,128)(2,1)S(1)}, bf16[144,1280]{1,0:T(8,128)(2,1)}, u32[]{:S(2)}, u32[]{:S(2)}) collective-permute-start(bf16[144,1280]{1,0:T(8,128)(2,1)S(1)} %get-tuple-element.144), channel_id=1, source_target_pairs={{0,8},{4,12},{8,0},{12,4},{16,24},{20,28},{24,16},{28,20},{1,9},{5... | collective-permute-start | bytes 1105928 | tf_op jit(solution)/shard_map/cond/branch_1_fun/ppermute | solution.py:32
  64.3 31.2 %collective-permute-start.23 = (bf16[320,1280]{1,0:T(8,128)(2,1)}, bf16[320,1280]{1,0:T(8,128)(2,1)}, u32[]{:S(2)}, u32[]{:S(2)}) collective-permute-start(bf16[320,1280]{1,0:T(8,128)(2,1)} %collective-permute-done.22), channel_id=1, source_target_pairs={{0,4},{4,0},{8,12},{12,8},{16,20},{20,16},{24,28},{28,24},{1,5},{5... | collective-permute-start | bytes 2457608 | tf_op jit(solution)/shard_map/ppermute | solution.py:32
  64.9 30.7 %collective-permute-start.27 = (bf16[320,1280]{1,0:T(8,128)(2,1)}, bf16[320,1280]{1,0:T(8,128)(2,1)}, u32[]{:S(2)}, u32[]{:S(2)}) collective-permute-start(bf16[320,1280]{1,0:T(8,128)(2,1)} %collective-permute-done.22), channel_id=1, source_target_pairs={{0,8},{4,12},{8,0},{12,4},{16,24},{20,28},{24,16},{28,20},{1,9},{5... | collective-permute-start | bytes 2457608 | tf_op jit(solution)/shard_map/ppermute | solution.py:32
  65.5 23.5 %collective-permute-start.2 = (bf16[144,1280]{1,0:T(8,128)(2,1)}, bf16[144,1280]{1,0:T(8,128)(2,1)S(1)}, u32[]{:S(2)}, u32[]{:S(2)}) collective-permute-start(bf16[144,1280]{1,0:T(8,128)(2,1)} %get-tuple-element.179), channel_id=1, source_target_pairs={{0,16},{4,20},{8,24},{12,28},{16,0},{20,4},{24,8},{28,12},{1,17},{... | collective-permute-start | bytes 1105928 | tf_op jit(solution)/shard_map/cond/branch_1_fun/ppermute | solution.py:32
  95.1 5.5 %collective-permute-start.24 = (bf16[2,256,1280]{2,1,0:T(8,128)(2,1)}, bf16[2,256,1280]{2,1,0:T(8,128)(2,1)S(1)}, u32[]{:S(2)}, u32[]{:S(2)}) collective-permute-start(bf16[2,256,1280]{2,1,0:T(8,128)(2,1)} %get-tuple-element.278), channel_id=1, source_target_pairs={{0,1},{1,0},{2,3},{3,2},{4,5},{5,4},{6,7},{7,6},{8,9},{9,8},{10,11... | collective-permute-start | bytes 3932168 | tf_op jit(solution)/shard_map/ppermute | solution.py:32
  95.1 5.3 %collective-permute-start.26 = (bf16[320,1280]{1,0:T(8,128)(2,1)}, bf16[320,1280]{1,0:T(8,128)(2,1)}, u32[]{:S(2)}, u32[]{:S(2)}) collective-permute-start(bf16[320,1280]{1,0:T(8,128)(2,1)} %collective-permute-done.20.refs_3_), channel_id=1, source_target_pairs={{0,1},{1,0},{2,3},{3,2},{4,5},{5,4},{6,7},{7,6},{8,9},{9,8},{10,11... | collective-permute-start | bytes 2457608 | tf_op jit(solution)/shard_map/ppermute | solution.py:32
  95.6 23.5 %collective-permute-start.29 = (bf16[320,1280]{1,0:T(8,128)(2,1)}, bf16[320,1280]{1,0:T(8,128)(2,1)}, u32[]{:S(2)}, u32[]{:S(2)}) collective-permute-start(bf16[320,1280]{1,0:T(8,128)(2,1)} %collective-permute-done.27), channel_id=1, source_target_pairs={{0,4},{4,0},{8,12},{12,8},{16,20},{20,16},{24,28},{28,24},{1,5},{5... | collective-permute-start | bytes 2457608 | tf_op jit(solution)/shard_map/ppermute | solution.py:32
  97.2 21.9 %collective-permute-start.28 = (bf16[320,1280]{1,0:T(8,128)(2,1)}, bf16[320,1280]{1,0:T(8,128)(2,1)}, u32[]{:S(2)}, u32[]{:S(2)}) collective-permute-start(bf16[320,1280]{1,0:T(8,128)(2,1)} %collective-permute-done.20.refs_3_), channel_id=1, source_target_pairs={{0,8},{4,12},{8,0},{12,4},{16,24},{20,28},{24,16},{28,20},{1,9},{5... | collective-permute-start | bytes 2457608 | tf_op jit(solution)/shard_map/ppermute | solution.py:32
  100.6 5.1 %collective-permute-start.3 = (bf16[320,1280]{1,0:T(8,128)(2,1)}, bf16[320,1280]{1,0:T(8,128)(2,1)}, u32[]{:S(2)}, u32[]{:S(2)}) collective-permute-start(bf16[320,1280]{1,0:T(8,128)(2,1)} %get-tuple-element.186.refs_2_), channel_id=1, source_target_pairs={{0,1},{1,0},{2,3},{3,2},{4,5},{5,4},{6,7},{7,6},{8,9},{9,8},{10,11... | collective-permute-start | bytes 2457608 | tf_op jit(solution)/shard_map/cond/branch_1_fun/ppermute | solution.py:32
  104.5 10.0 %collective-permute-start.5 = (bf16[256,640]{1,0:T(8,128)(2,1)S(1)}, bf16[256,640]{1,0:T(8,128)(2,1)}, u32[]{:S(2)}, u32[]{:S(2)}) collective-permute-start(bf16[256,640]{1,0:T(8,128)(2,1)S(1)} %bitcast.28), channel_id=1, source_target_pairs={{0,2},{1,3},{2,0},{3,1},{4,6},{5,7},{6,4},{7,5},{8,10},{9,11},{10,... | collective-permute-start | bytes 983048 | tf_op jit(solution)/shard_map/cond/branch_1_fun/ppermute | solution.py:32
  114.5 31.9 %collective-permute-start.30 = (bf16[256,640]{1,0:T(8,128)(2,1)}, bf16[256,640]{1,0:T(8,128)(2,1)S(1)}, u32[]{:S(2)}, u32[]{:S(2)}) collective-permute-start(bf16[256,640]{1,0:T(8,128)(2,1)} %bitcast.21), channel_id=1, source_target_pairs={{0,2},{1,3},{2,0},{3,1},{4,6},{5,7},{6,4},{7,5},{8,10},{9,11},{10,... | collective-permute-start | bytes 983048 | tf_op jit(solution)/shard_map/ppermute | solution.py:32
  119.7 7.4 %collective-permute-start.10 = (bf16[320,1280]{1,0:T(8,128)(2,1)}, bf16[320,1280]{1,0:T(8,128)(2,1)S(1)}, u32[]{:S(2)}, u32[]{:S(2)}) collective-permute-start(bf16[320,1280]{1,0:T(8,128)(2,1)} %get-tuple-element.199.refs_3_), channel_id=1, source_target_pairs={{0,1},{1,0},{2,3},{3,2},{4,5},{5,4},{6,7},{7,6},{8,9},{9,8},{10,11... | collective-permute-start | bytes 2457608 | tf_op jit(solution)/shard_map/cond/branch_1_fun/ppermute | solution.py:32
  119.8 7.3 %collective-permute-start.9 = (bf16[320,1280]{1,0:T(8,128)(2,1)}, bf16[320,1280]{1,0:T(8,128)(2,1)S(1)}, u32[]{:S(2)}, u32[]{:S(2)}) collective-permute-start(bf16[320,1280]{1,0:T(8,128)(2,1)} %get-tuple-element.198.refs_2_), channel_id=1, source_target_pairs={{0,1},{1,0},{2,3},{3,2},{4,5},{5,4},{6,7},{7,6},{8,9},{9,8},{10,11... | collective-permute-start | bytes 2457608 | tf_op jit(solution)/shard_map/cond/branch_1_fun/ppermute | solution.py:32
  126.1 9.8 %collective-permute-start.8 = (bf16[256,640]{1,0:T(8,128)(2,1)S(1)}, bf16[256,640]{1,0:T(8,128)(2,1)S(1)}, u32[]{:S(2)}, u32[]{:S(2)}) collective-permute-start(bf16[256,640]{1,0:T(8,128)(2,1)S(1)} %bitcast.29), channel_id=1, source_target_pairs={{0,2},{1,3},{2,0},{3,1},{4,6},{5,7},{6,4},{7,5},{8,10},{9,11},{10,... | collective-permute-start | bytes 983048 | tf_op jit(solution)/shard_map/cond/branch_1_fun/ppermute | solution.py:32
  135.9 10.6 %collective-permute-start.11 = (bf16[256,640]{1,0:T(8,128)(2,1)S(1)}, bf16[256,640]{1,0:T(8,128)(2,1)}, u32[]{:S(2)}, u32[]{:S(2)}) collective-permute-start(bf16[256,640]{1,0:T(8,128)(2,1)S(1)} %bitcast.27), channel_id=1, source_target_pairs={{0,2},{1,3},{2,0},{3,1},{4,6},{5,7},{6,4},{7,5},{8,10},{9,11},{10,... | collective-permute-start | bytes 983048 | tf_op jit(solution)/shard_map/cond/branch_1_fun/ppermute | solution.py:32
  (20 other events, 193.0 us)
